TPU v7x, 32 devices: a whole 2x2x4 slice. The times are simulated.
32 devices in a mesh: shard: 4 (over y, x), ctx: 2 (over core), tp: 4 (over z).
Axes of the slice: x: 2, y: 2, z: 4, core: 2. Of those that a mesh axis runs over, the one named last changes fastest.
Arguments:
- latent: bfloat16 [4, 4096, 768], P('shard', ('ctx', 'tp')), may hold values from -6 to 6
- condition: bfloat16 [4, 768], P('shard'), may hold values from -6 to 6
- modulator: bfloat16 [768, 4608], P('shard'), may hold values from -0.21875 to 0.21875
- modulator_bias: bfloat16 [4608], replicated, may hold values from -3 to 3
- projector: bfloat16 [768, 3, 768], P('shard', None, 'tp'), may hold values from -0.21875 to 0.21875
- projector_bias: bfloat16 [2, 768], P(None, 'tp'), may hold values from -3 to 3
- merger: bfloat16 [768, 768], P('tp', 'shard'), may hold values from -3 to 3
- merger_bias: bfloat16 [768], replicated, may hold values from -3 to 3
- expander: bfloat16 [768, 3072], P('shard', 'tp'), may hold values from -0.21875 to 0.21875
- expander_bias: bfloat16 [3072], P('tp'), may hold values from -3 to 3
- reducer: bfloat16 [3072, 768], P('tp', 'shard'), may hold values from -0.109375 to 0.109375
- reducer_bias: bfloat16 [768], replicated, may hold values from -3 to 3
- cotangent: bfloat16 [4, 4096, 768], P('shard', ('ctx', 'tp')), may hold values from -6 to 6
Outputs:
- block_output: bfloat16 [4, 4096, 768], P('shard', ('ctx', 'tp'))
- grad_latent: float32 [4, 4096, 768], P('shard', ('ctx', 'tp'))
- grad_condition: float32 [4, 768], P('shard')
- grad_modulator: float32 [768, 4608], P(('shard', 'ctx'), 'tp')
- grad_modulator_bias: float32 [4608], P('tp')
- grad_projector: float32 [768, 3, 768], P(('shard', 'ctx'), None, 'tp')
- grad_projector_bias: float32 [2, 768], P(None, 'tp')
- grad_merger: float32 [768, 768], P('tp', ('shard', 'ctx'))
- grad_merger_bias: float32 [768], replicated
- grad_expander: float32 [768, 3072], P(('shard', 'ctx'), 'tp')
- grad_expander_bias: float32 [3072], P('tp')
- grad_reducer: float32 [3072, 768], P('tp', ('shard', 'ctx'))
- grad_reducer_bias: float32 [768], replicated
All inputs are finite; a program needn't handle non-finite values.
Results may differ from a plain program's by a relative error of at most 0.015.
The roundings to bfloat16 on the way count: a program that leaves them out, or rounds other values in their place, can miss the bound.
Values may be sent and summed in bfloat16 or wider, within the bound.
No kernel may reach another device: no remote copies, remote signals or barrier semaphores. Data moves between devices by JAX's collectives and lax.ppermute only.
A program may use at most 256 MiB of HBM per device.

v0:
```python
import math

import jax
import jax.numpy as jnp
from jax import lax
from jax.sharding import PartitionSpec as P

HEAD_DIM = 64


PRECISE = lax.Precision.HIGHEST


def layer_norm(values):
    row_mean = jnp.mean(values, -1, keepdims=True)
    centered = values - row_mean
    variance = jnp.mean(centered * centered, -1, keepdims=True)
    return centered * lax.rsqrt(variance + 1e-06)


def gelu_tanh(values):
    return (
        0.5
        * values
        * (1.0 + jnp.tanh(0.7978845608028654 * (values + 0.044715 * values * values * values)))
    )


def silu_gate(values):
    return values * jax.nn.sigmoid(values)


def modulate(values, scale_part, shift_part):
    return layer_norm(values) * (1.0 + scale_part) + shift_part


def split_heads(array):
    return array.reshape(array.shape[0], -1, HEAD_DIM)


def block_rows(count):
    return math.gcd(count, 512)


def to_blocks(array, size):
    return array.reshape((array.shape[0] // size, size) + array.shape[1:])


def stats_blocks(stats, size):
    return stats.reshape(stats.shape[0], stats.shape[1] // size, size).transpose(1, 0, 2)


def stats_whole(blocks):
    return blocks.transpose(1, 0, 2).reshape(blocks.shape[1], blocks.shape[0] * blocks.shape[2])


def score_block(query_heads, key_heads):
    return jnp.einsum(
        "qhd,khd->hqk", query_heads, key_heads, preferred_element_type=jnp.float32
    ) * HEAD_DIM ** (-0.5)


def attend_block(queries, key_rows, value_rows):
    scores = score_block(split_heads(queries), split_heads(key_rows))
    top_score = jnp.max(scores, -1, keepdims=True)
    exponent = jnp.exp(scores - top_score)
    total = jnp.sum(exponent, -1, keepdims=True)
    softmaxed = (exponent / total).astype(jnp.bfloat16)
    mixed = jnp.einsum(
        "hqk,khd->qhd", softmaxed, split_heads(value_rows), preferred_element_type=jnp.float32
    )
    return (mixed.reshape(queries.shape), (top_score + jnp.log(total))[:, :, 0])


def attend_rows(operands):
    queries, key_rows, value_rows = operands
    size = block_rows(queries.shape[0])
    mixed, logsum = lax.map(
        lambda block: attend_block(block, key_rows, value_rows), to_blocks(queries, size)
    )
    return (mixed.reshape(queries.shape), stats_whole(logsum))


def probs_and_grads(queries, key_rows, value_rows, grad_rows, logsum):
    softmaxed = jnp.exp(
        score_block(split_heads(queries), split_heads(key_rows)) - logsum[:, :, None]
    )
    grad_probs = jnp.einsum(
        "qhd,khd->hqk",
        split_heads(grad_rows),
        split_heads(value_rows),
        preferred_element_type=jnp.float32,
    )
    return (softmaxed, grad_probs)


def keys_part(softmaxed, grad_scores, queries, grad_rows, key_shape):
    grad_keys = jnp.einsum(
        "hqk,qhd->khd", grad_scores, split_heads(queries), preferred_element_type=jnp.float32
    ) * HEAD_DIM ** (-0.5)
    grad_values = jnp.einsum(
        "hqk,qhd->khd",
        softmaxed.astype(jnp.bfloat16),
        split_heads(grad_rows),
        preferred_element_type=jnp.float32,
    )
    return (grad_keys.reshape(key_shape), grad_values.reshape(key_shape))


def attend_back(operands):
    queries, key_rows, value_rows, grad_rows, logsum = operands
    size = block_rows(queries.shape[0])

    def one_block(carry, parts):
        query_block, grad_block, logsum_block = parts
        softmaxed, grad_probs = probs_and_grads(
            query_block, key_rows, value_rows, grad_block, logsum_block
        )
        inner = jnp.sum(softmaxed * grad_probs, -1, keepdims=True)
        grad_scores = (softmaxed * (grad_probs - inner)).astype(jnp.bfloat16)
        grad_queries = jnp.einsum(
            "hqk,khd->qhd", grad_scores, split_heads(key_rows), preferred_element_type=jnp.float32
        ) * HEAD_DIM ** (-0.5)
        grad_keys, grad_values = keys_part(
            softmaxed, grad_scores, query_block, grad_block, key_rows.shape
        )
        return (
            (carry[0] + grad_keys, carry[1] + grad_values),
            grad_queries.reshape(query_block.shape),
        )

    start = (jnp.zeros(key_rows.shape, jnp.float32), jnp.zeros(key_rows.shape, jnp.float32))
    totals, grad_queries = lax.scan(
        one_block,
        start,
        (to_blocks(queries, size), to_blocks(grad_rows, size), stats_blocks(logsum, size)),
    )
    return (grad_queries.reshape(queries.shape), totals[0], totals[1])


def shards(
    latent,
    condition,
    modulator,
    modulator_bias,
    projector,
    projector_bias,
    merger,
    merger_bias,
    expander,
    expander_bias,
    reducer,
    reducer_bias,
    cotangent,
):
    full_modulator, full_projector, full_merger, full_expander, full_reducer = (
        lax.all_gather(modulator, "shard", axis=0, tiled=True),
        lax.all_gather(projector, "shard", axis=0, tiled=True),
        lax.all_gather(merger, "shard", axis=1, tiled=True),
        lax.all_gather(expander, "shard", axis=0, tiled=True),
        lax.all_gather(reducer, "shard", axis=1, tiled=True),
    )
    model_width = latent.shape[2]
    local_width = full_projector.shape[2]
    flat_projector = full_projector.reshape(model_width, 3 * local_width)
    gate_input, silu_back = jax.vjp(silu_gate, condition.astype(jnp.float32))
    scaled = gate_input.astype(jnp.bfloat16)
    modulation = jnp.dot(
        scaled, full_modulator, preferred_element_type=jnp.float32
    ) + modulator_bias.astype(jnp.float32)
    settings = [
        modulation[:, None, index * model_width : (index + 1) * model_width] for index in range(6)
    ]
    shift_one, scale_one, gate_one, shift_two, scale_two, gate_two = settings
    latent_wide = latent.astype(jnp.float32)
    normed_wide, norm_back = jax.vjp(modulate, latent_wide, scale_one, shift_one)
    row_block = lax.all_gather(normed_wide.astype(jnp.bfloat16), "tp", axis=1, tiled=True)
    projected = jnp.einsum(
        "btd,de->bte", row_block, flat_projector, preferred_element_type=jnp.float32
    )
    queries = (projected[:, :, :local_width] + projector_bias[0].astype(jnp.float32)).astype(
        jnp.bfloat16
    )
    key_rows = projected[:, :, local_width : 2 * local_width].astype(jnp.bfloat16)
    value_rows = (
        projected[:, :, 2 * local_width :] + projector_bias[1].astype(jnp.float32)
    ).astype(jnp.bfloat16)
    key_all, value_all = (
        lax.all_gather(key_rows, "ctx", axis=1, tiled=True),
        lax.all_gather(value_rows, "ctx", axis=1, tiled=True),
    )
    attended, logsum = lax.map(attend_rows, (queries, key_all, value_all))
    attended_low = attended.astype(jnp.bfloat16)
    merge_terms = jnp.einsum(
        "bth,hd->btd", attended_low, full_merger, preferred_element_type=jnp.float32
    )
    branch = lax.psum_scatter(
        merge_terms, "tp", scatter_dimension=1, tiled=True
    ) + merger_bias.astype(jnp.float32)
    middle = latent_wide + gate_one * branch
    normed_two_wide, norm_back_two = jax.vjp(modulate, middle, scale_two, shift_two)
    row_block_two = lax.all_gather(normed_two_wide.astype(jnp.bfloat16), "tp", axis=1, tiled=True)
    hidden = jnp.einsum(
        "btd,df->btf", row_block_two, full_expander, preferred_element_type=jnp.float32
    ) + expander_bias.astype(jnp.float32)
    activated, gelu_back = jax.vjp(gelu_tanh, hidden)
    activated_low = activated.astype(jnp.bfloat16)
    reduce_terms = jnp.einsum(
        "btf,fd->btd", activated_low, full_reducer, preferred_element_type=jnp.float32
    )
    feed = lax.psum_scatter(
        reduce_terms.astype(jnp.bfloat16), "tp", scatter_dimension=1, tiled=True
    ).astype(jnp.float32) + reducer_bias.astype(jnp.float32)
    block_output = (middle + gate_two * feed).astype(jnp.bfloat16)
    grad_output = cotangent.astype(jnp.float32)
    grad_feed = (gate_two * grad_output).astype(jnp.bfloat16)
    grad_gate_two = jnp.sum(grad_output * feed, 1, keepdims=True)
    grad_feed_rows = lax.all_gather(grad_feed, "tp", axis=1, tiled=True)
    grad_reducer = jnp.einsum(
        "btf,btd->fd", activated_low, grad_feed_rows, preferred_element_type=jnp.float32
    )
    grad_reducer_bias = jnp.sum(grad_feed_rows, (0, 1), dtype=jnp.float32)
    grad_activated = jnp.einsum(
        "btd,fd->btf", grad_feed_rows, full_reducer, preferred_element_type=jnp.float32
    )
    grad_hidden = gelu_back(grad_activated)[0].astype(jnp.bfloat16)
    grad_expander = jnp.einsum(
        "btd,btf->df", row_block_two, grad_hidden, preferred_element_type=jnp.float32
    )
    grad_expander_bias = jnp.sum(grad_hidden, (0, 1), dtype=jnp.float32)
    normed_two_terms = jnp.einsum(
        "btf,df->btd", grad_hidden, full_expander, preferred_element_type=jnp.float32
    )
    grad_normed_two = lax.psum_scatter(normed_two_terms, "tp", scatter_dimension=1, tiled=True)
    grad_middle_norm, grad_scale_two, grad_shift_two = norm_back_two(grad_normed_two)
    grad_middle = grad_output + grad_middle_norm
    grad_gate_one = jnp.sum(grad_middle * branch, 1, keepdims=True)
    grad_branch = (gate_one * grad_middle).astype(jnp.bfloat16)
    grad_branch_rows = lax.all_gather(grad_branch, "tp", axis=1, tiled=True)
    grad_merger = jnp.einsum(
        "bth,btd->hd", attended_low, grad_branch_rows, preferred_element_type=jnp.float32
    )
    grad_merger_bias = jnp.sum(grad_branch_rows, (0, 1), dtype=jnp.float32)
    grad_attended = jnp.einsum(
        "btd,hd->bth", grad_branch_rows, full_merger, preferred_element_type=jnp.float32
    ).astype(jnp.bfloat16)
    grad_queries, grad_key_all, grad_value_all = lax.map(
        attend_back, (queries, key_all, value_all, grad_attended, logsum)
    )
    grad_keys, grad_values = (
        lax.psum_scatter(
            grad_key_all.astype(jnp.bfloat16), "ctx", scatter_dimension=1, tiled=True
        ).astype(jnp.float32),
        lax.psum_scatter(
            grad_value_all.astype(jnp.bfloat16), "ctx", scatter_dimension=1, tiled=True
        ).astype(jnp.float32),
    )
    grad_qkv = jnp.concatenate(
        [
            grad_queries.astype(jnp.bfloat16),
            grad_keys.astype(jnp.bfloat16),
            grad_values.astype(jnp.bfloat16),
        ],
        2,
    )
    grad_projector = jnp.einsum(
        "btd,bte->de", row_block, grad_qkv, preferred_element_type=jnp.float32
    ).reshape(model_width, 3, local_width)
    column_sums = jnp.sum(grad_qkv, (0, 1), dtype=jnp.float32)
    grad_projector_bias = jnp.stack([column_sums[:local_width], column_sums[2 * local_width :]])
    normed_terms = jnp.einsum(
        "bte,de->btd", grad_qkv, flat_projector, preferred_element_type=jnp.float32
    )
    grad_normed = lax.psum_scatter(
        normed_terms.astype(jnp.bfloat16), "tp", scatter_dimension=1, tiled=True
    ).astype(jnp.float32)
    grad_latent_norm, grad_scale_one, grad_shift_one = norm_back(grad_normed)
    grad_latent = grad_middle + grad_latent_norm
    setting_terms = jnp.concatenate(
        [
            grad_shift_one,
            grad_scale_one,
            grad_gate_one,
            grad_shift_two,
            grad_scale_two,
            grad_gate_two,
        ],
        2,
    )[:, 0, :]
    grad_settings = lax.psum(setting_terms, ("ctx", "tp"))
    grad_gate_input = jnp.dot(
        grad_settings, full_modulator.astype(jnp.float32).T, precision=PRECISE
    )
    grad_condition = silu_back(grad_gate_input)[0]
    column_count = grad_settings.shape[1] // lax.axis_size("tp")
    leading = (lax.axis_index("ctx") == 0).astype(jnp.float32)
    own_scaled = scaled.astype(jnp.float32) * leading
    own_settings = lax.dynamic_slice_in_dim(
        grad_settings, lax.axis_index("tp") * column_count, column_count, 1
    )
    grad_modulator = jnp.dot(own_scaled.T, own_settings, precision=PRECISE)
    grad_modulator_bias = jnp.sum(own_settings, 0) * leading
    weight_parts = (
        lax.psum_scatter(grad_modulator, ("shard", "ctx"), scatter_dimension=0, tiled=True),
        lax.psum_scatter(grad_projector, ("shard", "ctx"), scatter_dimension=0, tiled=True),
        lax.psum_scatter(grad_merger, ("shard", "ctx"), scatter_dimension=1, tiled=True),
        lax.psum_scatter(grad_expander, ("shard", "ctx"), scatter_dimension=0, tiled=True),
        lax.psum_scatter(grad_reducer, ("shard", "ctx"), scatter_dimension=1, tiled=True),
    )
    bias_parts = lax.psum(
        (
            grad_modulator_bias,
            grad_projector_bias,
            grad_merger_bias,
            grad_expander_bias,
            grad_reducer_bias,
        ),
        ("shard", "ctx"),
    )
    return (
        block_output,
        grad_latent,
        grad_condition,
        weight_parts[0],
        bias_parts[0],
        weight_parts[1],
        bias_parts[1],
        weight_parts[2],
        bias_parts[2],
        weight_parts[3],
        bias_parts[3],
        weight_parts[4],
        bias_parts[4],
    )


def solution(mesh):
    in_specs = (
        P("shard", ("ctx", "tp"), None),
        P("shard", None),
        P("shard", None),
        P(),
        P("shard", None, "tp"),
        P(None, "tp"),
        P("tp", "shard"),
        P(),
        P("shard", "tp"),
        P("tp"),
        P("tp", "shard"),
        P(),
        P("shard", ("ctx", "tp"), None),
    )
    out_specs = (
        P("shard", ("ctx", "tp"), None),
        P("shard", ("ctx", "tp"), None),
        P("shard", None),
        P(("shard", "ctx"), "tp"),
        P("tp"),
        P(("shard", "ctx"), None, "tp"),
        P(None, "tp"),
        P("tp", ("shard", "ctx")),
        P(),
        P(("shard", "ctx"), "tp"),
        P("tp"),
        P("tp", ("shard", "ctx")),
        P(),
    )
    return jax.shard_map(shards, mesh=mesh, in_specs=in_specs, out_specs=out_specs, check_vma=False)
```

profile of v0, /device:TPU:0, one launch (start us, length us, event | category | flops | bytes accessed | tf_op | source)
XLA Modules:
  0.0 1543.0 jit_solution(14418516819414383911)
XLA Ops:
  11.4 77.9 %all-gather.10.cloned.1.call-done = bf16[768,4608]{1,0:T(8,128)(2,1)} async-done(((bf16[192,4608]{1,0:T(8,128)(2,1)}), bf16[768,4608]{1,0:T(8,128)(2,1)}) %all-gather.10.cloned.1.call-update) | async-done | bytes 7077904 | tf_op jit(solution)/shard_map/all_gather | solution.py:157
  96.2 17.7 %all_gather.35 = bf16[768,3,192]{2,1,0:T(4,128)(2,1)S(1)} all-gather(bf16[192,3,192]{2,1,0:T(4,128)(2,1)S(1)} %copy.37), channel_id=1, replica_groups=mesh['shard'=4,'ctx'=2,'tp'=4] {'shard'}, dimensions={0}, use_global_device_ids=true | all-gather | bytes 1105920 | tf_op jit(solution)/shard_map/all_gather | solution.py:158
  114.8 44.8 %all-gather.12.cloned.1.call-done = bf16[1,2048,768]{2,1,0:T(8,128)(2,1)} async-done(((bf16[1,512,768]{2,1,0:T(8,128)(2,1)}), bf16[1,2048,768]{2,1,0:T(8,128)(2,1)}) %all-gather.12.cloned.1.call-update) | async-done | bytes 3145744 | tf_op jit(solution)/shard_map/all_gather | solution.py:177
  188.4 124.7 %while.47 = (s32[]{:T(128)}, bf16[4,512,192]{1,2,0:T(8,128)(2,1)S(1)}, f32[4,3,512]{2,1,0:T(4,128)}, bf16[4,512,192]{1,2,0:T(8,128)(2,1)}, bf16[4096,192]{0,1:T(...) while((s32[]{:T(128)}, bf16[4,512,192]{1,2,0:T(8,128)(2,1)S(1)}, f32[4,3,512]{2,1,0:T(4,128)}, ...), condition=%wide.region_5.6_spmd, body=%wide.region_2.5_spmd.sunk | while | flops 1667234304 | bytes 180537456 | solution.py:78
  207.6 11.4 fusion.121
  318.5 111.4 %reduce-scatter.14.cloned.1.call-done = f32[1,512,768]{2,1,0:T(8,128)} async-done(((f32[1,2048,768]{2,1,0:T(8,128)}), f32[1,512,768]{2,1,0:T(8,128)}) %reduce-scatter.14.cloned.1.call-update) | async-done | bytes 1572880 | tf_op jit(solution)/shard_map/reduce_scatter | solution.py:197
  435.6 24.2 %all-gather.20.cloned.1.call-done = bf16[768,768]{1,0:T(8,128)(2,1)} async-done(((bf16[192,768]{1,0:T(8,128)(2,1)}), bf16[768,768]{1,0:T(8,128)(2,1)}) %all-gather.20.cloned.1.call-update) | async-done | bytes 1179664 | tf_op jit(solution)/shard_map/all_gather | solution.py:160
  459.9 65.7 %all-gather.18.cloned.1.call-done = bf16[1,2048,768]{2,1,0:T(8,128)(2,1)} async-done(((bf16[1,512,768]{2,1,0:T(8,128)(2,1)}), bf16[1,2048,768]{2,1,0:T(8,128)(2,1)}) %all-gather.18.cloned.1.call-update) | async-done | bytes 3145744 | tf_op jit(solution)/shard_map/all_gather | solution.py:202
  533.1 20.7 %all-gather.22.cloned.1.call-done = bf16[768,768]{0,1:T(8,128)(2,1)} async-done(((bf16[768,192]{0,1:T(8,128)(2,1)}), bf16[768,768]{0,1:T(8,128)(2,1)}) %all-gather.22.cloned.1.call-update) | async-done | bytes 1179664 | tf_op jit(solution)/shard_map/all_gather | solution.py:161
  553.8 65.7 %all-gather.24.cloned.1.call-done = bf16[1,2048,768]{2,1,0:T(8,128)(2,1)} async-done(((bf16[1,512,768]{2,1,0:T(8,128)(2,1)}), bf16[1,2048,768]{2,1,0:T(8,128)(2,1)}) %all-gather.24.cloned.1.call-update) | async-done | bytes 3145744 | tf_op jit(solution)/shard_map/all_gather | solution.py:218
  646.1 100.0 %reduce-scatter.18.cloned.1.call-done = f32[1,512,768]{2,1,0:T(8,128)} async-done(((f32[1,2048,768]{2,1,0:T(8,128)}), f32[1,512,768]{2,1,0:T(8,128)}) %reduce-scatter.18.cloned.1.call-update) | async-done | bytes 1572880 | tf_op jit(solution)/shard_map/reduce_scatter | solution.py:234
  748.7 60.5 %reduce-scatter.16.cloned.1.call-done = bf16[1,512,768]{2,1,0:T(8,128)(2,1)} async-done(((bf16[1,2048,768]{2,1,0:T(8,128)(2,1)}), bf16[1,512,768]{2,1,0:T(8,128)(2,1)}) %reduce-scatter.16.cloned.1.call-update) | async-done | bytes 786448 | tf_op jit(solution)/shard_map/reduce_scatter | solution.py:211
  814.9 63.6 %all-gather.26.cloned.1.call-done = bf16[1,2048,768]{2,1,0:T(8,128)(2,1)} async-done(((bf16[1,512,768]{2,1,0:T(8,128)(2,1)}), bf16[1,2048,768]{2,1,0:T(8,128)(2,1)}) %all-gather.26.cloned.1.call-update) | async-done | bytes 3145744 | tf_op jit(solution)/shard_map/all_gather | solution.py:239
  883.5 329.2 %while.48 = (s32[]{:T(128)}, f32[4096,192]{0,1:T(8,128)}, f32[4096,192]{0,1:T(8,128)}, bf16[4,512,192]{1,2,0:T(8,128)(2,1)}, bf16[4,512,192]{1,2,0:T(8,128)(2,1)...) while((s32[]{:T(128)}, f32[4096,192]{0,1:T(8,128)}, ...), condition=%wide.region_15.16_spmd.clone, body=%wide.region_13.15_spmd.clone.sunk | while | flops 4106156544 | bytes 271165696 | solution.py:133
  886.2 11.5 fusion.132
  907.9 16.5 %multiply_reduce_fusion.10 = (f32[3,512]{1,0:T(4,128)S(1)}, f32[3,512,4096]{2,1,0:T(8,128)}) fusion(f32[3,512,4096]{2,1,0:T(8,128)} %fusion.132, f32[3,512]{1,0:T(4,128)S(1)} %dynamic-slice_bitcast_fusion.2, bf16[512,3,64]{0,2,1:T(8,128)(2,1)S(1)} %bitcast.189, bf16[4096,3,64]{0,2,1:T(8,128)(2,1)} %bitcast.184), kind=kOutput, calls=%fused_computation.10.clone.1 | convolution fusion | flops 830470656 | bytes 52113408 | tf_op jit(solution)/shard_map/while/body/eval_jaxpr/while/body/eval_jaxpr/qhd,khd->hqk/dot_general | solution.py:88
  924.4 21.1 %multiply_convert_fusion.6 = bf16[3,512,4096]{2,1,0:T(8,128)(2,1)} fusion(f32[3,512,4096]{2,1,0:T(8,128)} %get-tuple-element.389, f32[3,512,4096]{2,1,0:T(8,128)} %fusion.132, f32[3,512]{1,0:T(4,128)S(1)} %get-tuple-element.390, f32[3,512]{1,0:T(4,128)S(1)} %dynamic-slice_bitcast_fusion.2), kind=kLoop, calls=%fused_computation.9.clone.1 | loop fusion | flops 31457280 | bytes 62926848 | tf_op jit(solution)/shard_map/while/body/eval_jaxpr/while/body/eval_jaxpr/convert_element_type | solution.py:120
  968.4 11.5 fusion.132
  990.1 16.5 %multiply_reduce_fusion.10 = (f32[3,512]{1,0:T(4,128)S(1)}, f32[3,512,4096]{2,1,0:T(8,128)}) fusion(f32[3,512,4096]{2,1,0:T(8,128)} %fusion.132, f32[3,512]{1,0:T(4,128)S(1)} %dynamic-slice_bitcast_fusion.2, bf16[512,3,64]{0,2,1:T(8,128)(2,1)S(1)} %bitcast.189, bf16[4096,3,64]{0,2,1:T(8,128)(2,1)} %bitcast.184), kind=kOutput, calls=%fused_computation.10.clone.1 | convolution fusion | flops 830470656 | bytes 52113408 | tf_op jit(solution)/shard_map/while/body/eval_jaxpr/while/body/eval_jaxpr/qhd,khd->hqk/dot_general | solution.py:88
  1006.6 21.1 %multiply_convert_fusion.6 = bf16[3,512,4096]{2,1,0:T(8,128)(2,1)} fusion(f32[3,512,4096]{2,1,0:T(8,128)} %get-tuple-element.389, f32[3,512,4096]{2,1,0:T(8,128)} %fusion.132, f32[3,512]{1,0:T(4,128)S(1)} %get-tuple-element.390, f32[3,512]{1,0:T(4,128)S(1)} %dynamic-slice_bitcast_fusion.2), kind=kLoop, calls=%fused_computation.9.clone.1 | loop fusion | flops 31457280 | bytes 62926848 | tf_op jit(solution)/shard_map/while/body/eval_jaxpr/while/body/eval_jaxpr/convert_element_type | solution.py:120
  1050.6 11.5 fusion.132
  1072.3 16.5 %multiply_reduce_fusion.10 = (f32[3,512]{1,0:T(4,128)S(1)}, f32[3,512,4096]{2,1,0:T(8,128)}) fusion(f32[3,512,4096]{2,1,0:T(8,128)} %fusion.132, f32[3,512]{1,0:T(4,128)S(1)} %dynamic-slice_bitcast_fusion.2, bf16[512,3,64]{0,2,1:T(8,128)(2,1)S(1)} %bitcast.189, bf16[4096,3,64]{0,2,1:T(8,128)(2,1)} %bitcast.184), kind=kOutput, calls=%fused_computation.10.clone.1 | convolution fusion | flops 830470656 | bytes 52113408 | tf_op jit(solution)/shard_map/while/body/eval_jaxpr/while/body/eval_jaxpr/qhd,khd->hqk/dot_general | solution.py:88
  1088.8 21.1 %multiply_convert_fusion.6 = bf16[3,512,4096]{2,1,0:T(8,128)(2,1)} fusion(f32[3,512,4096]{2,1,0:T(8,128)} %get-tuple-element.389, f32[3,512,4096]{2,1,0:T(8,128)} %fusion.132, f32[3,512]{1,0:T(4,128)S(1)} %get-tuple-element.390, f32[3,512]{1,0:T(4,128)S(1)} %dynamic-slice_bitcast_fusion.2), kind=kLoop, calls=%fused_computation.9.clone.1 | loop fusion | flops 31457280 | bytes 62926848 | tf_op jit(solution)/shard_map/while/body/eval_jaxpr/while/body/eval_jaxpr/convert_element_type | solution.py:120
  1132.9 11.5 fusion.132
  1154.5 16.5 %multiply_reduce_fusion.10 = (f32[3,512]{1,0:T(4,128)S(1)}, f32[3,512,4096]{2,1,0:T(8,128)}) fusion(f32[3,512,4096]{2,1,0:T(8,128)} %fusion.132, f32[3,512]{1,0:T(4,128)S(1)} %dynamic-slice_bitcast_fusion.2, bf16[512,3,64]{0,2,1:T(8,128)(2,1)S(1)} %bitcast.189, bf16[4096,3,64]{0,2,1:T(8,128)(2,1)} %bitcast.184), kind=kOutput, calls=%fused_computation.10.clone.1 | convolution fusion | flops 830470656 | bytes 52113408 | tf_op jit(solution)/shard_map/while/body/eval_jaxpr/while/body/eval_jaxpr/qhd,khd->hqk/dot_general | solution.py:88
  1171.0 21.1 %multiply_convert_fusion.6 = bf16[3,512,4096]{2,1,0:T(8,128)(2,1)} fusion(f32[3,512,4096]{2,1,0:T(8,128)} %get-tuple-element.389, f32[3,512,4096]{2,1,0:T(8,128)} %fusion.132, f32[3,512]{1,0:T(4,128)S(1)} %get-tuple-element.390, f32[3,512]{1,0:T(4,128)S(1)} %dynamic-slice_bitcast_fusion.2), kind=kLoop, calls=%fused_computation.9.clone.1 | loop fusion | flops 31457280 | bytes 62926848 | tf_op jit(solution)/shard_map/while/body/eval_jaxpr/while/body/eval_jaxpr/convert_element_type | solution.py:120
  1272.5 33.4 %reduce-scatter.24.cloned.1.call-done = bf16[1,512,768]{2,1,0:T(8,128)(2,1)} async-done(((bf16[1,2048,768]{2,1,0:T(8,128)(2,1)}), bf16[1,512,768]{2,1,0:T(8,128)(2,1)}) %reduce-scatter.24.cloned.1.call-update) | async-done | bytes 786448 | tf_op jit(solution)/shard_map/reduce_scatter | solution.py:274
  1312.2 27.8 %psum.42 = f32[1,4608]{1,0:T(1,128)S(1)} all-reduce(f32[1,4608]{1,0:T(1,128)S(1)} %bitcast.201), channel_id=1, replica_groups=mesh['shard'=4,'ctx'=2,'tp'=4] {'ctx','tp'}, use_global_device_ids=true, to_apply=%region_27.28 | all-reduce | flops 4608 | bytes 36864 | tf_op jit(solution)/shard_map/psum | solution.py:290
  1349.2 25.5 %all-reduce = (f32[1152]{0:T(1024)}, f32[2,192]{1,0:T(2,128)}, f32[768]{0:T(1024)}, f32[768]{0:T(1024)}, f32[768]{0:T(1024)}) all-reduce(f32[1152]{0:T(1024)S(1)} %broadcast_multiply_fusion.1, f32[2,192]{1,0:T(2,128)S(1)} %pad_maximum_fusion, ...), channel_id=1, replica_groups=mesh['shard'=4,'ctx'=2,'tp'=4] {'shard','ctx'}, use_global_device_ids=true, to_apply=%region_29.30 | all-reduce | flops 3840 | bytes 30720 | tf_op jit(solution)/shard_map/psum | solution.py:310
  1390.2 46.6 %reduce-scatter.30.cloned.1.call-done = f32[96,768]{1,0:T(8,128)} async-done(((f32[768,768]{1,0:T(8,128)}), f32[96,768]{1,0:T(8,128)}) %reduce-scatter.30.cloned.1.call-update) | async-done | bytes 294928 | tf_op jit(solution)/shard_map/reduce_scatter | solution.py:307
  1436.9 46.4 %reduce-scatter.28.cloned.1.call-done = f32[96,3,192]{2,0,1:T(8,128)} async-done(((f32[768,3,192]{2,0,1:T(8,128)}), f32[96,3,192]{2,0,1:T(8,128)}) %reduce-scatter.28.cloned.1.call-update) | async-done | bytes 221200 | tf_op jit(solution)/shard_map/reduce_scatter | solution.py:305
  1483.3 52.4 %reduce-scatter.26.cloned.1.call-done = f32[96,1152]{1,0:T(8,128)} async-done(((f32[768,1152]{1,0:T(8,128)}), f32[96,1152]{1,0:T(8,128)}) %reduce-scatter.26.cloned.1.call-update) | async-done | bytes 442384 | tf_op jit(solution)/shard_map/reduce_scatter | solution.py:304
  (327 shorter events, 434.7 us)
Async XLA Ops:
  7.2 82.1 %all-gather.10.cloned.1.call-start = ((), (), s32[]{:S(2)}) async-start(), calls=%async_computation.11 | async-start | bytes 8847360 | tf_op jit(solution)/shard_map/all_gather | solution.py:157
  7.9 151.6 %all-gather.12.cloned.1.call-start = ((), (), s32[]{:S(2)}) async-start(), calls=%async_computation.12 | async-start | bytes 3932160 | tf_op jit(solution)/shard_map/all_gather | solution.py:177
  9.3 84.8 %copy-start.28 = (f32[512]{0:T(512)}, f32[512]{0:T(512)S(1)}, u32[]{:S(2)}) copy-start(f32[512]{0:T(512)S(1)} %broadcast_multiply_fusion.3) | copy-start | bytes 6148
  11.4 82.7 %copy-start.37 = (f32[512]{0:T(512)}, f32[512]{0:T(512)S(1)}, u32[]{:S(2)}) copy-start(f32[512]{0:T(512)S(1)} %fusion.67) | copy-start | bytes 6148
  11.4 83.2 %copy-start.6 = (bf16[1,512,768]{2,1,0:T(8,128)(2,1)S(1)}, bf16[1,512,768]{2,1,0:T(8,128)(2,1)}, u32[]{:S(2)}) copy-start(bf16[1,512,768]{2,1,0:T(8,128)(2,1)} %param.17) | copy-start | bytes 2359300
  11.4 84.5 %copy-start.24 = (bf16[192,3,192]{2,0,1:T(8,128)(2,1)S(1)}, bf16[192,3,192]{2,0,1:T(8,128)(2,1)}, u32[]{:S(2)}) copy-start(bf16[192,3,192]{2,0,1:T(8,128)(2,1)} %param.21) | copy-start | bytes 663556
  95.9 85.5 %all-gather.16.cloned.1.call-start = ((), (), s32[]{:S(2)}) async-start(), calls=%async_computation.14 | async-start | bytes 2359296 | tf_op jit(solution)/shard_map/all_gather | solution.py:190
  166.7 21.6 %all-gather.14.cloned.1.call-start = ((), (), s32[]{:S(2)}) async-start(), calls=%async_computation.13 | async-start | bytes 2359296 | tf_op jit(solution)/shard_map/all_gather | solution.py:189
  169.2 260.7 %reduce-scatter.14.cloned.1.call-start = ((), (), s32[]{:S(2)}) async-start(), calls=%async_computation.15 | async-start | bytes 7864320 | tf_op jit(solution)/shard_map/reduce_scatter | solution.py:197
  188.4 125.7 %copy-start.20 = (bf16[192,768]{0,1:T(8,128)(2,1)S(1)}, bf16[192,768]{0,1:T(8,128)(2,1)}, u32[]{:S(2)}) copy-start(bf16[192,768]{0,1:T(8,128)(2,1)} %all_gather.38) | copy-start | bytes 884740
  317.8 112.1 %copy-start.7 = (bf16[1,512,768]{2,1,0:T(8,128)(2,1)S(1)}, bf16[1,512,768]{2,1,0:T(8,128)(2,1)}, u32[]{:S(2)}) copy-start(bf16[1,512,768]{2,1,0:T(8,128)(2,1)} %param.17) | copy-start | bytes 2359300
  317.8 112.1 %copy-start.33 = (f32[768]{0:T(1024)S(1)}, f32[768]{0:T(1024)}, u32[]{:S(2)}) copy-start(f32[768]{0:T(1024)} %get-tuple-element.233) | copy-start | bytes 9220
  317.8 114.2 %copy-start.30 = (f32[768]{0:T(1024)S(1)}, f32[768]{0:T(1024)}, u32[]{:S(2)}) copy-start(f32[768]{0:T(1024)} %get-tuple-element.230) | copy-start | bytes 9220
  317.8 114.2 %copy-start.47 = (f32[768]{0:T(1024)S(1)}, f32[768]{0:T(1024)}, u32[]{:S(2)}) copy-start(f32[768]{0:T(1024)} %get-tuple-element.229) | copy-start | bytes 9220
  317.8 142.0 %all-gather.20.cloned.1.call-start = ((), (), s32[]{:S(2)}) async-start(), calls=%async_computation.17 | async-start | bytes 1474560 | tf_op jit(solution)/shard_map/all_gather | solution.py:160
  318.4 207.1 %all-gather.18.cloned.1.call-start = ((), (), s32[]{:S(2)}) async-start(), calls=%async_computation.16 | async-start | bytes 3932160 | tf_op jit(solution)/shard_map/all_gather | solution.py:202
  318.5 113.2 %copy-start.31 = (f32[768]{0:T(1024)}, f32[768]{0:T(1024)S(1)}, u32[]{:S(2)}) copy-start(f32[768]{0:T(1024)S(1)} %convert_element_type.195) | copy-start | bytes 9220
  433.2 120.5 %all-gather.22.cloned.1.call-start = ((), (), s32[]{:S(2)}) async-start(), calls=%async_computation.18 | async-start | bytes 1474560 | tf_op jit(solution)/shard_map/all_gather | solution.py:161
  434.0 185.5 %all-gather.24.cloned.1.call-start = ((), (), s32[]{:S(2)}) async-start(), calls=%async_computation.20 | async-start | bytes 3932160 | tf_op jit(solution)/shard_map/all_gather | solution.py:218
  435.1 311.0 %reduce-scatter.18.cloned.1.call-start = ((), (), s32[]{:S(2)}) async-start(), calls=%async_computation.21 | async-start | bytes 7864320 | tf_op jit(solution)/shard_map/reduce_scatter | solution.py:234
  435.6 200.9 %copy-start.49 = (f32[768]{0:T(1024)}, f32[768]{0:T(1024)S(1)}, u32[]{:S(2)}) copy-start(f32[768]{0:T(1024)S(1)} %convert_element_type.197) | copy-start | bytes 9220
  636.5 172.7 %reduce-scatter.16.cloned.1.call-start = ((), (), s32[]{:S(2)}) async-start(), calls=%async_computation.19 | async-start | bytes 3932160 | tf_op jit(solution)/shard_map/reduce_scatter | solution.py:211
  645.4 233.0 %all-gather.26.cloned.1.call-start = ((), (), s32[]{:S(2)}) async-start(), calls=%async_computation.22 | async-start | bytes 3932160 | tf_op jit(solution)/shard_map/all_gather | solution.py:239
  646.1 166.3 %copy-start.34 = (f32[768]{0:T(1024)}, f32[768]{0:T(1024)S(1)}, u32[]{:S(2)}) copy-start(f32[768]{0:T(1024)S(1)} %convert_element_type.202) | copy-start | bytes 9220
  814.8 409.2 %reduce-scatter.20.cloned.1.call-start = ((), (), s32[]{:S(2)}) async-start(), calls=%async_computation.23 | async-start | bytes 2359296 | tf_op jit(solution)/shard_map/reduce_scatter | solution.py:251
  1216.1 20.4 %reduce-scatter.22.cloned.1.call-start = ((), (), s32[]{:S(2)}) async-start(), calls=%async_computation.24 | async-start | bytes 2359296 | tf_op jit(solution)/shard_map/reduce_scatter | solution.py:254
  1217.6 88.3 %reduce-scatter.24.cloned.1.call-start = ((), (), s32[]{:S(2)}) async-start(), calls=%async_computation.25 | async-start | bytes 3932160 | tf_op jit(solution)/shard_map/reduce_scatter | solution.py:274
  1244.3 101.1 %reduce-scatter.34.cloned.1.call-start = ((), (), s32[]{:S(2)}) async-start(), calls=%async_computation.30 | async-start | bytes 884736
  1249.5 140.7 %reduce-scatter.32.cloned.1.call-start = ((), (), s32[]{:S(2)}) async-start(), calls=%async_computation.29 | async-start | bytes 2654208 | tf_op jit(solution)/shard_map/reduce_scatter | solution.py:308
  1258.7 178.1 %reduce-scatter.30.cloned.1.call-start = ((), (), s32[]{:S(2)}) async-start(), calls=%async_computation.28 | async-start | bytes 2654208 | tf_op jit(solution)/shard_map/reduce_scatter | solution.py:307
  1266.0 217.3 %reduce-scatter.28.cloned.1.call-start = ((), (), s32[]{:S(2)}) async-start(), calls=%async_computation.27 | async-start | bytes 2654208 | tf_op jit(solution)/shard_map/reduce_scatter | solution.py:305
  1272.5 263.2 %reduce-scatter.26.cloned.1.call-start = ((), (), s32[]{:S(2)}) async-start(), calls=%async_computation.26 | async-start | bytes 3981312 | tf_op jit(solution)/shard_map/reduce_scatter | solution.py:304
  (61 other events, 868.2 us)
Sparse Core Ops, SparseCore 0:
  9.9 79.3 all-gather.9
  96.0 63.4 all-gather.11
  166.8 8.4 all-gather.15
  177.3 10.9 all-gather.13
  317.9 111.9 reduce-scatter.13
  431.6 28.2 all-gather.19
  462.0 63.4 all-gather.17
  527.4 26.3 all-gather.21
  555.9 63.4 all-gather.23
  636.6 109.3 reduce-scatter.17
  748.4 60.7 reduce-scatter.15
  814.9 63.5 all-gather.25
  1216.2 7.7 reduce-scatter.19
  1226.2 10.2 reduce-scatter.21
  1244.4 61.4 reduce-scatter.23
  1308.9 35.0 reduce-scatter.33
  1347.7 42.4 reduce-scatter.31
  1394.4 42.4 reduce-scatter.29
  1440.8 42.4 reduce-scatter.27
  1487.6 48.0 reduce-scatter.25
where the time goes:
time: 1550 us; the launch traced here: 1540 us
  waiting for transfers between devices  845 us (55%)
  matrix products  367 us (24%)
  other arithmetic  149 us (10%)
  local copies, waits for them, and re-layouts  83.2 us (5%)
  blocking collectives  81.4 us (5%)
  between operations  15.6 us (1%)
    reduce_scatter x1, waiting for transfers between devices, shards(): lax.psum_scatter(merge_terms, 'tp', scatter_dimension=1, tiled=True)  111 us
    reduce_scatter x1, waiting for transfers between devices, shards(): lax.psum_scatter(normed_two_terms, 'tp', scatter_dimension=1, tiled=True)  100 us
    convert_element_type x4, other arithmetic, one_block(): grad_scores = (softmaxed * (grad_probs - inner)).astype(jnp.bfloat16)  84.6 us
    all_gather x1, waiting for transfers between devices, shards(): lax.all_gather(modulator, 'shard', axis=0, tiled=True)  77.9 us
    dot_general x4, matrix products, probs_and_grads(): jnp.einsum('qhd,khd->hqk', split_heads(grad_rows), split_heads(value_rows...  65.8 us
    dot_general x8, matrix products, score_block(): jnp.einsum('qhd,khd->hqk', query_heads, key_heads, preferred_element_type...  65.8 us
    all_gather x1, waiting for transfers between devices, shards(): grad_feed_rows = lax.all_gather(grad_feed, 'tp', axis=1, tiled=True)  65.7 us
    all_gather x1, waiting for transfers between devices, shards(): lax.all_gather(normed_two_wide.astype(jnp.bfloat16), 'tp', axis=1, tiled=...  65.7 us
  transfers between devices with their start and end apart: 20, of which 18 were waited for; matrix products, arithmetic and copies ran while one was open for 6% of the time, Pallas kernels for 0%

commit v1 on v0

v1 whole, which is shorter than its diff:
```python
import functools
import math

import jax
import jax.numpy as jnp
from jax import lax
from jax.experimental import pallas as pl
from jax.experimental.pallas import tpu as pltpu
from jax.sharding import PartitionSpec as P

HEAD_DIM = 64
PRECISE = lax.Precision.HIGHEST
LOW = jnp.bfloat16
WIDE = jnp.float32


def layer_norm(values):
    row_mean = jnp.mean(values, -1, keepdims=True)
    centered = values - row_mean
    variance = jnp.mean(centered * centered, -1, keepdims=True)
    return centered * lax.rsqrt(variance + 1e-06)


def gelu_tanh(values):
    return (
        0.5
        * values
        * (1.0 + jnp.tanh(0.7978845608028654 * (values + 0.044715 * values * values * values)))
    )


def silu_gate(values):
    return values * jax.nn.sigmoid(values)


def modulate(values, scale_part, shift_part):
    return layer_norm(values) * (1.0 + scale_part) + shift_part


def dot_wide(left, right, left_dim, right_dim):
    return lax.dot_general(
        left, right, (((left_dim,), (right_dim,)), ((), ())), preferred_element_type=WIDE
    )


def gather_list(block, axis):
    count = lax.axis_size(axis)
    return [block] + [
        lax.ppermute(block, axis, [(i, (i - r) % count) for i in range(count)])
        for r in range(1, count)
    ]


def scatter_list(blocks, axis):
    count = lax.axis_size(axis)
    arrived = {
        (count - r) % count: lax.ppermute(
            blocks[r], axis, [(i, (i + r) % count) for i in range(count)]
        )
        for r in range(1, count)
    }
    arrived[0] = blocks[0]
    return [arrived[r] for r in range(count)]


def swap_ctx(block):
    count = lax.axis_size("ctx")
    return lax.ppermute(block, "ctx", [(i, (i + 1) % count) for i in range(count)])


def sum_over(value, axes):
    for axis in axes:
        step = 1
        while step < lax.axis_size(axis):
            value = value + lax.ppermute(
                value, axis, [(i, i ^ step) for i in range(lax.axis_size(axis))]
            )
            step *= 2
    return value


def after(value, *earlier):
    return lax.optimization_barrier((value,) + tuple(earlier))[0]


def attend_kernel(query_ref, key_ref, value_ref, far_key_ref, far_value_ref, out_ref, stat_ref, key_rows):
    near = key_ref.shape[2]
    key_rows[:near, :] = key_ref[0].T
    key_rows[near:, :] = far_key_ref[0].T
    queries = query_ref[0] * jnp.array(HEAD_DIM ** (-0.5), LOW)
    columns = queries.shape[1]
    top = total = mixed = None
    for half, values in enumerate((value_ref, far_value_ref)):
        scores = jnp.dot(
            key_rows[half * near : (half + 1) * near, :], queries, preferred_element_type=WIDE
        )
        block_top = jnp.max(scores, 0, keepdims=True)
        new_top = block_top if top is None else jnp.maximum(top, block_top)
        exponent = jnp.exp(scores - new_top)
        block_total = jnp.sum(exponent, 0, keepdims=True)
        block_mixed = jnp.dot(values[0], exponent.astype(LOW), preferred_element_type=WIDE)
        if top is None:
            total, mixed = block_total, block_mixed
        else:
            fade = jnp.exp(top - new_top)
            total = total * fade + block_total
            mixed = mixed * fade + block_mixed
        top = new_top
    out_ref[0] = (mixed / total).astype(LOW)
    stat_ref[0] = top + jnp.log(total)


def attend(near_rows, far_rows, place, width):
    heads, _, tokens = near_rows.shape
    size = HEAD_DIM

    def whole(row):
        return pl.BlockSpec((1, size, tokens), lambda h: (h, row, 0))

    return pl.pallas_call(
        attend_kernel,
        grid=(heads,),
        in_specs=[
            pl.BlockSpec((1, size, width), lambda h: (h, 0, place)),
            whole(1),
            whole(2),
            whole(0),
            whole(1),
        ],
        out_specs=[
            pl.BlockSpec((1, size, width), lambda h: (h, 0, 0)),
            pl.BlockSpec((1, 1, width), lambda h: (h, 0, 0)),
        ],
        out_shape=[
            jax.ShapeDtypeStruct((heads, size, width), LOW),
            jax.ShapeDtypeStruct((heads, 1, width), WIDE),
        ],
        scratch_shapes=[pltpu.VMEM((2 * tokens, size), LOW)],
        compiler_params=pltpu.CompilerParams(vmem_limit_bytes=48 * 2**20),
        cost_estimate=pl.CostEstimate(
            flops=heads * 2 * tokens * width * size * 4 * 4,
            bytes_accessed=heads * size * (width * 4 + tokens * 8),
            transcendentals=heads * 2 * tokens * width,
        ),
    )(near_rows, near_rows, near_rows, far_rows, far_rows)


def with_parts(rows, extra):
    high = extra.astype(LOW)
    rest = extra - high.astype(WIDE)
    middle = rest.astype(LOW)
    lowest = (rest - middle.astype(WIDE)).astype(LOW)
    fill = jnp.zeros((HEAD_DIM - 3, rows.shape[1]), LOW)
    return jnp.concatenate([rows, high, middle, lowest, fill], 0)


def attend_back_kernel(
    key_block, query_block,
    near_ref, far_ref, grad_ref, out_ref, stat_ref,
    grad_near_ref, grad_far_ref,
    key_rows, value_rows, key_columns, query_rows, grad_rows, query_more, grad_more, query_sum,
):
    size = HEAD_DIM
    tokens = near_ref.shape[2]
    queries = near_ref[0, :size, :] * jnp.array(size ** (-0.5), LOW)
    grads = grad_ref[0]
    ones = jnp.where(lax.broadcasted_iota(jnp.int32, (2 * tokens, size), 1) < 3, 1.0, 0.0).astype(LOW)
    key_rows[:tokens, :size] = near_ref[0, size : 2 * size, :].T
    key_rows[tokens:, :size] = far_ref[0, :size, :].T
    key_rows[:, size:] = ones
    value_rows[:tokens, :size] = near_ref[0, 2 * size :, :].T
    value_rows[tokens:, :size] = far_ref[0, size:, :].T
    value_rows[:, size:] = ones
    key_columns[:, :tokens] = near_ref[0, size : 2 * size, :]
    key_columns[:, tokens:] = far_ref[0, :size, :]
    query_rows[...] = queries.T
    grad_rows[...] = grads.T
    inner = jnp.sum(grads.astype(WIDE) * out_ref[0].astype(WIDE), 0, keepdims=True)
    query_more[...] = with_parts(queries, -stat_ref[0])
    grad_more[...] = with_parts(grads, -inner)
    query_sum[...] = jnp.zeros_like(query_sum)

    def key_step(target, key_row, value_row, base):
        def step(index, carry):
            local = pl.ds(pl.multiple_of(index * key_block, key_block), key_block)
            place = pl.ds(pl.multiple_of(base + index * key_block, key_block), key_block)
            keys, values, columns = key_rows[place, :], value_rows[place, :], key_columns[:, place]
            key_sum = jnp.zeros((key_block, size), WIDE)
            value_sum = jnp.zeros((key_block, size), WIDE)
            for part in range(tokens // query_block):
                span = slice(part * query_block, (part + 1) * query_block)
                probs = jnp.exp(jnp.dot(keys, query_more[:, span], preferred_element_type=WIDE))
                centered = jnp.dot(values, grad_more[:, span], preferred_element_type=WIDE)
                grad_scores = (probs * centered).astype(LOW)
                value_sum += jnp.dot(probs.astype(LOW), grad_rows[span, :], preferred_element_type=WIDE)
                key_sum += jnp.dot(grad_scores, query_rows[span, :], preferred_element_type=WIDE)
                query_sum[:, span] += jnp.dot(columns, grad_scores, preferred_element_type=WIDE)
            target[0, key_row : key_row + size, local] = key_sum.T.astype(LOW)
            target[0, value_row : value_row + size, local] = value_sum.T.astype(LOW)
            return carry

        lax.fori_loop(0, tokens // key_block, step, 0)

    key_step(grad_far_ref, 0, size, tokens)
    key_step(grad_near_ref, size, 2 * size, 0)
    grad_near_ref[0, :size, :] = (query_sum[...] * size ** (-0.5)).astype(LOW)


def attend_back(head, near_rows, far_rows, grads, outs, stats):
    _, _, tokens = near_rows.shape
    size = HEAD_DIM
    key_block, query_block = math.gcd(tokens, 1024), math.gcd(tokens, 512)

    def rows(count):
        return pl.BlockSpec((1, count, tokens), lambda i: (head, 0, 0))

    def result(count):
        return pl.BlockSpec((1, count, tokens), lambda i: (0, 0, 0))

    return pl.pallas_call(
        functools.partial(attend_back_kernel, key_block, query_block),
        grid=(1,),
        in_specs=[rows(3 * size), rows(2 * size), rows(size), rows(size), rows(1)],
        out_specs=[result(3 * size), result(2 * size)],
        out_shape=[
            jax.ShapeDtypeStruct((1, 3 * size, tokens), LOW),
            jax.ShapeDtypeStruct((1, 2 * size, tokens), LOW),
        ],
        scratch_shapes=[
            pltpu.VMEM((2 * tokens, 2 * size), LOW),
            pltpu.VMEM((2 * tokens, 2 * size), LOW),
            pltpu.VMEM((size, 2 * tokens), LOW),
            pltpu.VMEM((tokens, size), LOW),
            pltpu.VMEM((tokens, size), LOW),
            pltpu.VMEM((2 * size, tokens), LOW),
            pltpu.VMEM((2 * size, tokens), LOW),
            pltpu.VMEM((size, tokens), WIDE),
        ],
        compiler_params=pltpu.CompilerParams(vmem_limit_bytes=48 * 2**20),
        cost_estimate=pl.CostEstimate(
            flops=2 * tokens * tokens * size * 10 * 4,
            bytes_accessed=size * tokens * 2 * 12,
            transcendentals=2 * tokens * tokens,
        ),
    )(near_rows, far_rows, grads, outs, stats)


def reduce_weight(grad, across_tp):
    ctx_size, shard_size = lax.axis_size("ctx"), lax.axis_size("shard")
    rows = grad.shape[0] // (shard_size * ctx_size)
    low = grad.astype(LOW).reshape(shard_size, ctx_size, rows, grad.shape[1])
    core = lax.axis_index("ctx")
    mine = lax.dynamic_index_in_dim(low, core, 1, keepdims=False)
    theirs = lax.dynamic_index_in_dim(low, 1 - core, 1, keepdims=False)
    half = (mine.astype(WIDE) + swap_ctx(theirs).astype(WIDE)).astype(LOW)
    own = lax.psum_scatter(
        half.reshape(shard_size * rows, grad.shape[1]), "shard", scatter_dimension=0, tiled=True
    )
    if not across_tp:
        return own.astype(WIDE)
    count = lax.axis_size("tp")
    width = grad.shape[1] // count
    parts = scatter_list([own[:, r * width : (r + 1) * width] for r in range(count)], "tp")
    return sum(part.astype(WIDE) for part in parts)


def shards(
    latent,
    condition,
    modulator,
    modulator_bias,
    projector,
    projector_bias,
    merger,
    merger_bias,
    expander,
    expander_bias,
    reducer,
    reducer_bias,
    cotangent,
):
    tp_size, ctx_size, shard_size = (lax.axis_size(axis) for axis in ("tp", "ctx", "shard"))
    core = lax.axis_index("ctx")
    own_latent, own_cotangent = latent[0], cotangent[0]
    block, model_width = own_latent.shape
    local_width = projector.shape[2]
    heads = local_width // HEAD_DIM
    local_hidden = expander.shape[1]
    kept_rows = projector.shape[0]

    latent_blocks = gather_list(own_latent, "tp")

    conditions = lax.all_gather(condition, "shard", axis=0, tiled=True)
    scaled_all = silu_gate(conditions.astype(WIDE)).astype(LOW)
    place = lax.axis_index("shard") * kept_rows
    terms = jnp.dot(
        lax.dynamic_slice_in_dim(scaled_all, place, kept_rows, 1),
        modulator,
        preferred_element_type=WIDE,
    )
    terms = lax.all_to_all(terms, "shard", 0, 0, tiled=True)
    modulation = jnp.sum(terms, 0, keepdims=True) + modulator_bias.astype(WIDE)
    settings = [
        modulation[:, index * model_width : (index + 1) * model_width] for index in range(6)
    ]
    shift_one, scale_one, gate_one, shift_two, scale_two, gate_two = settings

    own_projector = (
        projector.reshape(kept_rows, 3, heads, HEAD_DIM)
        .transpose(2, 1, 3, 0)
        .reshape(3 * local_width, kept_rows)
    )
    head_projector = lax.all_gather(own_projector, "shard", axis=1, tiled=True)
    zero_bias = jnp.zeros((1, local_width), projector_bias.dtype)
    qkv_bias = (
        jnp.concatenate([projector_bias[:1], zero_bias, projector_bias[1:]], 0)
        .reshape(3, heads, HEAD_DIM)
        .transpose(1, 0, 2)
        .reshape(3 * local_width, 1)
        .astype(WIDE)
    )

    normed_rows = jnp.concatenate(
        [modulate(rows.astype(WIDE), scale_one, shift_one).astype(LOW) for rows in latent_blocks], 0
    )
    tokens = normed_rows.shape[0]
    projected = (dot_wide(head_projector, normed_rows, 1, 1) + qkv_bias).astype(LOW)
    near_rows = projected.reshape(heads, 3 * HEAD_DIM, tokens)
    far_rows = swap_ctx(near_rows[:, HEAD_DIM:, :])

    half_hidden = local_hidden // ctx_size
    expander_half = lax.dynamic_slice_in_dim(expander, core * half_hidden, half_hidden, 1)
    reducer_half = lax.dynamic_slice_in_dim(reducer, core * half_hidden, half_hidden, 0).T
    pieces = jnp.concatenate([expander_half, reducer_half], 1)
    pieces = after(pieces, latent_blocks[1], latent_blocks[2 % tp_size], latent_blocks[3 % tp_size])
    pieces = jnp.stack(gather_list(pieces, "tp"))
    pieces = lax.all_gather(pieces, "shard", axis=1, tiled=True)
    other = swap_ctx(pieces)
    first, second = jnp.where(core == 0, pieces, other), jnp.where(core == 0, other, pieces)
    full_expander = jnp.concatenate(
        [part[r, :, :half_hidden] for r in range(tp_size) for part in (first, second)], 1
    )
    full_reducer = jnp.concatenate(
        [part[r, :, half_hidden:] for r in range(tp_size) for part in (first, second)], 1
    )
    merger_pieces = jnp.stack(gather_list(merger.T, "tp"))
    merger_pieces = lax.all_gather(merger_pieces, "shard", axis=1, tiled=True)
    full_merger = jnp.concatenate([merger_pieces[r] for r in range(tp_size)], 1)
    full_expander_bias = jnp.concatenate(gather_list(expander_bias, "tp")).astype(WIDE)

    outs, stats, sent = [None] * tp_size, [None] * tp_size, [None] * tp_size
    order = sorted(range(tp_size), key=lambda r: -min(r, tp_size - r))
    for r in order:
        outs[r], stats[r] = attend(near_rows, far_rows, r, block)
        sent[r] = outs[r].reshape(local_width, block)
    attended = jnp.concatenate(scatter_list(sent, "tp"), 0)
    all_outs, all_stats = jnp.concatenate(outs, 2), jnp.concatenate(stats, 2)

    latent_wide = own_latent.astype(WIDE)
    branch = dot_wide(attended, full_merger, 0, 1) + merger_bias.astype(WIDE)
    middle = latent_wide + gate_one * branch
    normed_two_wide, norm_back_two = jax.vjp(modulate, middle, scale_two, shift_two)
    normed_two = normed_two_wide.astype(LOW)
    hidden = dot_wide(normed_two, full_expander, 1, 0) + full_expander_bias
    activated, gelu_back = jax.vjp(gelu_tanh, hidden)
    activated_low = activated.astype(LOW)
    feed = dot_wide(activated_low, full_reducer, 1, 1) + reducer_bias.astype(WIDE)
    block_output = (middle + gate_two * feed).astype(LOW)
    grad_output = own_cotangent.astype(WIDE)
    grad_feed = (gate_two * grad_output).astype(LOW)
    grad_gate_two = jnp.sum(grad_output * feed, 0, keepdims=True)
    grad_activated = dot_wide(grad_feed, full_reducer, 1, 0)
    grad_hidden = gelu_back(grad_activated)[0].astype(LOW)
    grad_normed_two = dot_wide(grad_hidden, full_expander, 1, 1)
    grad_middle_norm, grad_scale_two, grad_shift_two = norm_back_two(grad_normed_two)
    grad_middle = grad_output + grad_middle_norm
    grad_gate_one = jnp.sum(grad_middle * branch, 0, keepdims=True)
    grad_branch = (gate_one * grad_middle).astype(LOW)
    grad_attended = dot_wide(full_merger, grad_branch, 0, 1).astype(LOW)
    grad_blocks = scatter_list(
        [grad_attended[r * local_width : (r + 1) * local_width] for r in range(tp_size)], "tp"
    )
    all_grads = jnp.concatenate(grad_blocks, 1).reshape(heads, HEAD_DIM, tokens)

    grad_reducer = reduce_weight(dot_wide(grad_feed, activated_low, 0, 0), True).T
    grad_expander = reduce_weight(dot_wide(normed_two, grad_hidden, 0, 0), True)
    grad_merger = reduce_weight(dot_wide(grad_branch, attended, 0, 1), True).T

    tail_projector = after(head_projector, all_outs)
    full_projector = jnp.concatenate(gather_list(tail_projector, "tp"), 0).reshape(
        tp_size, heads, 3 * HEAD_DIM, model_width
    )
    head_grads, grad_normed = [], 0.0
    for head in range(heads):
        near, far = attend_back(head, near_rows, far_rows, all_grads, all_outs, all_stats)
        shared = near[0, HEAD_DIM:].astype(WIDE) + swap_ctx(far[0]).astype(WIDE)
        rows = jnp.concatenate([near[0, :HEAD_DIM], shared.astype(LOW)], 0)
        head_grads.append(rows)
        arrived = scatter_list([rows[:, r * block : (r + 1) * block] for r in range(tp_size)], "tp")
        grad_normed = grad_normed + dot_wide(
            jnp.concatenate(arrived, 0),
            full_projector[:, head].reshape(tp_size * 3 * HEAD_DIM, model_width),
            0,
            0,
        )
    qkv_grads = jnp.concatenate(head_grads, 0)
    grad_projector = reduce_weight(dot_wide(normed_rows, qkv_grads, 0, 1), False)
    grad_projector = (
        grad_projector.reshape(-1, heads, 3, HEAD_DIM).transpose(0, 2, 1, 3).reshape(-1, 3, local_width)
    )
    _, norm_back = jax.vjp(modulate, latent_wide, scale_one, shift_one)
    grad_latent_norm, grad_scale_one, grad_shift_one = norm_back(grad_normed)
    grad_latent = grad_middle + grad_latent_norm

    token_bias = jnp.concatenate(
        [
            jnp.sum(grad_feed, 0, keepdims=True, dtype=WIDE),
            jnp.sum(grad_branch, 0, keepdims=True, dtype=WIDE),
        ],
        0,
    )
    token_bias = sum_over(token_bias, ("ctx", "tp", "shard"))
    hidden_bias = jnp.sum(grad_hidden, 0, dtype=WIDE).reshape(tp_size, 1, local_hidden)
    hidden_bias = sum(
        part
        for part in [
            hidden_bias[0],
            *(
                lax.ppermute(
                    hidden_bias[r], "tp", [(i, (i + r) % tp_size) for i in range(tp_size)]
                )
                for r in range(1, tp_size)
            ),
        ]
    )
    hidden_bias = sum_over(hidden_bias, ("ctx", "shard"))[0]
    column_sums = jnp.sum(qkv_grads, 1, dtype=WIDE).reshape(heads, 3, HEAD_DIM)
    projector_sums = sum_over(
        jnp.stack([column_sums[:, 0].reshape(-1), column_sums[:, 2].reshape(-1)]), ("ctx", "shard")
    )

    own_settings = jnp.concatenate(
        [
            grad_shift_one,
            grad_scale_one,
            grad_gate_one,
            grad_shift_two,
            grad_scale_two,
            grad_gate_two,
        ],
        1,
    )
    own_settings = sum_over(own_settings, ("ctx", "tp"))
    all_settings = lax.all_gather(own_settings, "shard", axis=0, tiled=True)
    gate_terms = lax.dot_general(
        all_settings, modulator.astype(WIDE), (((1,), (1,)), ((), ())), precision=PRECISE
    )
    gate_terms = lax.all_to_all(gate_terms, "shard", 0, 1, tiled=True)
    _, silu_back = jax.vjp(silu_gate, condition.astype(WIDE))
    grad_condition = silu_back(gate_terms)[0]
    column_count = all_settings.shape[1] // tp_size
    tp_settings = lax.dynamic_slice_in_dim(
        all_settings, lax.axis_index("tp") * column_count, column_count, 1
    )
    row_count = kept_rows // ctx_size
    tp_scaled = lax.dynamic_slice_in_dim(
        scaled_all.astype(WIDE), place + core * row_count, row_count, 1
    )
    grad_modulator = lax.dot_general(
        tp_scaled, tp_settings, (((0,), (0,)), ((), ())), precision=PRECISE
    )
    grad_modulator_bias = jnp.sum(tp_settings, 0)
    return (
        block_output[None],
        grad_latent[None],
        grad_condition,
        grad_modulator,
        grad_modulator_bias,
        grad_projector,
        projector_sums,
        grad_merger,
        token_bias[1],
        grad_expander,
        hidden_bias,
        grad_reducer,
        token_bias[0],
    )


def solution(mesh):
    in_specs = (
        P("shard", ("ctx", "tp"), None),
        P("shard", None),
        P("shard", None),
        P(),
        P("shard", None, "tp"),
        P(None, "tp"),
        P("tp", "shard"),
        P(),
        P("shard", "tp"),
        P("tp"),
        P("tp", "shard"),
        P(),
        P("shard", ("ctx", "tp"), None),
    )
    out_specs = (
        P("shard", ("ctx", "tp"), None),
        P("shard", ("ctx", "tp"), None),
        P("shard", None),
        P(("shard", "ctx"), "tp"),
        P("tp"),
        P(("shard", "ctx"), None, "tp"),
        P(None, "tp"),
        P("tp", ("shard", "ctx")),
        P(),
        P(("shard", "ctx"), "tp"),
        P("tp"),
        P("tp", ("shard", "ctx")),
        P(),
    )
    return jax.shard_map(shards, mesh=mesh, in_specs=in_specs, out_specs=out_specs, check_vma=False)
```

time: 1550 us -> 662 us (0.43)
  waiting for transfers between devices: 845 us -> 213 us
  matrix products: 367 us -> 56.6 us
  Pallas kernels: 0 us -> 107 us
  starting transfers between devices: 1.54 us -> 98.3 us
  other arithmetic: 149 us -> 55.5 us
  blocking collectives: 81.4 us -> 32 us
    reduce_scatter x10 -> x4, waiting for transfers between devices: 473 us -> 0.01 us  [reduce_weight(): lax.psum_scatter(half.reshape(shard_size * rows, grad.shape[1]), 'shard',...]
    all_gather x9 -> x2, waiting for transfers between devices: 369 us -> 0.02 us  [the longest x1 0.02 us: shards(): merger_pieces = lax.all_gather(merger_pieces, 'shard', axis=1, tiled=True)]
    dot_general x41 -> x17, matrix products: 364 us -> 56.6 us  [the longest x14 53 us: dot_wide(): lax.dot_general(left, right, (((left_dim,), (right_dim,)), ((), ())), pre...]
    ppermute x0 -> x65, waiting for transfers between devices: none -> 211 us  [the longest x15 144 us: gather_list(): lax.ppermute(block, axis, [(i, (i - r) % count) for i in range(count)])]
    pallas_call x0 -> x7, Pallas kernels: none -> 107 us  [the longest x3 68.9 us: attend_back(): pl.pallas_call(functools.partial(attend_back_kernel, key_block, query_blo...]
    ppermute x0 -> x65, starting transfers between devices: none -> 91.5 us  [the longest x24 52.5 us: scatter_list(): lax.ppermute(blocks[r], axis, [(i, (i + r) % count) for i in range(count)])]
    convert_element_type x15 -> x11, other arithmetic: 95.1 us -> 13.9 us  [the longest x4 10.7 us: reduce_weight(): half = (mine.astype(WIDE) + swap_ctx(theirs).astype(WIDE)).astype(LOW)]
    psum x2 -> x0, blocking collectives: 53.3 us -> none  [the longest x1 27.8 us: shards(): grad_settings = lax.psum(setting_terms, ('ctx', 'tp'))]
  transfers between devices with their start and end apart: 20 -> 73, of which waited for: 18 -> 30; matrix products, arithmetic and copies ran while one was open for 6% -> 21% of each run, Pallas kernels for 0% -> 16%
where the time goes in v1:
time: 662 us; the launch traced here: 654 us
  waiting for transfers between devices  213 us (32%)
  Pallas kernels  107 us (16%)
  starting transfers between devices  98.3 us (15%)
  local copies, waits for them, and re-layouts  75.6 us (11%)
  matrix products  56.6 us (9%)
  other arithmetic  55.5 us (8%)
  blocking collectives  32 us (5%)
  between operations  16 us (2%)
    ppermute x15, waiting for transfers between devices, gather_list(): lax.ppermute(block, axis, [(i, (i - r) % count) for i in range(count)])  144 us
    pallas_call x3, Pallas kernels, attend_back(): pl.pallas_call(functools.partial(attend_back_kernel, key_block, query_blo...  68.9 us
    dot_general x14, matrix products, dot_wide(): lax.dot_general(left, right, (((left_dim,), (right_dim,)), ((), ())), pre...  53 us
    ppermute x24, starting transfers between devices, scatter_list(): lax.ppermute(blocks[r], axis, [(i, (i + r) % count) for i in range(count)])  52.5 us
    ppermute x24, waiting for transfers between devices, scatter_list(): lax.ppermute(blocks[r], axis, [(i, (i + r) % count) for i in range(count)])  49.7 us
    pallas_call x4, Pallas kernels, attend(): pl.pallas_call(attend_kernel, grid=(heads,), in_specs=[pl.BlockSpec((1, s...  38.1 us
    unnamed x169, local copies, waits for them, and re-layouts  35.5 us
    ppermute x15, starting transfers between devices, gather_list(): lax.ppermute(block, axis, [(i, (i - r) % count) for i in range(count)])  27.3 us
  transfers between devices with their start and end apart: 73, of which 30 were waited for; matrix products, arithmetic and copies ran while one was open for 21% of the time, Pallas kernels for 16%

profile of v1, /device:TPU:0, one launch (start us, length us, event | category | flops | bytes accessed | tf_op | source)
XLA Modules:
  0.0 653.9 jit_solution(16957727045113931108)
XLA Ops:
  28.1 15.5 %collective-permute-done = bf16[512,768]{1,0:T(8,128)(2,1)S(1)} collective-permute-done((bf16[512,768]{1,0:T(8,128)(2,1)S(1)}, bf16[512,768]{1,0:T(8,128)(2,1)S(1)}, u32[]{:S(2)}, u32[]{:S(2)}) %collective-permute-start) | collective-permute-done | bytes 786464 | tf_op jit(solution)/shard_map/ppermute | solution.py:49
  43.6 50.5 %collective-permute-done.1 = bf16[512,768]{1,0:T(8,128)(2,1)} collective-permute-done((bf16[512,768]{1,0:T(8,128)(2,1)S(1)}, bf16[512,768]{1,0:T(8,128)(2,1)}, u32[]{:S(2)}, u32[]{:S(2)}) %collective-permute-start.1) | collective-permute-done | bytes 786464 | tf_op jit(solution)/shard_map/ppermute | solution.py:49
  97.9 8.0 %collective-permute-done.12 = bf16[192,768]{1,0:T(8,128)(2,1)S(1)} collective-permute-done((bf16[192,768]{1,0:T(8,128)(2,1)S(1)}, bf16[192,768]{1,0:T(8,128)(2,1)S(1)}, u32[]{:S(2)}, u32[]{:S(2)}) %collective-permute-start.12) | collective-permute-done | bytes 294944 | tf_op jit(solution)/shard_map/ppermute | solution.py:49
  105.9 10.9 %collective-permute-done.11 = bf16[192,768]{1,0:T(8,128)(2,1)S(1)} collective-permute-done((bf16[192,768]{1,0:T(8,128)(2,1)S(1)}, bf16[192,768]{1,0:T(8,128)(2,1)S(1)}, u32[]{:S(2)}, u32[]{:S(2)}) %collective-permute-start.11) | collective-permute-done | bytes 294944 | tf_op jit(solution)/shard_map/ppermute | solution.py:49
  118.1 8.2 %all-gather = bf16[4,1,768]{2,1,0:T(2,128)(2,1)S(1)} all-gather(bf16[1,1,768]{2,1,0:T(2,128)(2,1)S(1)} %bitcast.310), channel_id=1, replica_groups=mesh['shard'=4,'ctx'=2,'tp'=4] {'shard'}, dimensions={0}, use_global_device_ids=true | all-gather | bytes 7680 | tf_op jit(solution)/shard_map/all_gather | solution.py:293
  138.0 16.5 %all_gather.16 = bf16[576,768]{0,1:T(8,128)(2,1)} all-gather(bf16[576,192]{0,1:T(8,128)(2,1)S(1)} %copy-done.30), channel_id=1, replica_groups=mesh['shard'=4,'ctx'=2,'tp'=4] {'shard'}, dimensions={1}, use_global_device_ids=true | all-gather | bytes 1105920 | tf_op jit(solution)/shard_map/all_gather | solution.py:313
  163.9 5.6 add_convert_fusion
  181.7 7.1 %fusion.135 = (bf16[1,768,192]{2,0,1:T(2,128)(2,1)}, bf16[1,768,192]{2,0,1:T(2,128)(2,1)}, bf16[1,768,192]{2,0,1:T(2,128)(2,1)}, bf16[1,768,192]{2,0,1:T(2,128)(2,1)}) fusion(bf16[4,768,192]{2,0,1:T(4,128)(2,1)} %all-gather.5.cloned.1.call-done), kind=kLoop, calls=%fused_computation.292 | loop fusion | bytes 2359296 | tf_op jit(solution)/shard_map/slice | solution.py:348
  204.3 9.5 %shard_map.231 = (bf16[3,64,512]{2,1,0:T(8,128)(2,1)S(1)}, f32[3,1,512]{2,1,0:T(1,128)S(1)}) custom-call(bf16[3,192,2048]{2,1,0:T(8,128)(2,1)S(1)} %bitcast.245, bf16[3,192,2048]{2,1,0:T(8,128)(2,1)S(1)} %bitcast.246, bf16[3,192,2048]{2,1,0:T(8,128)(2,1)S(1)} %bitcast.247, bf16[3,128,2048]{2,1,0:T(8,128)(2,1)S(1)} %copy-done.9, ...), custom_call_target="tpu_custom_call" | custom-call | flops 6442450944 | bytes 3538944 | tf_op jit(solution)/shard_map/pallas_call | solution.py:120
  214.0 9.5 %shard_map.230 = (bf16[3,64,512]{2,1,0:T(8,128)(2,1)S(1)}, f32[3,1,512]{2,1,0:T(1,128)S(1)}) custom-call(bf16[3,192,2048]{2,1,0:T(8,128)(2,1)S(1)} %bitcast.248, bf16[3,192,2048]{2,1,0:T(8,128)(2,1)S(1)} %bitcast.249, bf16[3,192,2048]{2,1,0:T(8,128)(2,1)S(1)} %bitcast.250, bf16[3,128,2048]{2,1,0:T(8,128)(2,1)S(1)} %copy-done.9, ...), custom_call_target="tpu_custom_call" | custom-call | flops 6442450944 | bytes 3538944 | tf_op jit(solution)/shard_map/pallas_call | solution.py:120
  227.1 9.5 %shard_map.229 = (bf16[3,64,512]{2,1,0:T(8,128)(2,1)S(1)}, f32[3,1,512]{2,1,0:T(1,128)S(1)}) custom-call(bf16[3,192,2048]{2,1,0:T(8,128)(2,1)S(1)} %bitcast.251, bf16[3,192,2048]{2,1,0:T(8,128)(2,1)S(1)} %bitcast.252, bf16[3,192,2048]{2,1,0:T(8,128)(2,1)S(1)} %bitcast.253, bf16[3,128,2048]{2,1,0:T(8,128)(2,1)S(1)} %copy-done.9, ...), custom_call_target="tpu_custom_call" | custom-call | flops 6442450944 | bytes 3538944 | tf_op jit(solution)/shard_map/pallas_call | solution.py:120
  236.9 9.5 %shard_map.228 = (bf16[3,64,512]{2,1,0:T(8,128)(2,1)S(1)}, f32[3,1,512]{2,1,0:T(1,128)S(1)}) custom-call(bf16[3,192,2048]{2,1,0:T(8,128)(2,1)S(1)} %bitcast.254, bf16[3,192,2048]{2,1,0:T(8,128)(2,1)S(1)} %bitcast.255, bf16[3,192,2048]{2,1,0:T(8,128)(2,1)S(1)} %bitcast.256, bf16[3,128,2048]{2,1,0:T(8,128)(2,1)S(1)} %copy-done.9, ...), custom_call_target="tpu_custom_call" | custom-call | flops 6442450944 | bytes 3538944 | tf_op jit(solution)/shard_map/pallas_call | solution.py:120
  258.5 15.2 %collective-permute-done.26 = bf16[576,768]{1,0:T(8,128)(2,1)S(1)} collective-permute-done((bf16[576,768]{1,0:T(8,128)(2,1)}, bf16[576,768]{1,0:T(8,128)(2,1)S(1)}, u32[]{:S(2)}, u32[]{:S(2)}) %collective-permute-start.26) | collective-permute-done | bytes 884768 | tf_op jit(solution)/shard_map/ppermute | solution.py:49
  273.8 36.9 %collective-permute-done.25 = bf16[576,768]{1,0:T(8,128)(2,1)S(1)} collective-permute-done((bf16[576,768]{1,0:T(8,128)(2,1)}, bf16[576,768]{1,0:T(8,128)(2,1)S(1)}, u32[]{:S(2)}, u32[]{:S(2)}) %collective-permute-start.25) | collective-permute-done | bytes 884768 | tf_op jit(solution)/shard_map/ppermute | solution.py:49
  312.9 6.6 %broadcast_select_fusion = (bf16[4,768,768]{2,1,0:T(8,128)(2,1)S(1)}, bf16[4,768,768]{2,1,0:T(8,128)(2,1)}) fusion(bf16[4,768,768]{2,1,0:T(8,128)(2,1)} %collective-permute-done.13, bf16[4,768,768]{2,1,0:T(8,128)(2,1)} %all-gather.7.cloned.1.call-done, pred[]{:T(512)S(6)} %eq.4), kind=kLoop, calls=%fused_computation.21 | loop fusion | flops 4718592 | bytes 18874368 | tf_op jit(solution)/shard_map/jit(_where)/select_n | solution.py:339
  327.0 5.2 fusion.127
  332.2 8.0 %convert_reduce_fusion = (f32[3072]{0:T(1024)S(1)}, bf16[512,3072]{1,0:T(8,128)(2,1)S(1)}) fusion(bf16[768,3072]{1,0:T(8,128)(2,1)S(1)} %get-tuple-element.120, bf16[1,512,768]{2,1,0:T(8,128)(2,1)S(1)} %copy-done.21, f32[768]{0:T(1024)S(1)} %get-tuple-element.93, f32[512,3072]{1,0:T(8,128)S(1)} %fusion.126, f32[3072]{0:T(1024)S(1)} %maximum_convert_fusion), kind=kOutput, calls=%fused_computation.10 | convolution fusion | flops 2459563008 | bytes 14969856 | tf_op jit(solution)/shard_map/dot_general | solution.py:41
  350.7 19.5 %collective-permute-start.19 = (bf16[192,512]{1,0:T(8,128)(2,1)S(1)}, bf16[192,512]{1,0:T(8,128)(2,1)S(1)}, u32[]{:S(2)}, u32[]{:S(2)}) collective-permute-start(bf16[192,512]{1,0:T(8,128)(2,1)S(1)} %get-tuple-element.157), channel_id=1, source_target_pairs={{0,1},{1,2},{2,3},{3,0},{4,5},{5,6},{6,7},{7,4},{8,9},{9,10},{10,1... | collective-permute-start | bytes 589832 | tf_op jit(solution)/shard_map/ppermute | solution.py:57
  388.3 23.1 %shard_map.232 = (bf16[1,192,2048]{2,1,0:T(8,128)(2,1)S(1)}, bf16[1,128,2048]{2,1,0:T(8,128)(2,1)}) custom-call(bf16[3,192,2048]{2,1,0:T(8,128)(2,1)} %bitcast.242, bf16[3,128,2048]{2,1,0:T(8,128)(2,1)S(1)} %copy-done.10, bf16[3,64,2048]{2,1,0:T(8,128)(2,1)S(1)} %bitcast.257, bf16[3,64,2048]{2,1,0:T(8,128)(2,1)S(1)} %constant_dynamic-update-slice_fusion.out_ref, ...), custom_call_target="tpu_custom_call" | custom-call | flops 21474836480 | bytes 3145728 | tf_op jit(solution)/shard_map/pallas_call | solution.py:220
  412.6 22.9 %shard_map.233 = (bf16[1,192,2048]{2,1,0:T(8,128)(2,1)S(1)}, bf16[1,128,2048]{2,1,0:T(8,128)(2,1)}) custom-call(bf16[3,192,2048]{2,1,0:T(8,128)(2,1)} %bitcast.243, bf16[3,128,2048]{2,1,0:T(8,128)(2,1)S(1)} %copy-done.10, bf16[3,64,2048]{2,1,0:T(8,128)(2,1)S(1)} %bitcast.258, bf16[3,64,2048]{2,1,0:T(8,128)(2,1)S(1)} %copy-done.6, ...), custom_call_target="tpu_custom_call" | custom-call | flops 21474836480 | bytes 3145728 | tf_op jit(solution)/shard_map/pallas_call | solution.py:220
  436.1 22.9 %shard_map.234 = (bf16[1,192,2048]{2,1,0:T(8,128)(2,1)S(1)}, bf16[1,128,2048]{2,1,0:T(8,128)(2,1)}) custom-call(bf16[3,192,2048]{2,1,0:T(8,128)(2,1)} %bitcast.244, bf16[3,128,2048]{2,1,0:T(8,128)(2,1)S(1)} %copy-done.10, bf16[3,64,2048]{2,1,0:T(8,128)(2,1)S(1)} %bitcast.259, bf16[3,64,2048]{2,1,0:T(8,128)(2,1)S(1)} %copy-done.7, ...), custom_call_target="tpu_custom_call" | custom-call | flops 21474836480 | bytes 3145728 | tf_op jit(solution)/shard_map/pallas_call | solution.py:220
  470.0 5.5 convolution_convert_fusion.3
  479.4 8.4 %convolution_convert_fusion = bf16[768,3072]{1,0:T(8,128)(2,1)} fusion(bf16[1,512,768]{2,1,0:T(8,128)(2,1)} %param.25, f32[768]{0:T(1024)S(1)} %get-tuple-element.93, f32[512,3072]{1,0:T(8,128)} %copy-done.67, f32[3072]{0:T(1024)S(1)} %maximum_convert_fusion), kind=kOutput, calls=%fused_computation.13 | convolution fusion | flops 2435186688 | bytes 11811840 | tf_op jit(solution)/shard_map/dot_general | solution.py:41
  494.7 4.8 fusion.7
  515.4 6.6 %collective-permute-done.22 = bf16[192,512]{1,0:T(8,128)(2,1)} collective-permute-done((bf16[192,512]{1,0:T(8,128)(2,1)}, bf16[192,512]{1,0:T(8,128)(2,1)}, u32[]{:S(2)}, u32[]{:S(2)}) %collective-permute-start.22) | collective-permute-done | bytes 196640 | tf_op jit(solution)/shard_map/ppermute | solution.py:57
  522.0 6.1 collective-permute-done.21
  530.1 6.3 collective-permute-start.34
  538.0 8.3 %collective-permute-done.28 = bf16[192,512]{1,0:T(8,128)(2,1)S(1)} collective-permute-done((bf16[192,512]{1,0:T(8,128)(2,1)S(1)}, bf16[192,512]{1,0:T(8,128)(2,1)S(1)}, u32[]{:S(2)}, u32[]{:S(2)}) %collective-permute-start.28) | collective-permute-done | bytes 196640 | tf_op jit(solution)/shard_map/ppermute | solution.py:57
  547.9 7.0 %collective-permute-done.33 = bf16[192,512]{1,0:T(8,128)(2,1)S(1)} collective-permute-done((bf16[192,512]{1,0:T(8,128)(2,1)S(1)}, bf16[192,512]{1,0:T(8,128)(2,1)S(1)}, u32[]{:S(2)}, u32[]{:S(2)}) %collective-permute-start.33) | collective-permute-done | bytes 196640 | tf_op jit(solution)/shard_map/ppermute | solution.py:57
  567.4 5.3 convert_reduce_fusion.7
  594.4 7.3 %all-gather.1 = f32[4,1,4608]{2,1,0:T(1,128)S(1)} all-gather(f32[1,1,4608]{2,1,0:T(1,128)S(1)} %add_bitcast_fusion.3), channel_id=1, replica_groups=mesh['shard'=4,'ctx'=2,'tp'=4] {'shard'}, dimensions={0}, use_global_device_ids=true | all-gather | bytes 92160 | tf_op jit(solution)/shard_map/all_gather | solution.py:454
  634.1 5.6 collective-permute-done.53
  (441 shorter events, 246.1 us)
Async XLA Ops:
  7.2 174.5 %all-gather.5.cloned.1.call-start = ((), (), s32[]{:S(2)}) async-start(), calls=%async_computation.6 | async-start | bytes 1966080 | tf_op jit(solution)/shard_map/all_gather | solution.py:347
  21.9 178.2 %all-gather.7.cloned.1.call-start = ((), (), s32[]{:S(2)}) async-start(), calls=%async_computation.7 | async-start | bytes 5898240 | tf_op jit(solution)/shard_map/all_gather | solution.py:337
  21.9 21.7 %collective-permute-start = (bf16[512,768]{1,0:T(8,128)(2,1)S(1)}, bf16[512,768]{1,0:T(8,128)(2,1)S(1)}, u32[]{:S(2)}, u32[]{:S(2)}) collective-permute-start(bf16[512,768]{1,0:T(8,128)(2,1)S(1)} %bitcast.265), channel_id=1, source_target_pairs={{0,3},{1,0},{2,1},{3,2},{4,7},{5,4},{6,5},{7,6},{8,11},{9,8},{10,9... | collective-permute-start | bytes 2359304 | tf_op jit(solution)/shard_map/ppermute | solution.py:49
  25.6 68.5 %collective-permute-start.1 = (bf16[512,768]{1,0:T(8,128)(2,1)S(1)}, bf16[512,768]{1,0:T(8,128)(2,1)}, u32[]{:S(2)}, u32[]{:S(2)}) collective-permute-start(bf16[512,768]{1,0:T(8,128)(2,1)S(1)} %bitcast.266), channel_id=1, source_target_pairs={{0,2},{1,3},{2,0},{3,1},{4,6},{5,7},{6,4},{7,5},{8,10},{9,11},{10,... | collective-permute-start | bytes 2359304 | tf_op jit(solution)/shard_map/ppermute | solution.py:49
  26.0 68.1 %collective-permute-start.2 = (bf16[512,768]{1,0:T(8,128)(2,1)S(1)}, bf16[512,768]{1,0:T(8,128)(2,1)}, u32[]{:S(2)}, u32[]{:S(2)}) collective-permute-start(bf16[512,768]{1,0:T(8,128)(2,1)S(1)} %bitcast.267), channel_id=1, source_target_pairs={{0,1},{1,2},{2,3},{3,0},{4,5},{5,6},{6,7},{7,4},{8,9},{9,10},{10,1... | collective-permute-start | bytes 2359304 | tf_op jit(solution)/shard_map/ppermute | solution.py:49
  94.1 22.7 %collective-permute-start.11 = (bf16[192,768]{1,0:T(8,128)(2,1)S(1)}, bf16[192,768]{1,0:T(8,128)(2,1)S(1)}, u32[]{:S(2)}, u32[]{:S(2)}) collective-permute-start(bf16[192,768]{1,0:T(8,128)(2,1)S(1)} %pad_maximum_fusion.9), channel_id=1, source_target_pairs={{0,2},{1,3},{2,0},{3,1},{4,6},{5,7},{6,4},{7,5},{8,10},{9,11},{10,... | collective-permute-start | bytes 884744 | tf_op jit(solution)/shard_map/ppermute | solution.py:49
  94.9 22.0 %collective-permute-start.10 = (bf16[192,768]{1,0:T(8,128)(2,1)S(1)}, bf16[192,768]{1,0:T(8,128)(2,1)S(1)}, u32[]{:S(2)}, u32[]{:S(2)}) collective-permute-start(bf16[192,768]{1,0:T(8,128)(2,1)S(1)} %pad_maximum_fusion.9), channel_id=1, source_target_pairs={{0,3},{1,0},{2,1},{3,2},{4,7},{5,4},{6,5},{7,6},{8,11},{9,8},{10,9... | collective-permute-start | bytes 884744 | tf_op jit(solution)/shard_map/ppermute | solution.py:49
  128.0 26.7 %all-to-all-start = ((f32[4,1,4608]{2,1,0:T(1,128)}), f32[4,1,4608]{2,1,0:T(1,128)S(1)}, u32[]{:S(2)}, u32[]{:S(2)}) async-start(f32[4,1,4608]{2,1,0:T(1,128)} %copy.55), calls=%async_computation | async-start | bytes 147456 | tf_op jit(solution)/shard_map/all_to_all | solution.py:301
  131.3 480.5 %reduce-scatter.7.cloned.1.call-start = ((), (), s32[]{:S(2)}) async-start(), calls=%async_computation.9 | async-start | bytes 737280 | tf_op jit(solution)/shard_map/reduce_scatter | solution.py:256
  172.3 27.8 %collective-permute-start.3 = (bf16[3,128,2048]{2,1,0:T(8,128)(2,1)}, bf16[3,128,2048]{2,1,0:T(8,128)(2,1)S(1)}, u32[]{:S(2)}, u32[]{:S(2)}) collective-permute-start(bf16[3,128,2048]{2,1,0:T(8,128)(2,1)} %slice.303), channel_id=1, source_target_pairs={{0,4},{4,0},{1,5},{5,1},{2,6},{6,2},{3,7},{7,3},{8,12},{12,8},{9,1... | collective-permute-start | bytes 4718600 | tf_op jit(solution)/shard_map/ppermute | solution.py:68
  200.1 112.8 %collective-permute-start.13 = (bf16[4,768,768]{2,1,0:T(8,128)(2,1)}, bf16[4,768,768]{2,1,0:T(8,128)(2,1)}, u32[]{:S(2)}, u32[]{:S(2)}) collective-permute-start(bf16[4,768,768]{2,1,0:T(8,128)(2,1)} %all-gather.7.cloned.1.call-done), channel_id=1, source_target_pairs={{0,4},{4,0},{1,5},{5,1},{2,6},{6,2},{3,7},{7,3},{8,12},{12,8},{9,1... | collective-permute-start | bytes 14155784 | tf_op jit(solution)/shard_map/ppermute | solution.py:68
  213.9 37.0 %collective-permute-start.6 = (bf16[192,512]{1,0:T(8,128)(2,1)S(1)}, bf16[192,512]{1,0:T(8,128)(2,1)}, u32[]{:S(2)}, u32[]{:S(2)}) collective-permute-start(bf16[192,512]{1,0:T(8,128)(2,1)S(1)} %bitcast.264), channel_id=1, source_target_pairs={{0,1},{1,2},{2,3},{3,0},{4,5},{5,6},{6,7},{7,4},{8,9},{9,10},{10,1... | collective-permute-start | bytes 589832 | tf_op jit(solution)/shard_map/ppermute | solution.py:57
  223.5 27.7 %collective-permute-start.5 = (bf16[192,512]{1,0:T(8,128)(2,1)S(1)}, bf16[192,512]{1,0:T(8,128)(2,1)}, u32[]{:S(2)}, u32[]{:S(2)}) collective-permute-start(bf16[192,512]{1,0:T(8,128)(2,1)S(1)} %bitcast.263), channel_id=1, source_target_pairs={{0,2},{1,3},{2,0},{3,1},{4,6},{5,7},{6,4},{7,5},{8,10},{9,11},{10,... | collective-permute-start | bytes 589832 | tf_op jit(solution)/shard_map/ppermute | solution.py:57
  236.7 17.6 %collective-permute-start.4 = (bf16[192,512]{1,0:T(8,128)(2,1)S(1)}, bf16[192,512]{1,0:T(8,128)(2,1)}, u32[]{:S(2)}, u32[]{:S(2)}) collective-permute-start(bf16[192,512]{1,0:T(8,128)(2,1)S(1)} %bitcast.262), channel_id=1, source_target_pairs={{0,3},{1,0},{2,1},{3,2},{4,7},{5,4},{6,5},{7,6},{8,11},{9,8},{10,9... | collective-permute-start | bytes 589832 | tf_op jit(solution)/shard_map/ppermute | solution.py:57
  249.1 24.7 %collective-permute-start.26 = (bf16[576,768]{1,0:T(8,128)(2,1)}, bf16[576,768]{1,0:T(8,128)(2,1)S(1)}, u32[]{:S(2)}, u32[]{:S(2)}) collective-permute-start(bf16[576,768]{1,0:T(8,128)(2,1)} %copy.69), channel_id=1, source_target_pairs={{0,1},{1,2},{2,3},{3,0},{4,5},{5,6},{6,7},{7,4},{8,9},{9,10},{10,1... | collective-permute-start | bytes 2654216 | tf_op jit(solution)/shard_map/ppermute | solution.py:49
  250.9 59.7 %collective-permute-start.25 = (bf16[576,768]{1,0:T(8,128)(2,1)}, bf16[576,768]{1,0:T(8,128)(2,1)S(1)}, u32[]{:S(2)}, u32[]{:S(2)}) collective-permute-start(bf16[576,768]{1,0:T(8,128)(2,1)} %copy.69), channel_id=1, source_target_pairs={{0,2},{1,3},{2,0},{3,1},{4,6},{5,7},{6,4},{7,5},{8,10},{9,11},{10,... | collective-permute-start | bytes 2654216 | tf_op jit(solution)/shard_map/ppermute | solution.py:49
  251.2 59.5 %collective-permute-start.24 = (bf16[576,768]{1,0:T(8,128)(2,1)}, bf16[576,768]{1,0:T(8,128)(2,1)S(1)}, u32[]{:S(2)}, u32[]{:S(2)}) collective-permute-start(bf16[576,768]{1,0:T(8,128)(2,1)} %copy.69), channel_id=1, source_target_pairs={{0,3},{1,0},{2,1},{3,2},{4,7},{5,4},{6,5},{7,6},{8,11},{9,8},{10,9... | collective-permute-start | bytes 2654216 | tf_op jit(solution)/shard_map/ppermute | solution.py:49
  350.7 33.0 %collective-permute-start.19 = (bf16[192,512]{1,0:T(8,128)(2,1)S(1)}, bf16[192,512]{1,0:T(8,128)(2,1)S(1)}, u32[]{:S(2)}, u32[]{:S(2)}) collective-permute-start(bf16[192,512]{1,0:T(8,128)(2,1)S(1)} %get-tuple-element.157), channel_id=1, source_target_pairs={{0,1},{1,2},{2,3},{3,0},{4,5},{5,6},{6,7},{7,4},{8,9},{9,10},{10,1... | collective-permute-start | bytes 589832 | tf_op jit(solution)/shard_map/ppermute | solution.py:57
  383.2 77.4 %collective-permute-start.42 = (bf16[4,96,768]{2,1,0:T(8,128)(2,1)S(1)}, bf16[4,96,768]{2,1,0:T(8,128)(2,1)S(1)}, u32[]{:S(2)}, u32[]{:S(2)}) collective-permute-start(bf16[4,96,768]{2,1,0:T(8,128)(2,1)S(1)} %dynamic-slice_bitcast_fusion.2), channel_id=1, source_target_pairs={{0,4},{4,0},{1,5},{5,1},{2,6},{6,2},{3,7},{7,3},{8,12},{12,8},{9,1... | collective-permute-start | bytes 1769480 | tf_op jit(solution)/shard_map/ppermute | solution.py:68
  383.2 111.5 %collective-permute-start.51 = (bf16[4,96,3072]{2,1,0:T(8,128)(2,1)}, bf16[4,96,3072]{2,1,0:T(8,128)(2,1)}, u32[]{:S(2)}, u32[]{:S(2)}) collective-permute-start(bf16[4,96,3072]{2,1,0:T(8,128)(2,1)} %dynamic-slice_bitcast_fusion.1), channel_id=1, source_target_pairs={{0,4},{4,0},{1,5},{5,1},{2,6},{6,2},{3,7},{7,3},{8,12},{12,8},{9,1... | collective-permute-start | bytes 7077896 | tf_op jit(solution)/shard_map/ppermute | solution.py:68
  383.8 104.0 %collective-permute-start.58 = (f32[1,768]{1,0:T(1,128)S(1)}, f32[1,768]{1,0:T(1,128)S(1)}, u32[]{:S(2)}, u32[]{:S(2)}) collective-permute-start(f32[1,768]{1,0:T(1,128)S(1)} %add_add_fusion.3), channel_id=1, source_target_pairs={{0,4},{4,0},{1,5},{5,1},{2,6},{6,2},{3,7},{7,3},{8,12},{12,8},{9,1... | collective-permute-start | bytes 9224 | tf_op jit(solution)/shard_map/ppermute | solution.py:75
  411.4 50.3 %collective-permute-start.20 = (bf16[128,2048]{1,0:T(8,128)(2,1)}, bf16[128,2048]{1,0:T(8,128)(2,1)}, u32[]{:S(2)}, u32[]{:S(2)}) collective-permute-start(bf16[128,2048]{1,0:T(8,128)(2,1)} %bitcast.50), channel_id=1, source_target_pairs={{0,4},{4,0},{1,5},{5,1},{2,6},{6,2},{3,7},{7,3},{8,12},{12,8},{9,1... | collective-permute-start | bytes 1572872 | tf_op jit(solution)/shard_map/ppermute | solution.py:68
  435.5 29.1 %collective-permute-start.27 = (bf16[128,2048]{1,0:T(8,128)(2,1)}, bf16[128,2048]{1,0:T(8,128)(2,1)}, u32[]{:S(2)}, u32[]{:S(2)}) collective-permute-start(bf16[128,2048]{1,0:T(8,128)(2,1)} %bitcast.55), channel_id=1, source_target_pairs={{0,4},{4,0},{1,5},{5,1},{2,6},{6,2},{3,7},{7,3},{8,12},{12,8},{9,1... | collective-permute-start | bytes 1572872 | tf_op jit(solution)/shard_map/ppermute | solution.py:68
  461.6 159.4 %reduce-scatter.5.cloned.1.call-start = ((), (), s32[]{:S(2)}) async-start(), calls=%async_computation.8 | async-start | bytes 614400 | tf_op jit(solution)/shard_map/reduce_scatter | solution.py:256
  489.2 133.8 %reduce-scatter.9.cloned.1.call-start = ((), (), s32[]{:S(2)}) async-start(), calls=%async_computation.10 | async-start | bytes 2949120 | tf_op jit(solution)/shard_map/reduce_scatter | solution.py:256
  492.5 69.7 %collective-permute-start.61 = (bf16[4,96,3072]{2,1,0:T(8,128)(2,1)}, bf16[4,96,3072]{2,1,0:T(8,128)(2,1)}, u32[]{:S(2)}, u32[]{:S(2)}) collective-permute-start(bf16[4,96,3072]{2,1,0:T(8,128)(2,1)} %dynamic-slice_bitcast_fusion), channel_id=1, source_target_pairs={{0,4},{4,0},{1,5},{5,1},{2,6},{6,2},{3,7},{7,3},{8,12},{12,8},{9,1... | collective-permute-start | bytes 7077896 | tf_op jit(solution)/shard_map/ppermute | solution.py:68
  493.1 92.9 %collective-permute-start.60 = (f32[1,768]{1,0:T(1,128)}, f32[1,768]{1,0:T(1,128)}, u32[]{:S(2)}, u32[]{:S(2)}) collective-permute-start(f32[1,768]{1,0:T(1,128)} %add.372), channel_id=1, source_target_pairs={{0,16},{8,24},{16,0},{24,8},{1,17},{9,25},{17,1},{25,9},{2,18},{10... | collective-permute-start | bytes 9224 | tf_op jit(solution)/shard_map/ppermute | solution.py:75
  499.5 128.9 %reduce-scatter.11.cloned.1.call-start = ((), (), s32[]{:S(2)}) async-start(), calls=%async_computation.11 | async-start | bytes 2949120 | tf_op jit(solution)/shard_map/reduce_scatter | solution.py:256
  528.1 18.2 %collective-permute-start.28 = (bf16[192,512]{1,0:T(8,128)(2,1)S(1)}, bf16[192,512]{1,0:T(8,128)(2,1)S(1)}, u32[]{:S(2)}, u32[]{:S(2)}) collective-permute-start(bf16[192,512]{1,0:T(8,128)(2,1)S(1)} %get-tuple-element.149), channel_id=1, source_target_pairs={{0,3},{1,0},{2,1},{3,2},{4,7},{5,4},{6,5},{7,6},{8,11},{9,8},{10,9... | collective-permute-start | bytes 589832 | tf_op jit(solution)/shard_map/ppermute | solution.py:57
  530.1 17.4 %collective-permute-start.34 = (bf16[192,512]{1,0:T(8,128)(2,1)S(1)}, bf16[192,512]{1,0:T(8,128)(2,1)S(1)}, u32[]{:S(2)}, u32[]{:S(2)}) collective-permute-start(bf16[192,512]{1,0:T(8,128)(2,1)S(1)} %get-tuple-element.146), channel_id=1, source_target_pairs={{0,1},{1,2},{2,3},{3,0},{4,5},{5,6},{6,7},{7,4},{8,9},{9,10},{10,1... | collective-permute-start | bytes 589832 | tf_op jit(solution)/shard_map/ppermute | solution.py:57
  538.0 16.9 %collective-permute-start.33 = (bf16[192,512]{1,0:T(8,128)(2,1)S(1)}, bf16[192,512]{1,0:T(8,128)(2,1)S(1)}, u32[]{:S(2)}, u32[]{:S(2)}) collective-permute-start(bf16[192,512]{1,0:T(8,128)(2,1)S(1)} %get-tuple-element.147), channel_id=1, source_target_pairs={{0,2},{1,3},{2,0},{3,1},{4,6},{5,7},{6,4},{7,5},{8,10},{9,11},{10,... | collective-permute-start | bytes 589832 | tf_op jit(solution)/shard_map/ppermute | solution.py:57
  547.5 34.9 %collective-permute-start.40 = (f32[2,192]{1,0:T(2,128)}, f32[2,192]{1,0:T(2,128)S(1)}, u32[]{:S(2)}, u32[]{:S(2)}) collective-permute-start(f32[2,192]{1,0:T(2,128)} %fusion.123), channel_id=1, source_target_pairs={{0,8},{8,0},{16,24},{24,16},{1,9},{9,1},{17,25},{25,17},{2,10},{10... | collective-permute-start | bytes 4616 | tf_op jit(solution)/shard_map/ppermute | solution.py:75
  (111 other events, 1259.6 us)
Sparse Core Ops, SparseCore 0:
  22.0 32.2 all-gather.4
  118.2 64.0 all-gather.6
  461.8 24.3 reduce-scatter.6
  489.3 24.4 reduce-scatter.4
  516.7 37.3 reduce-scatter.8
  566.4 35.1 reduce-scatter.10

commit v2 on v1

v2 whole, which is shorter than its diff:
```python
import functools
import math

import jax
import jax.numpy as jnp
from jax import lax
from jax.experimental import pallas as pl
from jax.experimental.pallas import tpu as pltpu
from jax.sharding import PartitionSpec as P

HEAD_DIM = 64
PRECISE = lax.Precision.HIGHEST
LOW = jnp.bfloat16
WIDE = jnp.float32


def layer_norm(values):
    row_mean = jnp.mean(values, -1, keepdims=True)
    centered = values - row_mean
    variance = jnp.mean(centered * centered, -1, keepdims=True)
    return centered * lax.rsqrt(variance + 1e-06)


def gelu_tanh(values):
    return (
        0.5
        * values
        * (1.0 + jnp.tanh(0.7978845608028654 * (values + 0.044715 * values * values * values)))
    )


def silu_gate(values):
    return values * jax.nn.sigmoid(values)


def modulate(values, scale_part, shift_part):
    return layer_norm(values) * (1.0 + scale_part) + shift_part


def dot_wide(left, right, left_dim, right_dim):
    return lax.dot_general(
        left, right, (((left_dim,), (right_dim,)), ((), ())), preferred_element_type=WIDE
    )


def gather_list(block, axis):
    count = lax.axis_size(axis)
    return [block] + [
        lax.ppermute(block, axis, [(i, (i - r) % count) for i in range(count)])
        for r in range(1, count)
    ]


def scatter_list(blocks, axis):
    count = lax.axis_size(axis)
    arrived = {
        (count - r) % count: lax.ppermute(
            blocks[r], axis, [(i, (i + r) % count) for i in range(count)]
        )
        for r in range(1, count)
    }
    arrived[0] = blocks[0]
    return [arrived[r] for r in range(count)]


def swap_ctx(block):
    count = lax.axis_size("ctx")
    return lax.ppermute(block, "ctx", [(i, (i + 1) % count) for i in range(count)])


def sum_over(value, axes):
    for axis in axes:
        step = 1
        while step < lax.axis_size(axis):
            value = value + lax.ppermute(
                value, axis, [(i, i ^ step) for i in range(lax.axis_size(axis))]
            )
            step *= 2
    return value


def rotated(rows, start):
    return lax.dynamic_slice_in_dim(jnp.concatenate([rows, rows], 0), start, rows.shape[0], 0)


def mirror(block, r):
    return lax.ppermute(block, "shard", [(i, i ^ r) for i in range(lax.axis_size("shard"))])


def mirror_gather(block):
    return [block] + [mirror(block, r) for r in range(1, lax.axis_size("shard"))]


def mirror_exchange(blocks):
    return [blocks[0]] + [mirror(block, r) for r, block in enumerate(blocks) if r > 0]


def in_shard_order(blocks):
    own, bit = lax.axis_index("shard"), 1
    while bit < len(blocks):
        flip = (own & bit) != 0
        blocks = [jnp.where(flip, blocks[j ^ bit], blocks[j]) for j in range(len(blocks))]
        bit *= 2
    return blocks


def tree_sum(blocks):
    while len(blocks) > 1:
        blocks = [blocks[i] + blocks[i + 1] for i in range(0, len(blocks), 2)]
    return blocks[0]


def ordered_call(kernel, operands, in_specs, out_specs, out_shape, before=(), through=(), **rest):
    count, through_count, results = len(operands), len(through), len(out_specs)
    extra = through_count + len(before)
    unread = pl.BlockSpec(memory_space=pl.ANY)

    def body(*refs):
        after_inputs = refs[count + extra :]
        kernel(*refs[:count], *after_inputs[:results], *after_inputs[results + through_count :])

    made = pl.pallas_call(
        body,
        in_specs=list(in_specs) + [unread] * extra,
        out_specs=list(out_specs) + [unread] * through_count,
        out_shape=list(out_shape) + [jax.ShapeDtypeStruct(x.shape, x.dtype) for x in through],
        input_output_aliases={count + i: results + i for i in range(through_count)},
        **rest,
    )(*operands, *through, *before)
    return made[:results], made[results:]


def tie(values, *before):
    return ordered_call(
        lambda *refs: None,
        (),
        (),
        (),
        (),
        before,
        values,
        cost_estimate=pl.CostEstimate(flops=1, bytes_accessed=1, transcendentals=0),
    )[1]


def attend_kernel(query_ref, key_ref, value_ref, far_key_ref, far_value_ref, out_ref, stat_ref, key_rows):
    near = key_ref.shape[2]
    key_rows[:near, :] = key_ref[0].T
    key_rows[near:, :] = far_key_ref[0].T
    queries = query_ref[0] * jnp.array(HEAD_DIM ** (-0.5), LOW)
    columns = queries.shape[1]
    top = total = mixed = None
    for half, values in enumerate((value_ref, far_value_ref)):
        scores = jnp.dot(
            key_rows[half * near : (half + 1) * near, :], queries, preferred_element_type=WIDE
        )
        block_top = jnp.max(scores, 0, keepdims=True)
        new_top = block_top if top is None else jnp.maximum(top, block_top)
        exponent = jnp.exp(scores - new_top)
        block_total = jnp.sum(exponent, 0, keepdims=True)
        block_mixed = jnp.dot(values[0], exponent.astype(LOW), preferred_element_type=WIDE)
        if top is None:
            total, mixed = block_total, block_mixed
        else:
            fade = jnp.exp(top - new_top)
            total = total * fade + block_total
            mixed = mixed * fade + block_mixed
        top = new_top
    out_ref[0] = (mixed / total).astype(LOW)
    stat_ref[0] = top + jnp.log(total)


def attend(near_rows, far_rows, place, width, before=(), through=()):
    heads, _, tokens = near_rows.shape
    size = HEAD_DIM

    def whole(row):
        return pl.BlockSpec((1, size, tokens), lambda h: (h, row, 0))

    return ordered_call(
        attend_kernel,
        (near_rows, near_rows, near_rows, far_rows, far_rows),
        grid=(heads,),
        in_specs=[
            pl.BlockSpec((1, size, width), lambda h: (h, 0, place)),
            whole(1),
            whole(2),
            whole(0),
            whole(1),
        ],
        out_specs=[
            pl.BlockSpec((1, size, width), lambda h: (h, 0, 0)),
            pl.BlockSpec((1, 1, width), lambda h: (h, 0, 0)),
        ],
        out_shape=[
            jax.ShapeDtypeStruct((heads, size, width), LOW),
            jax.ShapeDtypeStruct((heads, 1, width), WIDE),
        ],
        scratch_shapes=[pltpu.VMEM((2 * tokens, size), LOW)],
        compiler_params=pltpu.CompilerParams(vmem_limit_bytes=48 * 2**20),
        cost_estimate=pl.CostEstimate(
            flops=heads * 2 * tokens * width * size * 4 * 4,
            bytes_accessed=heads * size * (width * 4 + tokens * 8),
            transcendentals=heads * 2 * tokens * width,
        ),
        before=before,
        through=through,
    )


def with_parts(rows, extra):
    high = extra.astype(LOW)
    rest = extra - high.astype(WIDE)
    middle = rest.astype(LOW)
    lowest = (rest - middle.astype(WIDE)).astype(LOW)
    fill = jnp.zeros((HEAD_DIM - 3, rows.shape[1]), LOW)
    return jnp.concatenate([rows, high, middle, lowest, fill], 0)


def attend_back_kernel(
    key_block, query_block, first,
    query_ref, key_ref, value_ref, grad_ref, out_ref, stat_ref, sum_ref,
    grad_query_ref, grad_pair_ref,
    key_rows, value_rows, query_rows, grad_rows, query_more, grad_more, query_sum,
):
    size = HEAD_DIM
    tokens = query_ref.shape[2]
    keys_held = key_ref.shape[2]
    queries = query_ref[0] * jnp.array(size ** (-0.5), LOW)
    grads = grad_ref[0]
    ones = jnp.where(lax.broadcasted_iota(jnp.int32, (keys_held, size), 1) < 3, 1.0, 0.0).astype(LOW)
    key_rows[:, :size] = key_ref[0].T
    key_rows[:, size:] = ones
    value_rows[:, :size] = value_ref[0].T
    value_rows[:, size:] = ones
    query_rows[...] = queries.T
    grad_rows[...] = grads.T
    inner = jnp.sum(grads.astype(WIDE) * out_ref[0].astype(WIDE), 0, keepdims=True)
    query_more[...] = with_parts(queries, -stat_ref[0])
    grad_more[...] = with_parts(grads, -inner)
    query_sum[...] = jnp.zeros_like(query_sum) if first else sum_ref[0]

    def step(index, carry):
        place = pl.ds(pl.multiple_of(index * key_block, key_block), key_block)
        keys, values, columns = key_rows[place, :], value_rows[place, :], key_ref[0, :, place]
        key_sum = jnp.zeros((key_block, size), WIDE)
        value_sum = jnp.zeros((key_block, size), WIDE)
        for part in range(tokens // query_block):
            span = slice(part * query_block, (part + 1) * query_block)
            probs = jnp.exp(jnp.dot(keys, query_more[:, span], preferred_element_type=WIDE))
            centered = jnp.dot(values, grad_more[:, span], preferred_element_type=WIDE)
            grad_scores = (probs * centered).astype(LOW)
            value_sum += jnp.dot(probs.astype(LOW), grad_rows[span, :], preferred_element_type=WIDE)
            key_sum += jnp.dot(grad_scores, query_rows[span, :], preferred_element_type=WIDE)
            query_sum[:, span] += jnp.dot(columns, grad_scores, preferred_element_type=WIDE)
        grad_pair_ref[0, :size, place] = key_sum.T.astype(LOW)
        grad_pair_ref[0, size:, place] = value_sum.T.astype(LOW)
        return carry

    lax.fori_loop(0, keys_held // key_block, step, 0)
    if first:
        grad_query_ref[0] = query_sum[...]
    else:
        grad_query_ref[0] = (query_sum[...] * size ** (-0.5)).astype(LOW)


def attend_back(head, near_rows, pair_rows, key_place, grads, outs, stats, query_sum, before=(), through=()):
    tokens = near_rows.shape[2]
    size = HEAD_DIM
    key_block, query_block = math.gcd(tokens, 1024), math.gcd(tokens, 512)
    first = query_sum is None
    if first:
        query_sum = jnp.zeros((1, 8, 128), WIDE)

    def rows(count, place=0):
        return pl.BlockSpec((1, count, tokens), lambda i: (head, place, 0))

    def result(count):
        return pl.BlockSpec((1, count, tokens), lambda i: (0, 0, 0))

    return ordered_call(
        functools.partial(attend_back_kernel, key_block, query_block, first),
        (near_rows, pair_rows, pair_rows, grads, outs, stats, query_sum),
        grid=(1,),
        in_specs=[
            rows(size),
            rows(size, key_place),
            rows(size, key_place + 1),
            rows(size),
            rows(size),
            rows(1),
            pl.BlockSpec(query_sum.shape, lambda i: (0, 0, 0)),
        ],
        out_specs=[result(size), result(2 * size)],
        out_shape=[
            jax.ShapeDtypeStruct((1, size, tokens), WIDE if first else LOW),
            jax.ShapeDtypeStruct((1, 2 * size, tokens), LOW),
        ],
        scratch_shapes=[
            pltpu.VMEM((tokens, 2 * size), LOW),
            pltpu.VMEM((tokens, 2 * size), LOW),
            pltpu.VMEM((tokens, size), LOW),
            pltpu.VMEM((tokens, size), LOW),
            pltpu.VMEM((2 * size, tokens), LOW),
            pltpu.VMEM((2 * size, tokens), LOW),
            pltpu.VMEM((size, tokens), WIDE),
        ],
        compiler_params=pltpu.CompilerParams(vmem_limit_bytes=48 * 2**20),
        cost_estimate=pl.CostEstimate(
            flops=tokens * tokens * size * 10 * 4,
            bytes_accessed=size * tokens * 2 * 9,
            transcendentals=tokens * tokens,
        ),
        before=before,
        through=through,
    )


def weight_kernel(
    normed_ref, hidden_ref, far_hidden_ref, feed_ref, active_ref, far_active_ref, branch_ref, heads_ref,
    expander_ref, far_expander_ref, reducer_ref, far_reducer_ref, merger_ref,
    normed_columns, feed_columns, branch_columns,
):
    @pl.when(pl.program_id(0) == 0)
    def _():
        normed_columns[...] = normed_ref[...].T
        feed_columns[...] = feed_ref[...].T
        branch_columns[...] = branch_ref[...].T

    def product(left, right):
        return jnp.dot(left, right, preferred_element_type=WIDE).astype(LOW)

    expander_ref[...] = product(normed_columns[...], hidden_ref[...])
    far_expander_ref[...] = product(normed_columns[...], far_hidden_ref[...])
    reducer_ref[...] = product(feed_columns[...], active_ref[...])
    far_reducer_ref[...] = product(feed_columns[...], far_active_ref[...])
    count = merger_ref.shape[0]
    place = pl.ds(pl.multiple_of(pl.program_id(0) * count, count), count)
    merger_ref[...] = dot_wide(branch_columns[place, :], heads_ref[...], 1, 1).astype(LOW)


def weight_terms(normed, grad_hidden, grad_feed, activated, grad_branch, attended, steps, before):
    tokens, width = normed.shape
    share = grad_hidden[0].shape[1]

    def whole(array):
        return pl.BlockSpec(array.shape, lambda i: (0, 0))

    units = pl.BlockSpec((tokens, share // steps), lambda i: (0, i))
    made = pl.BlockSpec((width, share // steps), lambda i: (0, i))
    operands = (normed, *grad_hidden, grad_feed, *activated, grad_branch, attended)
    return ordered_call(
        weight_kernel,
        operands,
        grid=(steps,),
        in_specs=[whole(normed), units, units, whole(grad_feed), units, units]
        + [whole(grad_branch), whole(attended)],
        out_specs=[made] * 4 + [pl.BlockSpec((width // steps, attended.shape[0]), lambda i: (i, 0))],
        out_shape=[jax.ShapeDtypeStruct((width, share), LOW)] * 4
        + [jax.ShapeDtypeStruct((width, attended.shape[0]), LOW)],
        scratch_shapes=[pltpu.VMEM((width, tokens), LOW)] * 3,
        compiler_params=pltpu.CompilerParams(vmem_limit_bytes=48 * 2**20),
        cost_estimate=pl.CostEstimate(
            flops=2 * tokens * width * (4 * share + width), bytes_accessed=2**25, transcendentals=0
        ),
        before=before,
    )[0]


def core_half(grad):
    ctx_size, shard_size = lax.axis_size("ctx"), lax.axis_size("shard")
    rows = grad.shape[0] // (shard_size * ctx_size)
    low = grad.astype(LOW).reshape(shard_size, ctx_size, rows, grad.shape[1])
    core = lax.axis_index("ctx")
    mine = lax.dynamic_index_in_dim(low, core, 1, keepdims=False)
    theirs = lax.dynamic_index_in_dim(low, 1 - core, 1, keepdims=False)
    return (
        mine.reshape(shard_size * rows, grad.shape[1]),
        theirs.reshape(shard_size * rows, grad.shape[1]),
    )


def sum_low(left, right):
    return (left.astype(WIDE) + right.astype(WIDE)).astype(LOW)


def shards(
    latent,
    condition,
    modulator,
    modulator_bias,
    projector,
    projector_bias,
    merger,
    merger_bias,
    expander,
    expander_bias,
    reducer,
    reducer_bias,
    cotangent,
):
    tp_size, ctx_size, shard_size = (lax.axis_size(axis) for axis in ("tp", "ctx", "shard"))
    core = lax.axis_index("ctx")
    own_latent, own_cotangent = latent[0], cotangent[0]
    block, model_width = own_latent.shape
    local_width = projector.shape[2]
    heads = local_width // HEAD_DIM
    head_columns = 3 * HEAD_DIM
    local_hidden = expander.shape[1]
    half_hidden = local_hidden // ctx_size
    kept_rows = projector.shape[0]
    place = lax.axis_index("shard") * kept_rows

    conditions = jnp.concatenate(mirror_gather(condition.astype(WIDE)), 0)
    def half_units(weight, axis):
        return lax.dynamic_slice_in_dim(weight, core * half_hidden, half_hidden, axis)

    share = tp_size * half_hidden
    latent_blocks = gather_list(own_latent, "tp")
    own_reducer = lax.all_gather(
        jnp.concatenate(gather_list(half_units(reducer, 0).T, "tp"), 1), "shard", axis=0, tiled=True
    )

    scaled_all = silu_gate(conditions).astype(LOW)
    terms = jnp.dot(
        lax.dynamic_slice_in_dim(scaled_all, place, kept_rows, 1),
        modulator,
        preferred_element_type=WIDE,
    )
    terms = mirror_exchange([terms[r : r + 1] for r in range(shard_size)])
    modulation = tree_sum(terms) + modulator_bias.astype(WIDE)

    own_projector = (
        projector.reshape(kept_rows, 3, heads, HEAD_DIM)
        .transpose(0, 2, 1, 3)
        .reshape(kept_rows, 3 * local_width)
    )
    head_projector = jnp.concatenate(in_shard_order(mirror_gather(own_projector)), 0)
    zero_bias = jnp.zeros((1, local_width), projector_bias.dtype)
    qkv_bias = (
        jnp.concatenate([projector_bias[:1], zero_bias, projector_bias[1:]], 0)
        .reshape(3, heads, HEAD_DIM)
        .transpose(1, 0, 2)
        .reshape(3 * local_width, 1)
        .astype(WIDE)
    )
    settings = [
        modulation[:, index * model_width : (index + 1) * model_width] for index in range(6)
    ]
    shift_one, scale_one, gate_one, shift_two, scale_two, gate_two = settings

    latent_blocks = [latent_blocks[0], *tie(latent_blocks[1:], head_projector, modulation)]
    normed_rows = jnp.concatenate(
        [modulate(rows.astype(WIDE), scale_one, shift_one).astype(LOW) for rows in latent_blocks], 0
    )
    tokens = normed_rows.shape[0]
    projected = (dot_wide(head_projector, normed_rows, 0, 1) + qkv_bias).astype(LOW)
    near_rows = projected.reshape(heads, head_columns, tokens)
    far_rows = swap_ctx(near_rows[:, HEAD_DIM:, :])

    bias_rows = jnp.zeros((16, half_hidden + local_width), expander_bias.dtype)
    for index, part in enumerate((core, 1 - core)):
        half_bias = lax.dynamic_slice_in_dim(expander_bias, part * half_hidden, half_hidden, 0)
        bias_rows = bias_rows.at[index, :half_hidden].set(half_bias)
    pieces = jnp.concatenate([half_units(expander, 1), merger.T], 1)
    pieces = jnp.concatenate([pieces, bias_rows], 0)
    pieces = gather_list(tie([pieces], *latent_blocks[1:])[0], "tp")
    pieces = tie(pieces, near_rows)
    own_expander = lax.all_gather(
        jnp.concatenate([piece[:kept_rows, :half_hidden] for piece in pieces], 1),
        "shard",
        axis=0,
        tiled=True,
    )
    full_merger = lax.all_gather(
        jnp.concatenate([piece[:kept_rows, half_hidden:] for piece in pieces], 1),
        "shard",
        axis=0,
        tiled=True,
    )
    part_biases = [
        jnp.concatenate(
            [piece[kept_rows + index : kept_rows + index + 1, :half_hidden] for piece in pieces], 1
        )
        for index in range(2)
    ]
    outs, stats, sent = [None] * tp_size, [None] * tp_size, [None] * tp_size
    order = sorted(range(tp_size), key=lambda r: -min(r, tp_size - r))
    previous = ()
    for r in order:
        (outs[r], stats[r]), _ = attend(near_rows, far_rows, r, block, previous)
        sent[r] = outs[r].reshape(local_width, block)
        previous = (outs[r],)
    attended = jnp.concatenate(scatter_list(sent, "tp"), 0)
    all_outs, all_stats = jnp.concatenate(outs, 2), jnp.concatenate(stats, 2)

    own_expander, full_merger = tie([own_expander, full_merger], outs[order[-1]])
    expanders = [own_expander, swap_ctx(own_expander)]
    reducers = [own_reducer, swap_ctx(own_reducer)]
    core_width = model_width // ctx_size
    tail_projector = lax.dynamic_slice_in_dim(head_projector, core * core_width, core_width, 0).T
    projectors = lax.all_gather(
        tie([tail_projector], outs[order[-1]])[0], "tp", axis=0, tiled=True
    )
    latent_wide = own_latent.astype(WIDE)
    branch = dot_wide(attended, full_merger, 0, 1) + merger_bias.astype(WIDE)
    middle = latent_wide + gate_one * branch
    normed_two_wide, norm_back_two = jax.vjp(modulate, middle, scale_two, shift_two)
    normed_two = normed_two_wide.astype(LOW)
    grad_output = own_cotangent.astype(WIDE)
    grad_feed = (gate_two * grad_output).astype(LOW)
    feed, grad_normed_two = reducer_bias.astype(WIDE), 0.0
    activated, grad_hidden = [], []
    for full_expander, full_reducer, part_bias in zip(expanders, reducers, part_biases):
        hidden = dot_wide(normed_two, full_expander, 1, 0) + part_bias.astype(WIDE)
        active, gelu_back = jax.vjp(gelu_tanh, hidden)
        activated.append(active.astype(LOW))
        feed = feed + dot_wide(activated[-1], full_reducer, 1, 1)
        grad_hidden.append(gelu_back(dot_wide(grad_feed, full_reducer, 1, 0))[0].astype(LOW))
        grad_normed_two = grad_normed_two + dot_wide(grad_hidden[-1], full_expander, 1, 1)
    block_output = (middle + gate_two * feed).astype(LOW)
    grad_gate_two = jnp.sum(grad_output * feed, 0, keepdims=True)
    grad_middle_norm, grad_scale_two, grad_shift_two = norm_back_two(grad_normed_two)
    grad_middle = grad_output + grad_middle_norm
    grad_gate_one = jnp.sum(grad_middle * branch, 0, keepdims=True)
    grad_branch = (gate_one * grad_middle).astype(LOW)
    grad_attended = dot_wide(full_merger, grad_branch, 0, 1).astype(LOW)
    grad_blocks = scatter_list(
        [grad_attended[r * local_width : (r + 1) * local_width] for r in range(tp_size)], "tp"
    )

    weight_parts = weight_terms(
        normed_two, grad_hidden, grad_feed, activated, grad_branch, attended, tp_size, (grad_attended,)
    )
    grad_blocks = tie(grad_blocks, *weight_parts)
    all_grads = jnp.concatenate(grad_blocks, 1).reshape(heads, HEAD_DIM, tokens)

    def in_order(left, right, axis):
        return jnp.where(
            core == 0, jnp.concatenate([left, right], axis), jnp.concatenate([right, left], axis)
        )

    tp_turn = lax.rem(tp_size - lax.axis_index("tp"), tp_size)
    hidden_sums = in_order(
        *(jnp.sum(part, 0, dtype=WIDE).reshape(tp_size, half_hidden) for part in grad_hidden), 1
    )
    early_sums = jnp.concatenate(
        [
            grad_gate_one,
            grad_shift_two,
            grad_scale_two,
            grad_gate_two,
            jnp.sum(grad_feed, 0, keepdims=True, dtype=WIDE),
            jnp.sum(grad_branch, 0, keepdims=True, dtype=WIDE),
            rotated(hidden_sums, tp_turn),
        ],
        0,
    )

    def projector_half(rows):
        own, other = core_half(dot_wide(normed_rows, jnp.concatenate(rows, 0), 0, 1))
        return sum_low(own, swap_ctx(other))

    head_rows, arrived_rows = [], []
    for head in range(heads):
        before = ()
        if head == 1:
            before = (head_rows[0],)
        elif head == 2:
            before = (head_rows[1], *arrived_rows[0])
        (partial, far), _ = attend_back(
            head, near_rows, far_rows, 0, all_grads, all_outs, all_stats, None, before
        )
        before = ()
        if head == 0:
            came = tie([swap_ctx(weight_parts[i]) for i in (1, 3, 4)], partial)
            weight_halves = [sum_low(weight_parts[2 * i], came[i]) for i in range(3)]
            weight_sums = [
                lax.psum_scatter(half, "shard", scatter_dimension=0, tiled=True)
                for half in weight_halves
            ]
            before = tuple(weight_halves)
        elif head == 1:
            projectors = tie([projectors], partial)[0]
            other_projectors = swap_ctx(projectors)
        elif head == 2:
            early_projector = projector_half(head_rows)
            before = (other_projectors, *arrived_rows[1], early_projector)
        far_came = swap_ctx(far[0])
        (grad_query, near), _ = attend_back(
            head, near_rows, near_rows, 1, all_grads, all_outs, all_stats, partial, before
        )
        rows = jnp.concatenate([grad_query[0], sum_low(near[0], far_came)], 0)
        head_rows.append(rows)
        arrived_rows.append(
            scatter_list([rows[:, r * block : (r + 1) * block] for r in range(tp_size)], "tp")
        )
    rows = jnp.zeros((tp_size * heads * head_columns, block), LOW)
    for head, arrived in enumerate(arrived_rows):
        for r, part in enumerate(arrived):
            turn = lax.rem(lax.axis_index("tp") + r, tp_size)
            rows = lax.dynamic_update_slice_in_dim(
                rows, part, (turn * heads + head) * head_columns, 0
            )
    grad_normed = in_order(
        *(dot_wide(rows, part, 0, 0) for part in (projectors, other_projectors)), 1
    )
    _, norm_back = jax.vjp(modulate, latent_wide, scale_one, shift_one)
    grad_latent_norm, grad_scale_one, grad_shift_one = norm_back(grad_normed)
    grad_latent = grad_middle + grad_latent_norm

    def from_peers(columns):
        width = columns.shape[1] // tp_size
        parts = scatter_list([columns[:, r * width : (r + 1) * width] for r in range(tp_size)], "tp")
        return sum(part.astype(WIDE) for part in parts)

    row_count = kept_rows // ctx_size
    summed = from_peers(
        tie(
            [
                jnp.concatenate(
                    [
                        part[:, r * (part.shape[1] // tp_size) : (r + 1) * (part.shape[1] // tp_size)]
                        for r in range(tp_size)
                        for part in weight_sums
                    ],
                    1,
                )
            ],
            *arrived_rows[-1],
        )[0]
    )
    two = summed[:, : 2 * half_hidden]
    own_two = lax.dynamic_slice_in_dim(two, core * row_count, row_count, 0)
    other_two = swap_ctx(lax.dynamic_slice_in_dim(two, (1 - core) * row_count, row_count, 0))
    grad_expander = in_order(own_two[:, :half_hidden], other_two[:, :half_hidden], 1)
    grad_reducer = in_order(own_two[:, half_hidden:], other_two[:, half_hidden:], 1).T
    grad_merger = lax.dynamic_slice_in_dim(summed[:, 2 * half_hidden :], core * row_count, row_count, 0).T

    column_sums = jnp.sum(jnp.concatenate(head_rows, 0), 1, dtype=WIDE).reshape(heads, 3, HEAD_DIM)
    bias_sums = jnp.stack([column_sums[:, 0].reshape(-1), column_sums[:, 2].reshape(-1)])
    bias_sums = lax.dynamic_update_slice_in_dim(
        jnp.zeros((2, model_width), WIDE), bias_sums, lax.axis_index("tp") * local_width, 1
    )
    sums = jnp.concatenate([grad_shift_one, grad_scale_one, early_sums, bias_sums], 0)
    sums = tie([sums], summed)[0]
    all_sums = mirror_gather(sum_over(sums, ("ctx", "tp")))
    total = tree_sum(all_sums)

    projector_sums = [
        lax.psum_scatter(half, "shard", scatter_dimension=0, tiled=True)
        for half in (early_projector, projector_half(head_rows[-1:]))
    ]
    grad_projector = jnp.concatenate(tie(projector_sums, *all_sums[1:]), 1)
    grad_projector = (
        grad_projector.astype(WIDE)
        .reshape(-1, heads, 3, HEAD_DIM)
        .transpose(0, 2, 1, 3)
        .reshape(-1, 3, local_width)
    )

    hidden_bias = lax.dynamic_index_in_dim(total[8:-2], lax.axis_index("tp"), 0, keepdims=False)
    projector_bias_sums = lax.dynamic_slice_in_dim(
        total[-2:], lax.axis_index("tp") * local_width, local_width, 1
    )
    total_settings = total[:6].reshape(-1)
    all_settings = jnp.concatenate([part[:6] for part in all_sums], 0).reshape(shard_size, -1)
    gate_terms = lax.dot_general(
        all_settings, modulator.astype(WIDE), (((1,), (1,)), ((), ())), precision=PRECISE
    )
    gate_terms = in_shard_order(mirror_exchange([gate_terms[r : r + 1] for r in range(shard_size)]))
    _, silu_back = jax.vjp(silu_gate, condition.astype(WIDE))
    grad_condition = silu_back(jnp.concatenate(gate_terms, 1))[0]
    column_count = all_settings.shape[1] // tp_size
    tp_settings = lax.dynamic_slice_in_dim(
        all_settings, lax.axis_index("tp") * column_count, column_count, 1
    )
    tp_scaled = lax.dynamic_slice_in_dim(
        scaled_all.astype(WIDE), place + core * row_count, row_count, 1
    )
    grad_modulator = lax.dot_general(
        tp_scaled, tp_settings, (((0,), (0,)), ((), ())), precision=PRECISE
    )
    grad_modulator_bias = lax.dynamic_slice_in_dim(
        total_settings, lax.axis_index("tp") * column_count, column_count, 0
    )
    return (
        block_output[None],
        grad_latent[None],
        grad_condition,
        grad_modulator,
        grad_modulator_bias,
        grad_projector,
        projector_bias_sums,
        grad_merger,
        total[7],
        grad_expander,
        hidden_bias,
        grad_reducer,
        total[6],
    )


def solution(mesh):
    in_specs = (
        P("shard", ("ctx", "tp"), None),
        P("shard", None),
        P("shard", None),
        P(),
        P("shard", None, "tp"),
        P(None, "tp"),
        P("tp", "shard"),
        P(),
        P("shard", "tp"),
        P("tp"),
        P("tp", "shard"),
        P(),
        P("shard", ("ctx", "tp"), None),
    )
    out_specs = (
        P("shard", ("ctx", "tp"), None),
        P("shard", ("ctx", "tp"), None),
        P("shard", None),
        P(("shard", "ctx"), "tp"),
        P("tp"),
        P(("shard", "ctx"), None, "tp"),
        P(None, "tp"),
        P("tp", ("shard", "ctx")),
        P(),
        P(("shard", "ctx"), "tp"),
        P("tp"),
        P("tp", ("shard", "ctx")),
        P(),
    )
    return jax.shard_map(shards, mesh=mesh, in_specs=in_specs, out_specs=out_specs, check_vma=False)
```

time: 662 us -> 552 us (0.83)
  waiting for transfers between devices: 213 us -> 105 us
  blocking collectives: 32 us -> 0 us
  Pallas kernels: 107 us -> 128 us
  starting transfers between devices: 98.3 us -> 82.6 us
  local copies, waits for them, and re-layouts: 75.6 us -> 88.3 us
    ppermute x15 -> x9, waiting for transfers between devices: 144 us -> 50.3 us  [gather_list(): lax.ppermute(block, axis, [(i, (i - r) % count) for i in range(count)])]
    all_gather x3 -> x0, blocking collectives: 32 us -> none  [the longest x1 16.5 us: shards(): head_projector = lax.all_gather(own_projector, 'shard', axis=1, tiled=True)]
    ppermute x24 -> x18, starting transfers between devices: 52.5 us -> 22.9 us  [scatter_list(): lax.ppermute(blocks[r], axis, [(i, (i + r) % count) for i in range(count)])]
    pallas_call x7 -> x22, Pallas kernels: 107 us -> 128 us  [ordered_call(): pl.pallas_call(body, in_specs=list(in_specs) + [unread] * extra, out_spec...]
    ppermute x3 -> x15, starting transfers between devices: 4.22 us -> 20.2 us  [mirror(): lax.ppermute(block, 'shard', [(i, i ^ r) for i in range(lax.axis_size('sh...]
    ppermute x24 -> x18, waiting for transfers between devices: 49.7 us -> 38.6 us  [scatter_list(): lax.ppermute(blocks[r], axis, [(i, (i + r) % count) for i in range(count)])]
    dynamic_update_slice x0 -> x10, local copies, waits for them, and re-layouts: none -> 10.4 us  [the longest x9 9.05 us: shards(): lax.dynamic_update_slice_in_dim(rows, part, (turn * heads + head) * head_...]
    ppermute x14 -> x3, waiting for transfers between devices: 16.7 us -> 6.79 us  [sum_over(): lax.ppermute(value, axis, [(i, i ^ step) for i in range(lax.axis_size(axi...]
  transfers between devices with their start and end apart: 73 -> 67, of which waited for: 30 -> 17; matrix products, arithmetic and copies ran while one was open for 21% -> 33% of each run, Pallas kernels for 16% -> 24%
where the time goes in v2:
time: 552 us; the launch traced here: 542 us
  Pallas kernels  128 us (23%)
  waiting for transfers between devices  105 us (19%)
  local copies, waits for them, and re-layouts  88.3 us (16%)
  starting transfers between devices  82.6 us (15%)
  matrix products  62.5 us (11%)
  other arithmetic  58.8 us (11%)
  between operations  16 us (3%)
    pallas_call x22, Pallas kernels, ordered_call(): pl.pallas_call(body, in_specs=list(in_specs) + [unread] * extra, out_spec...  128 us
    dot_general x15, matrix products, dot_wide(): lax.dot_general(left, right, (((left_dim,), (right_dim,)), ((), ())), pre...  58.8 us
    ppermute x9, waiting for transfers between devices, gather_list(): lax.ppermute(block, axis, [(i, (i - r) % count) for i in range(count)])  50.3 us
    ppermute x18, waiting for transfers between devices, scatter_list(): lax.ppermute(blocks[r], axis, [(i, (i + r) % count) for i in range(count)])  38.6 us
    unnamed x271, local copies, waits for them, and re-layouts  33 us
    ppermute x9, starting transfers between devices, gather_list(): lax.ppermute(block, axis, [(i, (i - r) % count) for i in range(count)])  27.9 us
    ppermute x18, starting transfers between devices, scatter_list(): lax.ppermute(blocks[r], axis, [(i, (i + r) % count) for i in range(count)])  22.9 us
    ppermute x15, starting transfers between devices, mirror(): lax.ppermute(block, 'shard', [(i, i ^ r) for i in range(lax.axis_size('sh...  20.2 us
  transfers between devices with their start and end apart: 67, of which 17 were waited for; matrix products, arithmetic and copies ran while one was open for 33% of the time, Pallas kernels for 24%

profile of v2, /device:TPU:0, one launch (start us, length us, event | category | flops | bytes accessed | tf_op | source)
XLA Modules:
  0.0 541.9 jit_solution(2984418003848659202)
XLA Ops:
  8.1 3.9 collective-permute-start.2
  31.8 3.5 collective-permute-start.19
  39.0 43.3 %collective-permute-done.19 = bf16[192,384]{1,0:T(8,128)(2,1)S(1)} collective-permute-done((bf16[192,384]{1,0:T(8,128)(2,1)S(1)}, bf16[192,384]{1,0:T(8,128)(2,1)S(1)}, u32[]{:S(2)}, u32[]{:S(2)}) %collective-permute-start.19) | collective-permute-done | bytes 147488 | tf_op jit(solution)/shard_map/ppermute | solution.py:49
  100.9 15.4 %collective-permute-start.17 = (bf16[208,576]{1,0:T(8,128)(2,1)}, bf16[208,576]{1,0:T(8,128)(2,1)}, u32[]{:S(2)}, u32[]{:S(2)}) collective-permute-start(bf16[208,576]{1,0:T(8,128)(2,1)} %shard_map.233.refs_0_), channel_id=1, source_target_pairs={{0,2},{1,3},{2,0},{3,1},{4,6},{5,7},{6,4},{7,5},{8,10},{9,11},{10,... | collective-permute-start | bytes 718856 | tf_op jit(solution)/shard_map/ppermute | solution.py:49
  124.3 6.6 %add_convert_fusion.2 = bf16[576,2048]{1,0:T(8,128)(2,1)} fusion(bf16[768,576]{0,1:T(8,128)(2,1)S(1)} %copy-done.57, f32[576]{0:T(1024)S(1)} %reshape.369, bf16[512,768]{1,0:T(8,128)(2,1)S(1)} %get-tuple-element.257, bf16[512,768]{1,0:T(8,128)(2,1)S(1)} %get-tuple-element.256, bf16[512,768]{1,0:T(8,128)(2,1)S(1)} %get-tuple-element.255, ...), kind=kOutput, calls=%fused_computation.7 | convolution fusion | flops 1826881536 | bytes 6392064 | tf_op jit(solution)/shard_map/dot_general | solution.py:41
  130.9 4.1 collective-permute-done.17.refs_2_
  154.4 10.6 %shard_map.229 = (bf16[3,64,512]{2,1,0:T(8,128)(2,1)S(1)}, f32[3,1,512]{2,1,0:T(1,128)S(1)}) custom-call(bf16[3,192,2048]{2,1,0:T(8,128)(2,1)S(1)} %bitcast.132, bf16[3,192,2048]{2,1,0:T(8,128)(2,1)S(1)} %bitcast.133, bf16[3,192,2048]{2,1,0:T(8,128)(2,1)S(1)} %bitcast.134, bf16[3,128,2048]{2,1,0:T(8,128)(2,1)} %collective-permute-done.12.refs_3_.refs_4_.refs_1_.refs_2_, ...), custom_call_target="tpu_custom_call" | custom-call | flops 6442450944 | bytes 3538944 | tf_op jit(solution)/shard_map/pallas_call | solution.py:122
  165.0 10.6 %shard_map.230 = (bf16[3,64,512]{2,1,0:T(8,128)(2,1)S(1)}, f32[3,1,512]{2,1,0:T(1,128)S(1)}) custom-call(bf16[3,192,2048]{2,1,0:T(8,128)(2,1)S(1)} %bitcast.135, bf16[3,192,2048]{2,1,0:T(8,128)(2,1)S(1)} %bitcast.136, bf16[3,192,2048]{2,1,0:T(8,128)(2,1)S(1)} %bitcast.137, bf16[3,128,2048]{2,1,0:T(8,128)(2,1)} %collective-permute-done.12.refs_3_.refs_4_.refs_1_.refs_2_, ...), custom_call_target="tpu_custom_call" | custom-call | flops 6442450944 | bytes 3538944 | tf_op jit(solution)/shard_map/pallas_call | solution.py:122
  176.5 10.6 %shard_map.231 = (bf16[3,64,512]{2,1,0:T(8,128)(2,1)S(1)}, f32[3,1,512]{2,1,0:T(1,128)S(1)}) custom-call(bf16[3,192,2048]{2,1,0:T(8,128)(2,1)S(1)} %bitcast.138, bf16[3,192,2048]{2,1,0:T(8,128)(2,1)S(1)} %bitcast.139, bf16[3,192,2048]{2,1,0:T(8,128)(2,1)S(1)} %bitcast.140, bf16[3,128,2048]{2,1,0:T(8,128)(2,1)} %collective-permute-done.12.refs_3_.refs_4_.refs_1_.refs_2_, ...), custom_call_target="tpu_custom_call" | custom-call | flops 6442450944 | bytes 3538944 | tf_op jit(solution)/shard_map/pallas_call | solution.py:122
  187.2 3.7 collective-permute-start.13
  190.8 10.6 %shard_map.232 = (bf16[3,64,512]{2,1,0:T(8,128)(2,1)S(1)}, f32[3,1,512]{2,1,0:T(1,128)S(1)}) custom-call(bf16[3,192,2048]{2,1,0:T(8,128)(2,1)S(1)} %bitcast.142, bf16[3,192,2048]{2,1,0:T(8,128)(2,1)S(1)} %bitcast.141, bf16[3,192,2048]{2,1,0:T(8,128)(2,1)S(1)} %bitcast.143, bf16[3,128,2048]{2,1,0:T(8,128)(2,1)} %collective-permute-done.12.refs_3_.refs_4_.refs_1_.refs_2_, ...), custom_call_target="tpu_custom_call" | custom-call | flops 6442450944 | bytes 3538944 | tf_op jit(solution)/shard_map/pallas_call | solution.py:122
  208.4 3.7 fusion.102
  216.0 13.7 %convert_reduce_fusion.2 = (f32[1536]{0:T(1024)}, bf16[512,1536]{1,0:T(8,128)(2,1)S(1)}, bf16[512,1536]{1,0:T(8,128)(2,1)}) fusion(f32[512,1536]{1,0:T(8,128)S(1)} %convolution_add_fusion.1, bf16[512,768]{1,0:T(8,128)(2,1)S(1)} %get-tuple-element.188.refs_3_, bf16[768,1536]{1,0:T(8,128)(2,1)S(1)} %copy-done.124), kind=kOutput, calls=%fused_computation.28 | convolution fusion | flops 1229978112 | bytes 9443328 | tf_op jit(solution)/shard_map/dot_general | solution.py:41
  231.1 6.9 %convert_reduce_fusion.1 = (f32[1536]{0:T(1024)}, bf16[512,1536]{1,0:T(8,128)(2,1)S(1)}, bf16[512,1536]{1,0:T(8,128)(2,1)}) fusion(f32[512,1536]{1,0:T(8,128)S(1)} %convolution_add_fusion, bf16[512,768]{1,0:T(8,128)(2,1)S(1)} %get-tuple-element.188.refs_3_, bf16[768,1536]{1,0:T(8,128)(2,1)} %collective-permute-done.23), kind=kOutput, calls=%fused_computation.27 | convolution fusion | flops 1229978112 | bytes 9443328 | tf_op jit(solution)/shard_map/dot_general | solution.py:41
  245.6 11.0 %shard_map.236 = (bf16[768,1536]{1,0:T(8,128)(2,1)}, bf16[768,1536]{1,0:T(8,128)(2,1)}, bf16[768,1536]{1,0:T(8,128)(2,1)}, bf16[768,1536]{1,0:T(8,128)(2,1)}, bf16[768,768]{1,0:T(8,128)(2,1)S(1)}) custom-call(bf16[512,768]{1,0:T(8,128)(2,1)S(1)} %add_convert_fusion.5.refs_0_, bf16[512,1536]{1,0:T(8,128)(2,1)} %copy-done.125, bf16[512,1536]{1,0:T(8,128)(2,1)} %copy-done.127, ...), custom_call_target="tpu_custom_call" | custom-call | flops 5435817984 | bytes 33554432 | tf_op jit(solution)/shard_map/pallas_call | solution.py:122
  266.8 12.1 %collective-permute-done.25.refs_2_ = bf16[192,512]{1,0:T(8,128)(2,1)S(1)} collective-permute-done((bf16[192,512]{1,0:T(8,128)(2,1)S(1)}, bf16[192,512]{1,0:T(8,128)(2,1)S(1)}, u32[]{:S(2)}, u32[]{:S(2)}) %collective-permute-start.25) | collective-permute-done | bytes 196640 | tf_op jit(solution)/shard_map/ppermute | solution.py:57
  281.1 13.2 %shard_map.238 = (f32[1,64,2048]{2,1,0:T(8,128)S(1)}, bf16[1,128,2048]{2,1,0:T(8,128)(2,1)}) custom-call(bf16[3,192,2048]{2,1,0:T(8,128)(2,1)} %bitcast.123, bf16[3,128,2048]{2,1,0:T(8,128)(2,1)} %collective-permute-done.12.refs_3_.refs_4_.refs_1_.refs_2_, bf16[3,128,2048]{2,1,0:T(8,128)(2,1)} %collective-permute-done.12.refs_3_.refs_4_.refs_1_.refs_2_, ...), custom_call_target="tpu_custom_call" | custom-call | flops 10737418240 | bytes 2359296 | tf_op jit(solution)/shard_map/pallas_call | solution.py:122
  299.1 4.4 add_convert_fusion.1.refs_7_
  305.1 4.3 fusion.114
  311.3 4.6 add_convert_fusion.refs_8_
  319.2 12.5 %shard_map.240 = (bf16[1,64,2048]{2,1,0:T(8,128)(2,1)S(1)}, bf16[1,128,2048]{2,1,0:T(8,128)(2,1)S(1)}) custom-call(bf16[3,192,2048]{2,1,0:T(8,128)(2,1)} %bitcast.124, bf16[3,192,2048]{2,1,0:T(8,128)(2,1)} %bitcast.125, bf16[3,192,2048]{2,1,0:T(8,128)(2,1)} %bitcast.126, bf16[3,64,2048]{2,1,0:T(8,128)(2,1)S(1)} %bitcast.158, ...), custom_call_target="tpu_custom_call" | custom-call | flops 10737418240 | bytes 2359296 | tf_op jit(solution)/shard_map/pallas_call | solution.py:122
  334.7 12.8 %shard_map.241 = (f32[1,64,2048]{2,1,0:T(8,128)S(1)}, bf16[1,128,2048]{2,1,0:T(8,128)(2,1)}) custom-call(bf16[3,192,2048]{2,1,0:T(8,128)(2,1)} %bitcast.127, bf16[3,128,2048]{2,1,0:T(8,128)(2,1)} %collective-permute-done.12.refs_3_.refs_4_.refs_1_.refs_2_, bf16[3,128,2048]{2,1,0:T(8,128)(2,1)} %collective-permute-done.12.refs_3_.refs_4_.refs_1_.refs_2_, ...), custom_call_target="tpu_custom_call" | custom-call | flops 10737418240 | bytes 2359296 | tf_op jit(solution)/shard_map/pallas_call | solution.py:122
  358.5 11.1 %shard_map.242 = (bf16[1,64,2048]{2,1,0:T(8,128)(2,1)S(1)}, bf16[1,128,2048]{2,1,0:T(8,128)(2,1)S(1)}) custom-call(bf16[3,192,2048]{2,1,0:T(8,128)(2,1)S(1)} %bitcast.144, bf16[3,192,2048]{2,1,0:T(8,128)(2,1)S(1)} %bitcast.145, bf16[3,192,2048]{2,1,0:T(8,128)(2,1)S(1)} %bitcast.146, bf16[3,64,2048]{2,1,0:T(8,128)(2,1)S(1)} %bitcast.160, ...), custom_call_target="tpu_custom_call" | custom-call | flops 10737418240 | bytes 2359296 | tf_op jit(solution)/shard_map/pallas_call | solution.py:122
  381.5 12.8 %shard_map.243 = (f32[1,64,2048]{2,1,0:T(8,128)S(1)}, bf16[1,128,2048]{2,1,0:T(8,128)(2,1)}) custom-call(bf16[3,192,2048]{2,1,0:T(8,128)(2,1)} %bitcast.128, bf16[3,128,2048]{2,1,0:T(8,128)(2,1)} %collective-permute-done.12.refs_3_.refs_4_.refs_1_.refs_2_, bf16[3,128,2048]{2,1,0:T(8,128)(2,1)} %collective-permute-done.12.refs_3_.refs_4_.refs_1_.refs_2_, ...), custom_call_target="tpu_custom_call" | custom-call | flops 10737418240 | bytes 2359296 | tf_op jit(solution)/shard_map/pallas_call | solution.py:122
  404.5 12.2 %shard_map.246 = (bf16[1,64,2048]{2,1,0:T(8,128)(2,1)S(1)}, bf16[1,128,2048]{2,1,0:T(8,128)(2,1)S(1)}) custom-call(bf16[3,192,2048]{2,1,0:T(8,128)(2,1)} %bitcast.129, bf16[3,192,2048]{2,1,0:T(8,128)(2,1)} %bitcast.130, bf16[3,192,2048]{2,1,0:T(8,128)(2,1)} %bitcast.131, bf16[3,64,2048]{2,1,0:T(8,128)(2,1)S(1)} %bitcast.162, ...), custom_call_target="tpu_custom_call" | custom-call | flops 10737418240 | bytes 2359296 | tf_op jit(solution)/shard_map/pallas_call | solution.py:122
  436.7 5.4 %collective-permute-done.42.refs_3_ = bf16[192,512]{1,0:T(8,128)(2,1)} collective-permute-done((bf16[192,512]{1,0:T(8,128)(2,1)}, bf16[192,512]{1,0:T(8,128)(2,1)}, u32[]{:S(2)}, u32[]{:S(2)}) %collective-permute-start.42) | collective-permute-done | bytes 196640 | tf_op jit(solution)/shard_map/ppermute | solution.py:57
  448.5 3.7 fusion.117
  463.4 3.8 collective-permute-start.44
  467.3 6.8 %fusion.42 = (f32[768]{0:T(1024)S(1)}, f32[768]{0:T(1024)S(1)}, bf16[1,512,768]{2,1,0:T(8,128)(2,1)}, f32[1,512,768]{2,1,0:T(8,128)}) fusion(bf16[1,512,768]{2,1,0:T(8,128)(2,1)S(1)} %copy-done.54, f32[512,768]{1,0:T(8,128)} %fusion.114, f32[768]{0:T(1024)S(1)} %convert_element_type.251, f32[512,768]{1,0:T(8,128)} %get-tuple-element.269, ...), kind=kOutput, calls=%fused_computation.76 | convolution fusion | flops 1213463040 | bytes 14958592 | tf_op jit(solution)/shard_map/dot_general | solution.py:41
  477.6 15.6 %collective-permute-done.45 = bf16[192,960]{1,0:T(8,128)(2,1)} collective-permute-done((bf16[192,960]{1,0:T(8,128)(2,1)}, bf16[192,960]{1,0:T(8,128)(2,1)}, u32[]{:S(2)}, u32[]{:S(2)}) %collective-permute-start.45) | collective-permute-done | bytes 368672 | tf_op jit(solution)/shard_map/ppermute | solution.py:57
  498.1 8.0 %collective-permute-start.48 = (f32[14,768]{1,0:T(8,128)S(1)}, f32[14,768]{1,0:T(8,128)S(1)}, u32[]{:S(2)}, u32[]{:S(2)}) collective-permute-start(f32[14,768]{1,0:T(8,128)S(1)} %add.457), channel_id=1, source_target_pairs={{0,1},{1,0},{2,3},{3,2},{4,5},{5,4},{6,7},{7,6},{8,9},{9,8},{10,11... | collective-permute-start | bytes 129032 | tf_op jit(solution)/shard_map/ppermute | solution.py:75
  509.3 4.7 collective-permute-done.49
  (588 shorter events, 219.3 us)
Async XLA Ops:
  7.2 198.4 %all-gather.9.cloned.1.call-start = ((), (), s32[]{:S(2)}) async-start(), calls=%async_computation.7 | async-start | bytes 2949120 | tf_op jit(solution)/shard_map/all_gather | solution.py:420
  29.4 66.3 %collective-permute-start.9 = (bf16[512,768]{1,0:T(8,128)(2,1)S(1)}, bf16[512,768]{1,0:T(8,128)(2,1)S(1)}, u32[]{:S(2)}, u32[]{:S(2)}) collective-permute-start(bf16[512,768]{1,0:T(8,128)(2,1)S(1)} %bitcast.166), channel_id=1, source_target_pairs={{0,3},{1,0},{2,1},{3,2},{4,7},{5,4},{6,5},{7,6},{8,11},{9,8},{10,9... | collective-permute-start | bytes 2359304 | tf_op jit(solution)/shard_map/ppermute | solution.py:49
  30.7 67.7 %collective-permute-start.10 = (bf16[512,768]{1,0:T(8,128)(2,1)S(1)}, bf16[512,768]{1,0:T(8,128)(2,1)}, u32[]{:S(2)}, u32[]{:S(2)}) collective-permute-start(bf16[512,768]{1,0:T(8,128)(2,1)S(1)} %bitcast.167), channel_id=1, source_target_pairs={{0,2},{1,3},{2,0},{3,1},{4,6},{5,7},{6,4},{7,5},{8,10},{9,11},{10,... | collective-permute-start | bytes 2359304 | tf_op jit(solution)/shard_map/ppermute | solution.py:49
  31.4 67.0 %collective-permute-start.11 = (bf16[512,768]{1,0:T(8,128)(2,1)S(1)}, bf16[512,768]{1,0:T(8,128)(2,1)}, u32[]{:S(2)}, u32[]{:S(2)}) collective-permute-start(bf16[512,768]{1,0:T(8,128)(2,1)S(1)} %bitcast.168), channel_id=1, source_target_pairs={{0,1},{1,2},{2,3},{3,0},{4,5},{5,6},{6,7},{7,4},{8,9},{9,10},{10,1... | collective-permute-start | bytes 2359304 | tf_op jit(solution)/shard_map/ppermute | solution.py:49
  31.8 50.5 %collective-permute-start.19 = (bf16[192,384]{1,0:T(8,128)(2,1)S(1)}, bf16[192,384]{1,0:T(8,128)(2,1)S(1)}, u32[]{:S(2)}, u32[]{:S(2)}) collective-permute-start(bf16[192,384]{1,0:T(8,128)(2,1)S(1)} %dynamic-slice_bitcast_fusion.1), channel_id=1, source_target_pairs={{0,3},{1,0},{2,1},{3,2},{4,7},{5,4},{6,5},{7,6},{8,11},{9,8},{10,9... | collective-permute-start | bytes 442376 | tf_op jit(solution)/shard_map/ppermute | solution.py:49
  35.3 48.6 %collective-permute-start.6 = (bf16[192,576]{0,1:T(8,128)(2,1)}, bf16[192,576]{0,1:T(8,128)(2,1)}, u32[]{:S(2)}, u32[]{:S(2)}) collective-permute-start(bf16[192,576]{0,1:T(8,128)(2,1)} %bitcast.172), channel_id=1, source_target_pairs={{0,24},{8,16},{16,8},{24,0},{1,25},{9,17},{17,9},{25,1},{2,26},{10... | collective-permute-start | bytes 663560 | tf_op jit(solution)/shard_map/ppermute | solution.py:87
  87.2 118.5 %all-gather.7.cloned.1.call-start = ((), (), s32[]{:S(2)}) async-start(), calls=%async_computation.6 | async-start | bytes 1474560 | tf_op jit(solution)/shard_map/all_gather | solution.py:475
  98.5 32.4 %collective-permute-start.16 = (bf16[208,576]{1,0:T(8,128)(2,1)}, bf16[208,576]{1,0:T(8,128)(2,1)}, u32[]{:S(2)}, u32[]{:S(2)}) collective-permute-start(bf16[208,576]{1,0:T(8,128)(2,1)} %shard_map.233.refs_0_), channel_id=1, source_target_pairs={{0,3},{1,0},{2,1},{3,2},{4,7},{5,4},{6,5},{7,6},{8,11},{9,8},{10,9... | collective-permute-start | bytes 718856 | tf_op jit(solution)/shard_map/ppermute | solution.py:49
  100.9 34.1 %collective-permute-start.17 = (bf16[208,576]{1,0:T(8,128)(2,1)}, bf16[208,576]{1,0:T(8,128)(2,1)}, u32[]{:S(2)}, u32[]{:S(2)}) collective-permute-start(bf16[208,576]{1,0:T(8,128)(2,1)} %shard_map.233.refs_0_), channel_id=1, source_target_pairs={{0,2},{1,3},{2,0},{3,1},{4,6},{5,7},{6,4},{7,5},{8,10},{9,11},{10,... | collective-permute-start | bytes 718856 | tf_op jit(solution)/shard_map/ppermute | solution.py:49
  139.5 68.8 %all-gather.5.cloned.1.call-start = ((), (), s32[]{:S(2)}) async-start(), calls=%async_computation.5 | async-start | bytes 2949120 | tf_op jit(solution)/shard_map/all_gather | solution.py:469
  146.2 208.3 %all-gather.11.cloned.1.call-start = ((), (), s32[]{:S(2)}) async-start(), calls=%async_computation.8 | async-start | bytes 2211840 | tf_op jit(solution)/shard_map/all_gather | solution.py:502
  176.2 26.6 %collective-permute-start.15 = (bf16[192,512]{1,0:T(8,128)(2,1)S(1)}, bf16[192,512]{1,0:T(8,128)(2,1)S(1)}, u32[]{:S(2)}, u32[]{:S(2)}) collective-permute-start(bf16[192,512]{1,0:T(8,128)(2,1)S(1)} %bitcast.165), channel_id=1, source_target_pairs={{0,1},{1,2},{2,3},{3,0},{4,5},{5,6},{6,7},{7,4},{8,9},{9,10},{10,1... | collective-permute-start | bytes 589832 | tf_op jit(solution)/shard_map/ppermute | solution.py:57
  176.2 26.6 %collective-permute-start.14 = (bf16[192,512]{1,0:T(8,128)(2,1)S(1)}, bf16[192,512]{1,0:T(8,128)(2,1)}, u32[]{:S(2)}, u32[]{:S(2)}) collective-permute-start(bf16[192,512]{1,0:T(8,128)(2,1)S(1)} %bitcast.164), channel_id=1, source_target_pairs={{0,2},{1,3},{2,0},{3,1},{4,6},{5,7},{6,4},{7,5},{8,10},{9,11},{10,... | collective-permute-start | bytes 589832 | tf_op jit(solution)/shard_map/ppermute | solution.py:57
  202.7 252.1 %reduce-scatter.10.cloned.1.call-start = ((), (), s32[]{:S(2)}) async-start(), calls=%async_computation.11 | async-start | bytes 1474560 | tf_op jit(solution)/shard_map/reduce_scatter | solution.py:579
  205.6 25.5 %collective-permute-start.23 = (bf16[768,1536]{1,0:T(8,128)(2,1)}, bf16[768,1536]{1,0:T(8,128)(2,1)}, u32[]{:S(2)}, u32[]{:S(2)}) collective-permute-start(bf16[768,1536]{1,0:T(8,128)(2,1)} %all-gather.9.cloned.1.call-done), channel_id=1, source_target_pairs={{0,4},{4,0},{1,5},{5,1},{2,6},{6,2},{3,7},{7,3},{8,12},{12,8},{9,1... | collective-permute-start | bytes 7077896 | tf_op jit(solution)/shard_map/ppermute | solution.py:68
  208.4 21.4 %collective-permute-start.22 = (bf16[768,1536]{1,0:T(8,128)(2,1)}, bf16[768,1536]{1,0:T(8,128)(2,1)S(1)}, u32[]{:S(2)}, u32[]{:S(2)}) collective-permute-start(bf16[768,1536]{1,0:T(8,128)(2,1)} %get-tuple-element.92), channel_id=1, source_target_pairs={{0,4},{4,0},{1,5},{5,1},{2,6},{6,2},{3,7},{7,3},{8,12},{12,8},{9,1... | collective-permute-start | bytes 7077896 | tf_op jit(solution)/shard_map/ppermute | solution.py:68
  256.6 38.5 %collective-permute-start.27 = (bf16[768,1536]{1,0:T(8,128)(2,1)}, bf16[768,1536]{1,0:T(8,128)(2,1)}, u32[]{:S(2)}, u32[]{:S(2)}) collective-permute-start(bf16[768,1536]{1,0:T(8,128)(2,1)} %get-tuple-element.94.refs_5_), channel_id=1, source_target_pairs={{0,4},{4,0},{1,5},{5,1},{2,6},{6,2},{3,7},{7,3},{8,12},{12,8},{9,1... | collective-permute-start | bytes 7077896 | tf_op jit(solution)/shard_map/ppermute | solution.py:68
  257.2 37.9 %collective-permute-start.28 = (bf16[768,1536]{1,0:T(8,128)(2,1)}, bf16[768,1536]{1,0:T(8,128)(2,1)}, u32[]{:S(2)}, u32[]{:S(2)}) collective-permute-start(bf16[768,1536]{1,0:T(8,128)(2,1)} %get-tuple-element.96.refs_7_), channel_id=1, source_target_pairs={{0,4},{4,0},{1,5},{5,1},{2,6},{6,2},{3,7},{7,3},{8,12},{12,8},{9,1... | collective-permute-start | bytes 7077896 | tf_op jit(solution)/shard_map/ppermute | solution.py:68
  266.8 28.3 %collective-permute-start.29 = (bf16[768,768]{1,0:T(8,128)(2,1)S(1)}, bf16[768,768]{1,0:T(8,128)(2,1)}, u32[]{:S(2)}, u32[]{:S(2)}) collective-permute-start(bf16[768,768]{1,0:T(8,128)(2,1)S(1)} %get-tuple-element.97.refs_8_), channel_id=1, source_target_pairs={{0,4},{4,0},{1,5},{5,1},{2,6},{6,2},{3,7},{7,3},{8,12},{12,8},{9,1... | collective-permute-start | bytes 3538952 | tf_op jit(solution)/shard_map/ppermute | solution.py:68
  299.0 157.1 %reduce-scatter.6.cloned.1.call-start = ((), (), s32[]{:S(2)}) async-start(), calls=%async_computation.9 | async-start | bytes 2949120 | tf_op jit(solution)/shard_map/reduce_scatter | solution.py:579
  303.5 153.8 %reduce-scatter.8.cloned.1.call-start = ((), (), s32[]{:S(2)}) async-start(), calls=%async_computation.10 | async-start | bytes 2949120 | tf_op jit(solution)/shard_map/reduce_scatter | solution.py:579
  311.2 20.5 %collective-permute-start.30 = (bf16[128,2048]{1,0:T(8,128)(2,1)}, bf16[128,2048]{1,0:T(8,128)(2,1)}, u32[]{:S(2)}, u32[]{:S(2)}) collective-permute-start(bf16[128,2048]{1,0:T(8,128)(2,1)} %bitcast.18), channel_id=1, source_target_pairs={{0,4},{4,0},{1,5},{5,1},{2,6},{6,2},{3,7},{7,3},{8,12},{12,8},{9,1... | collective-permute-start | bytes 1572872 | tf_op jit(solution)/shard_map/ppermute | solution.py:68
  347.6 24.9 %collective-permute-start.34 = (bf16[128,2048]{1,0:T(8,128)(2,1)}, bf16[128,2048]{1,0:T(8,128)(2,1)}, u32[]{:S(2)}, u32[]{:S(2)}) collective-permute-start(bf16[128,2048]{1,0:T(8,128)(2,1)} %bitcast.21), channel_id=1, source_target_pairs={{0,4},{4,0},{1,5},{5,1},{2,6},{6,2},{3,7},{7,3},{8,12},{12,8},{9,1... | collective-permute-start | bytes 1572872 | tf_op jit(solution)/shard_map/ppermute | solution.py:68
  354.5 45.8 %collective-permute-start.38 = (bf16[2304,384]{1,0:T(8,128)(2,1)}, bf16[2304,384]{1,0:T(8,128)(2,1)}, u32[]{:S(2)}, u32[]{:S(2)}) collective-permute-start(bf16[2304,384]{1,0:T(8,128)(2,1)} %shard_map.245), channel_id=1, source_target_pairs={{0,4},{4,0},{1,5},{5,1},{2,6},{6,2},{3,7},{7,3},{8,12},{12,8},{9,1... | collective-permute-start | bytes 5308424 | tf_op jit(solution)/shard_map/ppermute | solution.py:68
  354.6 174.9 %reduce-scatter.12.cloned.1.call-start = ((), (), s32[]{:S(2)}) async-start(), calls=%async_computation.12 | async-start | bytes 368640 | tf_op jit(solution)/shard_map/reduce_scatter | solution.py:651
  377.3 20.5 %collective-permute-start.37 = (bf16[192,512]{1,0:T(8,128)(2,1)S(1)}, bf16[192,512]{1,0:T(8,128)(2,1)S(1)}, u32[]{:S(2)}, u32[]{:S(2)}) collective-permute-start(bf16[192,512]{1,0:T(8,128)(2,1)S(1)} %get-tuple-element.217), channel_id=1, source_target_pairs={{0,1},{1,2},{2,3},{3,0},{4,5},{5,6},{6,7},{7,4},{8,9},{9,10},{10,1... | collective-permute-start | bytes 589832 | tf_op jit(solution)/shard_map/ppermute | solution.py:57
  395.1 21.7 %collective-permute-start.40 = (bf16[128,2048]{1,0:T(8,128)(2,1)}, bf16[128,2048]{1,0:T(8,128)(2,1)}, u32[]{:S(2)}, u32[]{:S(2)}) collective-permute-start(bf16[128,2048]{1,0:T(8,128)(2,1)} %bitcast.28), channel_id=1, source_target_pairs={{0,4},{4,0},{1,5},{5,1},{2,6},{6,2},{3,7},{7,3},{8,12},{12,8},{9,1... | collective-permute-start | bytes 1572872 | tf_op jit(solution)/shard_map/ppermute | solution.py:68
  400.1 129.4 %reduce-scatter.14.cloned.1.call-start = ((), (), s32[]{:S(2)}) async-start(), calls=%async_computation.13 | async-start | bytes 245760 | tf_op jit(solution)/shard_map/reduce_scatter | solution.py:651
  431.8 64.5 %collective-permute-start.56 = (bf16[384,192]{1,0:T(8,128)(2,1)}, bf16[384,192]{1,0:T(8,128)(2,1)}, u32[]{:S(2)}, u32[]{:S(2)}) collective-permute-start(bf16[384,192]{1,0:T(8,128)(2,1)} %bitcast.178), channel_id=1, source_target_pairs={{0,4},{4,0},{1,5},{5,1},{2,6},{6,2},{3,7},{7,3},{8,12},{12,8},{9,1... | collective-permute-start | bytes 442376 | tf_op jit(solution)/shard_map/ppermute | solution.py:68
  463.4 29.9 %collective-permute-start.45 = (bf16[192,960]{1,0:T(8,128)(2,1)}, bf16[192,960]{1,0:T(8,128)(2,1)}, u32[]{:S(2)}, u32[]{:S(2)}) collective-permute-start(bf16[192,960]{1,0:T(8,128)(2,1)} %get-tuple-element.207), channel_id=1, source_target_pairs={{0,2},{1,3},{2,0},{3,1},{4,6},{5,7},{6,4},{7,5},{8,10},{9,11},{10,... | collective-permute-start | bytes 1105928 | tf_op jit(solution)/shard_map/ppermute | solution.py:57
  463.4 29.9 %collective-permute-start.44 = (bf16[192,960]{1,0:T(8,128)(2,1)}, bf16[192,960]{1,0:T(8,128)(2,1)}, u32[]{:S(2)}, u32[]{:S(2)}) collective-permute-start(bf16[192,960]{1,0:T(8,128)(2,1)} %get-tuple-element.205), channel_id=1, source_target_pairs={{0,3},{1,0},{2,1},{3,2},{4,7},{5,4},{6,5},{7,6},{8,11},{9,8},{10,9... | collective-permute-start | bytes 1105928 | tf_op jit(solution)/shard_map/ppermute | solution.py:57
  506.1 27.4 %collective-permute-start.57 = (f32[96,768]{1,0:T(8,128)S(1)}, f32[96,768]{1,0:T(8,128)S(1)}, u32[]{:S(2)}, u32[]{:S(2)}) collective-permute-start(f32[96,768]{1,0:T(8,128)S(1)} %constant_dynamic-slice_fusion.1), channel_id=1, source_target_pairs={{0,4},{4,0},{1,5},{5,1},{2,6},{6,2},{3,7},{7,3},{8,12},{12,8},{9,1... | collective-permute-start | bytes 884744 | tf_op jit(solution)/shard_map/ppermute | solution.py:68
  (164 other events, 1626.2 us)
Sparse Core Ops, SparseCore 0:
  87.3 51.4 all-gather.8
  141.2 27.7 all-gather.6
  170.8 37.4 all-gather.4
  210.3 40.3 all-gather.10
  299.1 27.4 reduce-scatter.9
  329.5 37.3 reduce-scatter.5
  369.9 37.3 reduce-scatter.7
  410.7 24.1 reduce-scatter.11
  498.1 29.0 reduce-scatter.13

commit v3 on v2

--- a/solution.py
+++ b/solution.py
@@ -318,7 +318,7 @@
 
 def weight_kernel(
     normed_ref, hidden_ref, far_hidden_ref, feed_ref, active_ref, far_active_ref, branch_ref, heads_ref,
-    expander_ref, far_expander_ref, reducer_ref, far_reducer_ref, merger_ref,
+    near_ref, far_ref,
     normed_columns, feed_columns, branch_columns,
 ):
     @pl.when(pl.program_id(0) == 0)
@@ -327,44 +327,49 @@
         feed_columns[...] = feed_ref[...].T
         branch_columns[...] = branch_ref[...].T
 
-    def product(left, right):
-        return jnp.dot(left, right, preferred_element_type=WIDE).astype(LOW)
-
-    expander_ref[...] = product(normed_columns[...], hidden_ref[...])
-    far_expander_ref[...] = product(normed_columns[...], far_hidden_ref[...])
-    reducer_ref[...] = product(feed_columns[...], active_ref[...])
-    far_reducer_ref[...] = product(feed_columns[...], far_active_ref[...])
-    count = merger_ref.shape[0]
-    place = pl.ds(pl.multiple_of(pl.program_id(0) * count, count), count)
-    merger_ref[...] = dot_wide(branch_columns[place, :], heads_ref[...], 1, 1).astype(LOW)
-
-
-def weight_terms(normed, grad_hidden, grad_feed, activated, grad_branch, attended, steps, before):
+    units, features = hidden_ref.shape[1], heads_ref.shape[0]
+    merger = dot_wide(branch_columns[...], heads_ref[...], 1, 1).astype(LOW)
+    for made_ref, hidden, active in (
+        (near_ref, hidden_ref, active_ref),
+        (far_ref, far_hidden_ref, far_active_ref),
+    ):
+        for start, left, right in ((0, normed_columns, hidden), (units, feed_columns, active)):
+            made_ref[:, start : start + units] = jnp.dot(
+                left[...], right[...], preferred_element_type=WIDE
+            ).astype(LOW)
+        made_ref[:, 2 * units :] = jnp.zeros((made_ref.shape[0], made_ref.shape[1] - 2 * units), LOW)
+        made_ref[:, 2 * units : 2 * units + features] = merger
+
+
+def padded_columns(count):
+    return -(-count // 128) * 128
+
+
+def weight_terms(normed, grad_hidden, grad_feed, activated, grad_branch, attended, steps):
     tokens, width = normed.shape
-    share = grad_hidden[0].shape[1]
+    units, features = grad_hidden[0].shape[1] // steps, attended.shape[0] // steps
+    columns = padded_columns(2 * units + features)
 
     def whole(array):
         return pl.BlockSpec(array.shape, lambda i: (0, 0))
 
-    units = pl.BlockSpec((tokens, share // steps), lambda i: (0, i))
-    made = pl.BlockSpec((width, share // steps), lambda i: (0, i))
-    operands = (normed, *grad_hidden, grad_feed, *activated, grad_branch, attended)
-    return ordered_call(
+    taken = pl.BlockSpec((tokens, units), lambda i: (0, i))
+    made = pl.BlockSpec((width, columns), lambda i: (0, i))
+    return pl.pallas_call(
         weight_kernel,
-        operands,
         grid=(steps,),
-        in_specs=[whole(normed), units, units, whole(grad_feed), units, units]
-        + [whole(grad_branch), whole(attended)],
-        out_specs=[made] * 4 + [pl.BlockSpec((width // steps, attended.shape[0]), lambda i: (i, 0))],
-        out_shape=[jax.ShapeDtypeStruct((width, share), LOW)] * 4
-        + [jax.ShapeDtypeStruct((width, attended.shape[0]), LOW)],
+        in_specs=[whole(normed), taken, taken, whole(grad_feed), taken, taken]
+        + [whole(grad_branch), pl.BlockSpec((features, tokens), lambda i: (i, 0))],
+        out_specs=[made] * 2,
+        out_shape=[jax.ShapeDtypeStruct((width, steps * columns), LOW)] * 2,
         scratch_shapes=[pltpu.VMEM((width, tokens), LOW)] * 3,
         compiler_params=pltpu.CompilerParams(vmem_limit_bytes=48 * 2**20),
         cost_estimate=pl.CostEstimate(
-            flops=2 * tokens * width * (4 * share + width), bytes_accessed=2**25, transcendentals=0
+            flops=2 * tokens * width * steps * (4 * units + features),
+            bytes_accessed=2**25,
+            transcendentals=0,
         ),
-        before=before,
-    )[0]
+    )(normed, *grad_hidden, grad_feed, *activated, grad_branch, attended)
 
 
 def core_half(grad):
@@ -529,10 +534,9 @@
         [grad_attended[r * local_width : (r + 1) * local_width] for r in range(tp_size)], "tp"
     )
 
-    weight_parts = weight_terms(
-        normed_two, grad_hidden, grad_feed, activated, grad_branch, attended, tp_size, (grad_attended,)
-    )
-    grad_blocks = tie(grad_blocks, *weight_parts)
+    weight_near, weight_far = weight_terms(
+        normed_two, grad_hidden, grad_feed, activated, grad_branch, attended, tp_size
+    )
     all_grads = jnp.concatenate(grad_blocks, 1).reshape(heads, HEAD_DIM, tokens)
 
     def in_order(left, right, axis):
@@ -573,13 +577,10 @@
         )
         before = ()
         if head == 0:
-            came = tie([swap_ctx(weight_parts[i]) for i in (1, 3, 4)], partial)
-            weight_halves = [sum_low(weight_parts[2 * i], came[i]) for i in range(3)]
-            weight_sums = [
-                lax.psum_scatter(half, "shard", scatter_dimension=0, tiled=True)
-                for half in weight_halves
-            ]
-            before = tuple(weight_halves)
+            (weight_came,) = tie([swap_ctx(weight_far)], partial)
+            weight_half = sum_low(weight_near, weight_came)
+            weight_sum = lax.psum_scatter(weight_half, "shard", scatter_dimension=0, tiled=True)
+            before = (weight_half,)
         elif head == 1:
             projectors = tie([projectors], partial)[0]
             other_projectors = swap_ctx(projectors)
@@ -615,27 +616,13 @@
         return sum(part.astype(WIDE) for part in parts)
 
     row_count = kept_rows // ctx_size
-    summed = from_peers(
-        tie(
-            [
-                jnp.concatenate(
-                    [
-                        part[:, r * (part.shape[1] // tp_size) : (r + 1) * (part.shape[1] // tp_size)]
-                        for r in range(tp_size)
-                        for part in weight_sums
-                    ],
-                    1,
-                )
-            ],
-            *arrived_rows[-1],
-        )[0]
-    )
+    summed = from_peers(weight_sum)
     two = summed[:, : 2 * half_hidden]
     own_two = lax.dynamic_slice_in_dim(two, core * row_count, row_count, 0)
     other_two = swap_ctx(lax.dynamic_slice_in_dim(two, (1 - core) * row_count, row_count, 0))
     grad_expander = in_order(own_two[:, :half_hidden], other_two[:, :half_hidden], 1)
     grad_reducer = in_order(own_two[:, half_hidden:], other_two[:, half_hidden:], 1).T
-    grad_merger = lax.dynamic_slice_in_dim(summed[:, 2 * half_hidden :], core * row_count, row_count, 0).T
+    grad_merger = lax.dynamic_slice_in_dim(summed[:, 2 * half_hidden : 2 * half_hidden + local_width], core * row_count, row_count, 0).T
 
     column_sums = jnp.sum(jnp.concatenate(head_rows, 0), 1, dtype=WIDE).reshape(heads, 3, HEAD_DIM)
     bias_sums = jnp.stack([column_sums[:, 0].reshape(-1), column_sums[:, 2].reshape(-1)])

time: 552 us -> 553 us (level)
  starting transfers between devices: 82.6 us -> 96.9 us
  waiting for transfers between devices: 105 us -> 115 us
  local copies, waits for them, and re-layouts: 88.3 us -> 78.4 us
  matrix products: 62.5 us -> 55.3 us
  other arithmetic: 58.8 us -> 53.1 us
    ppermute x18, starting transfers between devices: 22.9 us -> 37.6 us  [scatter_list(): lax.ppermute(blocks[r], axis, [(i, (i + r) % count) for i in range(count)])]
    pallas_call x22 -> x19, Pallas kernels: 128 us -> 115 us  [ordered_call(): pl.pallas_call(body, in_specs=list(in_specs) + [unread] * extra, out_spec...]
    pallas_call x0 -> x1, Pallas kernels: none -> 11.9 us  [weight_terms(): pl.pallas_call(weight_kernel, grid=(steps,), in_specs=[whole(normed), tak...]
    dot_general x15, matrix products: 58.8 us -> 51.6 us  [dot_wide(): lax.dot_general(left, right, (((left_dim,), (right_dim,)), ((), ())), pre...]
    ppermute x18, waiting for transfers between devices: 38.6 us -> 44.8 us  [scatter_list(): lax.ppermute(blocks[r], axis, [(i, (i + r) % count) for i in range(count)])]
    unnamed x271 -> x257, local copies, waits for them, and re-layouts: 33 us -> 29.4 us
    convert_element_type x5 -> x3, other arithmetic: 14.1 us -> 12.8 us  [sum_low(): return (left.astype(WIDE) + right.astype(WIDE)).astype(LOW)]
  transfers between devices with their start and end apart: 67 -> 63, of which waited for: 17 -> 18; matrix products, arithmetic and copies ran while one was open for 33% -> 27% of each run, Pallas kernels for 24% -> 21%
where the time goes in v3:
time: 553 us; the launch traced here: 544 us
  Pallas kernels  127 us (23%)
  waiting for transfers between devices  115 us (21%)
  starting transfers between devices  96.9 us (18%)
  local copies, waits for them, and re-layouts  78.4 us (14%)
  matrix products  55.3 us (10%)
  other arithmetic  53.1 us (10%)
  between operations  17.9 us (3%)
    pallas_call x19, Pallas kernels, ordered_call(): pl.pallas_call(body, in_specs=list(in_specs) + [unread] * extra, out_spec...  115 us
    dot_general x15, matrix products, dot_wide(): lax.dot_general(left, right, (((left_dim,), (right_dim,)), ((), ())), pre...  51.6 us
    ppermute x9, waiting for transfers between devices, gather_list(): lax.ppermute(block, axis, [(i, (i - r) % count) for i in range(count)])  50.3 us
    ppermute x18, waiting for transfers between devices, scatter_list(): lax.ppermute(blocks[r], axis, [(i, (i + r) % count) for i in range(count)])  44.8 us
    ppermute x18, starting transfers between devices, scatter_list(): lax.ppermute(blocks[r], axis, [(i, (i + r) % count) for i in range(count)])  37.6 us
    unnamed x257, local copies, waits for them, and re-layouts  29.4 us
    ppermute x9, starting transfers between devices, gather_list(): lax.ppermute(block, axis, [(i, (i - r) % count) for i in range(count)])  27.9 us
    ppermute x15, starting transfers between devices, mirror(): lax.ppermute(block, 'shard', [(i, i ^ r) for i in range(lax.axis_size('sh...  20.2 us
  transfers between devices with their start and end apart: 63, of which 18 were waited for; matrix products, arithmetic and copies ran while one was open for 27% of the time, Pallas kernels for 21%

profile of v3, /device:TPU:0, one launch (start us, length us, event | category | flops | bytes accessed | tf_op | source)
XLA Modules:
  0.0 544.0 jit_solution(3415489614913213347)
XLA Ops:
  8.9 3.9 collective-permute-start.2
  39.8 43.3 %collective-permute-done.19 = bf16[192,384]{1,0:T(8,128)(2,1)S(1)} collective-permute-done((bf16[192,384]{1,0:T(8,128)(2,1)S(1)}, bf16[192,384]{1,0:T(8,128)(2,1)S(1)}, u32[]{:S(2)}, u32[]{:S(2)}) %collective-permute-start.19) | collective-permute-done | bytes 147488 | tf_op jit(solution)/shard_map/ppermute | solution.py:49
  101.7 15.4 %collective-permute-start.17 = (bf16[208,576]{1,0:T(8,128)(2,1)}, bf16[208,576]{1,0:T(8,128)(2,1)}, u32[]{:S(2)}, u32[]{:S(2)}) collective-permute-start(bf16[208,576]{1,0:T(8,128)(2,1)} %shard_map.233.refs_0_), channel_id=1, source_target_pairs={{0,2},{1,3},{2,0},{3,1},{4,6},{5,7},{6,4},{7,5},{8,10},{9,11},{10,... | collective-permute-start | bytes 718856 | tf_op jit(solution)/shard_map/ppermute | solution.py:49
  125.1 6.7 %add_convert_fusion.1 = bf16[576,2048]{1,0:T(8,128)(2,1)} fusion(bf16[768,576]{0,1:T(8,128)(2,1)S(1)} %copy-done.50, f32[576]{0:T(1024)S(1)} %reshape.369, bf16[512,768]{1,0:T(8,128)(2,1)S(1)} %get-tuple-element.222, bf16[512,768]{1,0:T(8,128)(2,1)S(1)} %get-tuple-element.221, bf16[512,768]{1,0:T(8,128)(2,1)S(1)} %get-tuple-element.220, ...), kind=kOutput, calls=%fused_computation.6 | convolution fusion | flops 1826881536 | bytes 6392064 | tf_op jit(solution)/shard_map/dot_general | solution.py:41
  131.7 4.1 collective-permute-done.17.refs_2_
  154.7 10.6 %shard_map.229 = (bf16[3,64,512]{2,1,0:T(8,128)(2,1)S(1)}, f32[3,1,512]{2,1,0:T(1,128)S(1)}) custom-call(bf16[3,192,2048]{2,1,0:T(8,128)(2,1)S(1)} %bitcast.129, bf16[3,192,2048]{2,1,0:T(8,128)(2,1)S(1)} %bitcast.130, bf16[3,192,2048]{2,1,0:T(8,128)(2,1)S(1)} %bitcast.131, bf16[3,128,2048]{2,1,0:T(8,128)(2,1)} %collective-permute-done.12.refs_3_.refs_4_.refs_1_.refs_2_, ...), custom_call_target="tpu_custom_call" | custom-call | flops 6442450944 | bytes 3538944 | tf_op jit(solution)/shard_map/pallas_call | solution.py:122
  165.3 10.7 %shard_map.230 = (bf16[3,64,512]{2,1,0:T(8,128)(2,1)S(1)}, f32[3,1,512]{2,1,0:T(1,128)S(1)}) custom-call(bf16[3,192,2048]{2,1,0:T(8,128)(2,1)S(1)} %bitcast.132, bf16[3,192,2048]{2,1,0:T(8,128)(2,1)S(1)} %bitcast.133, bf16[3,192,2048]{2,1,0:T(8,128)(2,1)S(1)} %bitcast.134, bf16[3,128,2048]{2,1,0:T(8,128)(2,1)} %collective-permute-done.12.refs_3_.refs_4_.refs_1_.refs_2_, ...), custom_call_target="tpu_custom_call" | custom-call | flops 6442450944 | bytes 3538944 | tf_op jit(solution)/shard_map/pallas_call | solution.py:122
  176.4 10.6 %shard_map.231 = (bf16[3,64,512]{2,1,0:T(8,128)(2,1)S(1)}, f32[3,1,512]{2,1,0:T(1,128)S(1)}) custom-call(bf16[3,192,2048]{2,1,0:T(8,128)(2,1)S(1)} %bitcast.135, bf16[3,192,2048]{2,1,0:T(8,128)(2,1)S(1)} %bitcast.136, bf16[3,192,2048]{2,1,0:T(8,128)(2,1)S(1)} %bitcast.137, bf16[3,128,2048]{2,1,0:T(8,128)(2,1)} %collective-permute-done.12.refs_3_.refs_4_.refs_1_.refs_2_, ...), custom_call_target="tpu_custom_call" | custom-call | flops 6442450944 | bytes 3538944 | tf_op jit(solution)/shard_map/pallas_call | solution.py:122
  187.0 3.9 collective-permute-start.13
  190.9 10.6 %shard_map.232 = (bf16[3,64,512]{2,1,0:T(8,128)(2,1)S(1)}, f32[3,1,512]{2,1,0:T(1,128)S(1)}) custom-call(bf16[3,192,2048]{2,1,0:T(8,128)(2,1)S(1)} %bitcast.139, bf16[3,192,2048]{2,1,0:T(8,128)(2,1)S(1)} %bitcast.138, bf16[3,192,2048]{2,1,0:T(8,128)(2,1)S(1)} %bitcast.140, bf16[3,128,2048]{2,1,0:T(8,128)(2,1)} %collective-permute-done.12.refs_3_.refs_4_.refs_1_.refs_2_, ...), custom_call_target="tpu_custom_call" | custom-call | flops 6442450944 | bytes 3538944 | tf_op jit(solution)/shard_map/pallas_call | solution.py:122
  203.2 6.5 %all-gather.5.cloned.1.call-done.refs_0_ = bf16[768,1536]{1,0:T(8,128)(2,1)} async-done(((bf16[192,1536]{1,0:T(8,128)(2,1)}), bf16[768,1536]{1,0:T(8,128)(2,1)}) %all-gather.5.cloned.1.call-update) | async-done | bytes 2359312 | tf_op jit(solution)/shard_map/all_gather | solution.py:474
  209.8 3.9 fusion.102
  217.6 5.3 convert_reduce_fusion.2
  224.3 7.1 %convert_reduce_fusion.1 = (f32[1536]{0:T(1024)}, bf16[512,1536]{1,0:T(8,128)(2,1)S(1)}, bf16[512,1536]{1,0:T(8,128)(2,1)}) fusion(f32[512,1536]{1,0:T(8,128)S(1)} %convolution_add_fusion, bf16[512,768]{1,0:T(8,128)(2,1)S(1)} %get-tuple-element.168.feed_ref, bf16[768,1536]{1,0:T(8,128)(2,1)} %collective-permute-done.23), kind=kOutput, calls=%fused_computation.26 | convolution fusion | flops 1229978112 | bytes 9443328 | tf_op jit(solution)/shard_map/dot_general | solution.py:41
  237.2 11.9 %shard_map.237 = (bf16[768,4096]{1,0:T(8,128)(2,1)}, bf16[768,4096]{1,0:T(8,128)(2,1)}) custom-call(bf16[512,768]{1,0:T(8,128)(2,1)S(1)} %add_convert_fusion.3.normed_ref, bf16[512,1536]{1,0:T(8,128)(2,1)S(1)} %get-tuple-element.162.hidden_ref, bf16[512,1536]{1,0:T(8,128)(2,1)} %copy-done.120, bf16[512,768]{1,0:T(8,128)(2,1)S(1)} %get-tuple-element.168.feed_ref, ...), custom_call_target="tpu_custom_call" | custom-call | flops 5435817984 | bytes 33554432 | tf_op jit(solution)/shard_map/pallas_call | solution.py:358
  258.5 4.3 collective-permute-done.26
  262.8 16.4 %collective-permute-done.25 = bf16[192,512]{1,0:T(8,128)(2,1)S(1)} collective-permute-done((bf16[192,512]{1,0:T(8,128)(2,1)S(1)}, bf16[192,512]{1,0:T(8,128)(2,1)S(1)}, u32[]{:S(2)}, u32[]{:S(2)}) %collective-permute-start.25) | collective-permute-done | bytes 196640 | tf_op jit(solution)/shard_map/ppermute | solution.py:57
  279.3 12.3 %shard_map.236 = (f32[1,64,2048]{2,1,0:T(8,128)S(1)}, bf16[1,128,2048]{2,1,0:T(8,128)(2,1)S(1)}) custom-call(bf16[3,192,2048]{2,1,0:T(8,128)(2,1)} %bitcast.123, bf16[3,128,2048]{2,1,0:T(8,128)(2,1)} %collective-permute-done.12.refs_3_.refs_4_.refs_1_.refs_2_, bf16[3,128,2048]{2,1,0:T(8,128)(2,1)} %collective-permute-done.12.refs_3_.refs_4_.refs_1_.refs_2_, ...), custom_call_target="tpu_custom_call" | custom-call | flops 10737418240 | bytes 2359296 | tf_op jit(solution)/shard_map/pallas_call | solution.py:122
  293.2 10.3 %add_convert_fusion.refs_7_ = bf16[768,4096]{1,0:T(8,128)(2,1)} fusion(bf16[768,4096]{1,0:T(8,128)(2,1)} %shard_map.238, bf16[768,4096]{1,0:T(8,128)(2,1)} %get-tuple-element.88), kind=kLoop, calls=%fused_computation | loop fusion | flops 12582912 | bytes 18874368 | tf_op jit(solution)/shard_map/convert_element_type | solution.py:389
  305.5 4.8 fusion.111
  314.9 11.4 %shard_map.239 = (bf16[1,64,2048]{2,1,0:T(8,128)(2,1)S(1)}, bf16[1,128,2048]{2,1,0:T(8,128)(2,1)S(1)}) custom-call(bf16[3,192,2048]{2,1,0:T(8,128)(2,1)S(1)} %bitcast.141, bf16[3,192,2048]{2,1,0:T(8,128)(2,1)S(1)} %bitcast.142, bf16[3,192,2048]{2,1,0:T(8,128)(2,1)S(1)} %bitcast.143, bf16[3,64,2048]{2,1,0:T(8,128)(2,1)S(1)} %bitcast.158, ...), custom_call_target="tpu_custom_call" | custom-call | flops 10737418240 | bytes 2359296 | tf_op jit(solution)/shard_map/pallas_call | solution.py:122
  328.1 12.9 %shard_map.240 = (f32[1,64,2048]{2,1,0:T(8,128)S(1)}, bf16[1,128,2048]{2,1,0:T(8,128)(2,1)}) custom-call(bf16[3,192,2048]{2,1,0:T(8,128)(2,1)} %bitcast.124, bf16[3,128,2048]{2,1,0:T(8,128)(2,1)} %collective-permute-done.12.refs_3_.refs_4_.refs_1_.refs_2_, bf16[3,128,2048]{2,1,0:T(8,128)(2,1)} %collective-permute-done.12.refs_3_.refs_4_.refs_1_.refs_2_, ...), custom_call_target="tpu_custom_call" | custom-call | flops 10737418240 | bytes 2359296 | tf_op jit(solution)/shard_map/pallas_call | solution.py:122
  344.0 12.8 %collective-permute-start.29 = (bf16[192,512]{1,0:T(8,128)(2,1)}, bf16[192,512]{1,0:T(8,128)(2,1)S(1)}, u32[]{:S(2)}, u32[]{:S(2)}) collective-permute-start(bf16[192,512]{1,0:T(8,128)(2,1)} %get-tuple-element.200), channel_id=1, source_target_pairs={{0,3},{1,0},{2,1},{3,2},{4,7},{5,4},{6,5},{7,6},{8,11},{9,8},{10,9... | collective-permute-start | bytes 589832 | tf_op jit(solution)/shard_map/ppermute | solution.py:57
  364.1 11.1 %shard_map.241 = (bf16[1,64,2048]{2,1,0:T(8,128)(2,1)S(1)}, bf16[1,128,2048]{2,1,0:T(8,128)(2,1)S(1)}) custom-call(bf16[3,192,2048]{2,1,0:T(8,128)(2,1)S(1)} %bitcast.144, bf16[3,192,2048]{2,1,0:T(8,128)(2,1)S(1)} %bitcast.145, bf16[3,192,2048]{2,1,0:T(8,128)(2,1)S(1)} %bitcast.146, bf16[3,64,2048]{2,1,0:T(8,128)(2,1)S(1)} %bitcast.160, ...), custom_call_target="tpu_custom_call" | custom-call | flops 10737418240 | bytes 2359296 | tf_op jit(solution)/shard_map/pallas_call | solution.py:122
  390.1 12.8 %shard_map.242 = (f32[1,64,2048]{2,1,0:T(8,128)S(1)}, bf16[1,128,2048]{2,1,0:T(8,128)(2,1)}) custom-call(bf16[3,192,2048]{2,1,0:T(8,128)(2,1)} %bitcast.125, bf16[3,128,2048]{2,1,0:T(8,128)(2,1)} %collective-permute-done.12.refs_3_.refs_4_.refs_1_.refs_2_, bf16[3,128,2048]{2,1,0:T(8,128)(2,1)} %collective-permute-done.12.refs_3_.refs_4_.refs_1_.refs_2_, ...), custom_call_target="tpu_custom_call" | custom-call | flops 10737418240 | bytes 2359296 | tf_op jit(solution)/shard_map/pallas_call | solution.py:122
  411.0 12.2 %shard_map.245 = (bf16[1,64,2048]{2,1,0:T(8,128)(2,1)S(1)}, bf16[1,128,2048]{2,1,0:T(8,128)(2,1)S(1)}) custom-call(bf16[3,192,2048]{2,1,0:T(8,128)(2,1)} %bitcast.126, bf16[3,192,2048]{2,1,0:T(8,128)(2,1)} %bitcast.127, bf16[3,192,2048]{2,1,0:T(8,128)(2,1)} %bitcast.128, bf16[3,64,2048]{2,1,0:T(8,128)(2,1)S(1)} %bitcast.162, ...), custom_call_target="tpu_custom_call" | custom-call | flops 10737418240 | bytes 2359296 | tf_op jit(solution)/shard_map/pallas_call | solution.py:122
  443.0 6.3 %collective-permute-done.40 = bf16[192,512]{1,0:T(8,128)(2,1)} collective-permute-done((bf16[192,512]{1,0:T(8,128)(2,1)}, bf16[192,512]{1,0:T(8,128)(2,1)}, u32[]{:S(2)}, u32[]{:S(2)}) %collective-permute-start.40) | collective-permute-done | bytes 196640 | tf_op jit(solution)/shard_map/ppermute | solution.py:57
  464.6 4.1 collective-permute-start.42
  468.7 7.2 %fusion.42 = (f32[768]{0:T(1024)S(1)}, f32[768]{0:T(1024)S(1)}, bf16[1,512,768]{2,1,0:T(8,128)(2,1)}, f32[1,512,768]{2,1,0:T(8,128)}) fusion(bf16[1,512,768]{2,1,0:T(8,128)(2,1)S(1)} %copy-done.47, f32[512,768]{1,0:T(8,128)} %fusion.111, f32[768]{0:T(1024)S(1)} %copy-done.100, f32[512,768]{1,0:T(8,128)} %get-tuple-element.234, f32[512,768]{1,0:T(8,128)} %copy-done.44, ...), kind=kOutput, calls=%fused_computation.74 | convolution fusion | flops 1213463040 | bytes 14958592 | tf_op jit(solution)/shard_map/dot_general | solution.py:41
  478.8 15.7 %collective-permute-done.43 = bf16[192,1024]{1,0:T(8,128)(2,1)} collective-permute-done((bf16[192,1024]{1,0:T(8,128)(2,1)}, bf16[192,1024]{1,0:T(8,128)(2,1)}, u32[]{:S(2)}, u32[]{:S(2)}) %collective-permute-start.43) | collective-permute-done | bytes 393248 | tf_op jit(solution)/shard_map/ppermute | solution.py:57
  499.3 8.0 %collective-permute-start.46 = (f32[14,768]{1,0:T(8,128)S(1)}, f32[14,768]{1,0:T(8,128)S(1)}, u32[]{:S(2)}, u32[]{:S(2)}) collective-permute-start(f32[14,768]{1,0:T(8,128)S(1)} %add.445), channel_id=1, source_target_pairs={{0,1},{1,0},{2,3},{3,2},{4,5},{5,4},{6,7},{7,6},{8,9},{9,8},{10,11... | collective-permute-start | bytes 129032 | tf_op jit(solution)/shard_map/ppermute | solution.py:75
  510.5 4.7 collective-permute-done.47
  (556 shorter events, 204.3 us)
Async XLA Ops:
  8.1 195.0 %all-gather.9.cloned.1.call-start = ((), (), s32[]{:S(2)}) async-start(), calls=%async_computation.5 | async-start | bytes 2949120 | tf_op jit(solution)/shard_map/all_gather | solution.py:425
  16.4 19.6 %collective-permute-start.20 = (bf16[192,384]{1,0:T(8,128)(2,1)S(1)}, bf16[192,384]{1,0:T(8,128)(2,1)}, u32[]{:S(2)}, u32[]{:S(2)}) collective-permute-start(bf16[192,384]{1,0:T(8,128)(2,1)S(1)} %dynamic-slice_bitcast_fusion.1), channel_id=1, source_target_pairs={{0,2},{1,3},{2,0},{3,1},{4,6},{5,7},{6,4},{7,5},{8,10},{9,11},{10,... | collective-permute-start | bytes 442376 | tf_op jit(solution)/shard_map/ppermute | solution.py:49
  30.2 66.3 %collective-permute-start.9 = (bf16[512,768]{1,0:T(8,128)(2,1)S(1)}, bf16[512,768]{1,0:T(8,128)(2,1)S(1)}, u32[]{:S(2)}, u32[]{:S(2)}) collective-permute-start(bf16[512,768]{1,0:T(8,128)(2,1)S(1)} %bitcast.167), channel_id=1, source_target_pairs={{0,3},{1,0},{2,1},{3,2},{4,7},{5,4},{6,5},{7,6},{8,11},{9,8},{10,9... | collective-permute-start | bytes 2359304 | tf_op jit(solution)/shard_map/ppermute | solution.py:49
  31.6 67.7 %collective-permute-start.10 = (bf16[512,768]{1,0:T(8,128)(2,1)S(1)}, bf16[512,768]{1,0:T(8,128)(2,1)}, u32[]{:S(2)}, u32[]{:S(2)}) collective-permute-start(bf16[512,768]{1,0:T(8,128)(2,1)S(1)} %bitcast.168), channel_id=1, source_target_pairs={{0,2},{1,3},{2,0},{3,1},{4,6},{5,7},{6,4},{7,5},{8,10},{9,11},{10,... | collective-permute-start | bytes 2359304 | tf_op jit(solution)/shard_map/ppermute | solution.py:49
  32.3 67.0 %collective-permute-start.11 = (bf16[512,768]{1,0:T(8,128)(2,1)S(1)}, bf16[512,768]{1,0:T(8,128)(2,1)}, u32[]{:S(2)}, u32[]{:S(2)}) collective-permute-start(bf16[512,768]{1,0:T(8,128)(2,1)S(1)} %bitcast.169), channel_id=1, source_target_pairs={{0,1},{1,2},{2,3},{3,0},{4,5},{5,6},{6,7},{7,4},{8,9},{9,10},{10,1... | collective-permute-start | bytes 2359304 | tf_op jit(solution)/shard_map/ppermute | solution.py:49
  32.6 50.5 %collective-permute-start.19 = (bf16[192,384]{1,0:T(8,128)(2,1)S(1)}, bf16[192,384]{1,0:T(8,128)(2,1)S(1)}, u32[]{:S(2)}, u32[]{:S(2)}) collective-permute-start(bf16[192,384]{1,0:T(8,128)(2,1)S(1)} %dynamic-slice_bitcast_fusion.1), channel_id=1, source_target_pairs={{0,3},{1,0},{2,1},{3,2},{4,7},{5,4},{6,5},{7,6},{8,11},{9,8},{10,9... | collective-permute-start | bytes 442376 | tf_op jit(solution)/shard_map/ppermute | solution.py:49
  36.1 48.6 %collective-permute-start.6 = (bf16[192,576]{0,1:T(8,128)(2,1)}, bf16[192,576]{0,1:T(8,128)(2,1)}, u32[]{:S(2)}, u32[]{:S(2)}) collective-permute-start(bf16[192,576]{0,1:T(8,128)(2,1)} %bitcast.173), channel_id=1, source_target_pairs={{0,24},{8,16},{16,8},{24,0},{1,25},{9,17},{17,9},{25,1},{2,26},{10... | collective-permute-start | bytes 663560 | tf_op jit(solution)/shard_map/ppermute | solution.py:87
  88.0 115.2 %all-gather.7.cloned.1.call-start = ((), (), s32[]{:S(2)}) async-start(), calls=%async_computation.4 | async-start | bytes 1474560 | tf_op jit(solution)/shard_map/all_gather | solution.py:480
  99.3 32.4 %collective-permute-start.16 = (bf16[208,576]{1,0:T(8,128)(2,1)}, bf16[208,576]{1,0:T(8,128)(2,1)}, u32[]{:S(2)}, u32[]{:S(2)}) collective-permute-start(bf16[208,576]{1,0:T(8,128)(2,1)} %shard_map.233.refs_0_), channel_id=1, source_target_pairs={{0,3},{1,0},{2,1},{3,2},{4,7},{5,4},{6,5},{7,6},{8,11},{9,8},{10,9... | collective-permute-start | bytes 718856 | tf_op jit(solution)/shard_map/ppermute | solution.py:49
  101.7 34.1 %collective-permute-start.17 = (bf16[208,576]{1,0:T(8,128)(2,1)}, bf16[208,576]{1,0:T(8,128)(2,1)}, u32[]{:S(2)}, u32[]{:S(2)}) collective-permute-start(bf16[208,576]{1,0:T(8,128)(2,1)} %shard_map.233.refs_0_), channel_id=1, source_target_pairs={{0,2},{1,3},{2,0},{3,1},{4,6},{5,7},{6,4},{7,5},{8,10},{9,11},{10,... | collective-permute-start | bytes 718856 | tf_op jit(solution)/shard_map/ppermute | solution.py:49
  140.3 69.4 %all-gather.5.cloned.1.call-start = ((), (), s32[]{:S(2)}) async-start(), calls=%async_computation.3 | async-start | bytes 2949120 | tf_op jit(solution)/shard_map/all_gather | solution.py:474
  147.0 212.5 %all-gather.11.cloned.1.call-start = ((), (), s32[]{:S(2)}) async-start(), calls=%async_computation.6 | async-start | bytes 2211840 | tf_op jit(solution)/shard_map/all_gather | solution.py:507
  175.9 26.2 %collective-permute-start.15 = (bf16[192,512]{1,0:T(8,128)(2,1)S(1)}, bf16[192,512]{1,0:T(8,128)(2,1)S(1)}, u32[]{:S(2)}, u32[]{:S(2)}) collective-permute-start(bf16[192,512]{1,0:T(8,128)(2,1)S(1)} %bitcast.164), channel_id=1, source_target_pairs={{0,1},{1,2},{2,3},{3,0},{4,5},{5,6},{6,7},{7,4},{8,9},{9,10},{10,1... | collective-permute-start | bytes 589832 | tf_op jit(solution)/shard_map/ppermute | solution.py:57
  176.0 26.1 %collective-permute-start.14 = (bf16[192,512]{1,0:T(8,128)(2,1)S(1)}, bf16[192,512]{1,0:T(8,128)(2,1)S(1)}, u32[]{:S(2)}, u32[]{:S(2)}) collective-permute-start(bf16[192,512]{1,0:T(8,128)(2,1)S(1)} %bitcast.163), channel_id=1, source_target_pairs={{0,2},{1,3},{2,0},{3,1},{4,6},{5,7},{6,4},{7,5},{8,10},{9,11},{10,... | collective-permute-start | bytes 589832 | tf_op jit(solution)/shard_map/ppermute | solution.py:57
  203.1 21.2 %collective-permute-start.23 = (bf16[768,1536]{1,0:T(8,128)(2,1)}, bf16[768,1536]{1,0:T(8,128)(2,1)}, u32[]{:S(2)}, u32[]{:S(2)}) collective-permute-start(bf16[768,1536]{1,0:T(8,128)(2,1)} %all-gather.9.cloned.1.call-done), channel_id=1, source_target_pairs={{0,4},{4,0},{1,5},{5,1},{2,6},{6,2},{3,7},{7,3},{8,12},{12,8},{9,1... | collective-permute-start | bytes 7077896 | tf_op jit(solution)/shard_map/ppermute | solution.py:68
  249.2 43.2 %collective-permute-start.27 = (bf16[768,4096]{1,0:T(8,128)(2,1)}, bf16[768,4096]{1,0:T(8,128)(2,1)}, u32[]{:S(2)}, u32[]{:S(2)}) collective-permute-start(bf16[768,4096]{1,0:T(8,128)(2,1)} %get-tuple-element.89), channel_id=1, source_target_pairs={{0,4},{4,0},{1,5},{5,1},{2,6},{6,2},{3,7},{7,3},{8,12},{12,8},{9,1... | collective-permute-start | bytes 18874376 | tf_op jit(solution)/shard_map/ppermute | solution.py:68
  250.6 211.6 %reduce-scatter.4.cloned.1.call-start = ((), (), s32[]{:S(2)}) async-start(), calls=%async_computation.7 | async-start | bytes 7864320 | tf_op jit(solution)/shard_map/reduce_scatter | solution.py:582
  254.6 24.6 %collective-permute-start.25 = (bf16[192,512]{1,0:T(8,128)(2,1)S(1)}, bf16[192,512]{1,0:T(8,128)(2,1)S(1)}, u32[]{:S(2)}, u32[]{:S(2)}) collective-permute-start(bf16[192,512]{1,0:T(8,128)(2,1)S(1)} %get-tuple-element.206), channel_id=1, source_target_pairs={{0,2},{1,3},{2,0},{3,1},{4,6},{5,7},{6,4},{7,5},{8,10},{9,11},{10,... | collective-permute-start | bytes 589832 | tf_op jit(solution)/shard_map/ppermute | solution.py:57
  257.0 22.2 %collective-permute-start.24 = (bf16[192,512]{1,0:T(8,128)(2,1)S(1)}, bf16[192,512]{1,0:T(8,128)(2,1)S(1)}, u32[]{:S(2)}, u32[]{:S(2)}) collective-permute-start(bf16[192,512]{1,0:T(8,128)(2,1)S(1)} %get-tuple-element.207), channel_id=1, source_target_pairs={{0,3},{1,0},{2,1},{3,2},{4,7},{5,4},{6,5},{7,6},{8,11},{9,8},{10,9... | collective-permute-start | bytes 589832 | tf_op jit(solution)/shard_map/ppermute | solution.py:57
  303.6 226.9 %reduce-scatter.6.cloned.1.call-start = ((), (), s32[]{:S(2)}) async-start(), calls=%async_computation.8 | async-start | bytes 368640 | tf_op jit(solution)/shard_map/reduce_scatter | solution.py:638
  341.0 39.5 %collective-permute-start.32 = (bf16[128,2048]{1,0:T(8,128)(2,1)}, bf16[128,2048]{1,0:T(8,128)(2,1)}, u32[]{:S(2)}, u32[]{:S(2)}) collective-permute-start(bf16[128,2048]{1,0:T(8,128)(2,1)} %bitcast.21), channel_id=1, source_target_pairs={{0,4},{4,0},{1,5},{5,1},{2,6},{6,2},{3,7},{7,3},{8,12},{12,8},{9,1... | collective-permute-start | bytes 1572872 | tf_op jit(solution)/shard_map/ppermute | solution.py:68
  344.0 32.0 %collective-permute-start.29 = (bf16[192,512]{1,0:T(8,128)(2,1)}, bf16[192,512]{1,0:T(8,128)(2,1)S(1)}, u32[]{:S(2)}, u32[]{:S(2)}) collective-permute-start(bf16[192,512]{1,0:T(8,128)(2,1)} %get-tuple-element.200), channel_id=1, source_target_pairs={{0,3},{1,0},{2,1},{3,2},{4,7},{5,4},{6,5},{7,6},{8,11},{9,8},{10,9... | collective-permute-start | bytes 589832 | tf_op jit(solution)/shard_map/ppermute | solution.py:57
  356.8 20.4 %collective-permute-start.30 = (bf16[192,512]{1,0:T(8,128)(2,1)}, bf16[192,512]{1,0:T(8,128)(2,1)}, u32[]{:S(2)}, u32[]{:S(2)}) collective-permute-start(bf16[192,512]{1,0:T(8,128)(2,1)} %get-tuple-element.201), channel_id=1, source_target_pairs={{0,2},{1,3},{2,0},{3,1},{4,6},{5,7},{6,4},{7,5},{8,10},{9,11},{10,... | collective-permute-start | bytes 589832 | tf_op jit(solution)/shard_map/ppermute | solution.py:57
  359.5 47.4 %collective-permute-start.36 = (bf16[2304,384]{1,0:T(8,128)(2,1)}, bf16[2304,384]{1,0:T(8,128)(2,1)}, u32[]{:S(2)}, u32[]{:S(2)}) collective-permute-start(bf16[2304,384]{1,0:T(8,128)(2,1)} %shard_map.244), channel_id=1, source_target_pairs={{0,4},{4,0},{1,5},{5,1},{2,6},{6,2},{3,7},{7,3},{8,12},{12,8},{9,1... | collective-permute-start | bytes 5308424 | tf_op jit(solution)/shard_map/ppermute | solution.py:68
  383.5 19.5 %collective-permute-start.33 = (bf16[192,512]{1,0:T(8,128)(2,1)S(1)}, bf16[192,512]{1,0:T(8,128)(2,1)S(1)}, u32[]{:S(2)}, u32[]{:S(2)}) collective-permute-start(bf16[192,512]{1,0:T(8,128)(2,1)S(1)} %get-tuple-element.195), channel_id=1, source_target_pairs={{0,3},{1,0},{2,1},{3,2},{4,7},{5,4},{6,5},{7,6},{8,11},{9,8},{10,9... | collective-permute-start | bytes 589832 | tf_op jit(solution)/shard_map/ppermute | solution.py:57
  403.0 20.3 %collective-permute-start.38 = (bf16[128,2048]{1,0:T(8,128)(2,1)}, bf16[128,2048]{1,0:T(8,128)(2,1)}, u32[]{:S(2)}, u32[]{:S(2)}) collective-permute-start(bf16[128,2048]{1,0:T(8,128)(2,1)} %bitcast.28), channel_id=1, source_target_pairs={{0,4},{4,0},{1,5},{5,1},{2,6},{6,2},{3,7},{7,3},{8,12},{12,8},{9,1... | collective-permute-start | bytes 1572872 | tf_op jit(solution)/shard_map/ppermute | solution.py:68
  406.6 123.9 %reduce-scatter.8.cloned.1.call-start = ((), (), s32[]{:S(2)}) async-start(), calls=%async_computation.9 | async-start | bytes 245760 | tf_op jit(solution)/shard_map/reduce_scatter | solution.py:638
  431.1 19.9 %collective-permute-start.41 = (bf16[192,512]{1,0:T(8,128)(2,1)}, bf16[192,512]{1,0:T(8,128)(2,1)}, u32[]{:S(2)}, u32[]{:S(2)}) collective-permute-start(bf16[192,512]{1,0:T(8,128)(2,1)} %get-tuple-element.190), channel_id=1, source_target_pairs={{0,1},{1,2},{2,3},{3,0},{4,5},{5,6},{6,7},{7,4},{8,9},{9,10},{10,1... | collective-permute-start | bytes 589832 | tf_op jit(solution)/shard_map/ppermute | solution.py:57
  438.8 58.7 %collective-permute-start.54 = (bf16[384,192]{1,0:T(8,128)(2,1)}, bf16[384,192]{1,0:T(8,128)(2,1)}, u32[]{:S(2)}, u32[]{:S(2)}) collective-permute-start(bf16[384,192]{1,0:T(8,128)(2,1)} %bitcast.179), channel_id=1, source_target_pairs={{0,4},{4,0},{1,5},{5,1},{2,6},{6,2},{3,7},{7,3},{8,12},{12,8},{9,1... | collective-permute-start | bytes 442376 | tf_op jit(solution)/shard_map/ppermute | solution.py:68
  464.6 29.9 %collective-permute-start.43 = (bf16[192,1024]{1,0:T(8,128)(2,1)}, bf16[192,1024]{1,0:T(8,128)(2,1)}, u32[]{:S(2)}, u32[]{:S(2)}) collective-permute-start(bf16[192,1024]{1,0:T(8,128)(2,1)} %get-tuple-element.185), channel_id=1, source_target_pairs={{0,2},{1,3},{2,0},{3,1},{4,6},{5,7},{6,4},{7,5},{8,10},{9,11},{10,... | collective-permute-start | bytes 1179656 | tf_op jit(solution)/shard_map/ppermute | solution.py:57
  464.6 29.9 %collective-permute-start.42 = (bf16[192,1024]{1,0:T(8,128)(2,1)}, bf16[192,1024]{1,0:T(8,128)(2,1)}, u32[]{:S(2)}, u32[]{:S(2)}) collective-permute-start(bf16[192,1024]{1,0:T(8,128)(2,1)} %get-tuple-element.183), channel_id=1, source_target_pairs={{0,3},{1,0},{2,1},{3,2},{4,7},{5,4},{6,5},{7,6},{8,11},{9,8},{10,9... | collective-permute-start | bytes 1179656 | tf_op jit(solution)/shard_map/ppermute | solution.py:57
  507.3 27.3 %collective-permute-start.55 = (f32[96,768]{1,0:T(8,128)S(1)}, f32[96,768]{1,0:T(8,128)S(1)}, u32[]{:S(2)}, u32[]{:S(2)}) collective-permute-start(f32[96,768]{1,0:T(8,128)S(1)} %constant_dynamic-slice_fusion.1), channel_id=1, source_target_pairs={{0,4},{4,0},{1,5},{5,1},{2,6},{6,2},{3,7},{7,3},{8,12},{12,8},{9,1... | collective-permute-start | bytes 884744 | tf_op jit(solution)/shard_map/ppermute | solution.py:68
  (153 other events, 1498.0 us)
Sparse Core Ops, SparseCore 0:
  88.2 51.4 all-gather.8
  142.1 27.7 all-gather.6
  172.2 37.4 all-gather.4
  303.7 80.8 reduce-scatter.3
  406.7 24.1 reduce-scatter.5
  499.3 28.7 reduce-scatter.7
Sparse Core Ops, SparseCore 1:
  250.6 52.4 all-gather.10

commit v4 on v3

--- a/solution.py
+++ b/solution.py
@@ -630,7 +630,6 @@
         jnp.zeros((2, model_width), WIDE), bias_sums, lax.axis_index("tp") * local_width, 1
     )
     sums = jnp.concatenate([grad_shift_one, grad_scale_one, early_sums, bias_sums], 0)
-    sums = tie([sums], summed)[0]
     all_sums = mirror_gather(sum_over(sums, ("ctx", "tp")))
     total = tree_sum(all_sums)
 

time: 553 us -> 555 us (level)
  the two profiles are of different devices: /device:TPU:0 before, /device:TPU:9 now
where the time goes in v4:
time: 555 us; the launch traced here: 546 us
  waiting for transfers between devices  147 us (26%)
  Pallas kernels  127 us (23%)
  local copies, waits for them, and re-layouts  82 us (15%)
  starting transfers between devices  68.6 us (12%)
  matrix products  53.2 us (10%)
  other arithmetic  50.6 us (9%)
  between operations  17.9 us (3%)
    pallas_call x18, Pallas kernels, ordered_call(): pl.pallas_call(body, in_specs=list(in_specs) + [unread] * extra, out_spec...  115 us
    ppermute x9, waiting for transfers between devices, gather_list(): lax.ppermute(block, axis, [(i, (i - r) % count) for i in range(count)])  62.4 us
    ppermute x18, waiting for transfers between devices, scatter_list(): lax.ppermute(blocks[r], axis, [(i, (i + r) % count) for i in range(count)])  59.1 us
    dot_general x15, matrix products, dot_wide(): lax.dot_general(left, right, (((left_dim,), (right_dim,)), ((), ())), pre...  49.5 us
    unnamed x265, local copies, waits for them, and re-layouts  31 us
    ppermute x18, starting transfers between devices, scatter_list(): lax.ppermute(blocks[r], axis, [(i, (i + r) % count) for i in range(count)])  24.2 us
    ppermute x11, starting transfers between devices, swap_ctx(): lax.ppermute(block, 'ctx', [(i, (i + 1) % count) for i in range(count)])  16.2 us
    ppermute x15, starting transfers between devices, mirror(): lax.ppermute(block, 'shard', [(i, i ^ r) for i in range(lax.axis_size('sh...  15.3 us
  transfers between devices with their start and end apart: 63, of which 16 were waited for; matrix products, arithmetic and copies ran while one was open for 26% of the time, Pallas kernels for 21%

profile of v4, /device:TPU:9, one launch (start us, length us, event | category | flops | bytes accessed | tf_op | source)
XLA Modules:
  0.0 546.0 jit_solution(15009013419268574480)
XLA Ops:
  32.8 62.3 %collective-permute-done.19 = bf16[192,384]{1,0:T(8,128)(2,1)S(1)} collective-permute-done((bf16[192,384]{1,0:T(8,128)(2,1)S(1)}, bf16[192,384]{1,0:T(8,128)(2,1)S(1)}, u32[]{:S(2)}, u32[]{:S(2)}) %collective-permute-start.19) | collective-permute-done | bytes 147488 | tf_op jit(solution)/shard_map/ppermute | solution.py:49
  117.2 6.6 %add_convert_fusion.1 = bf16[576,2048]{1,0:T(8,128)(2,1)} fusion(bf16[768,576]{0,1:T(8,128)(2,1)S(1)} %copy-done.50, f32[576]{0:T(1024)S(1)} %reshape.369, bf16[512,768]{1,0:T(8,128)(2,1)S(1)} %get-tuple-element.222, bf16[512,768]{1,0:T(8,128)(2,1)S(1)} %get-tuple-element.221, bf16[512,768]{1,0:T(8,128)(2,1)S(1)} %get-tuple-element.220, ...), kind=kOutput, calls=%fused_computation.6 | convolution fusion | flops 1826881536 | bytes 6392064 | tf_op jit(solution)/shard_map/dot_general | solution.py:41
  131.3 7.3 %collective-permute-start.12 = (bf16[3,128,2048]{2,1,0:T(8,128)(2,1)}, bf16[3,128,2048]{2,1,0:T(8,128)(2,1)}, u32[]{:S(2)}, u32[]{:S(2)}) collective-permute-start(bf16[3,128,2048]{2,1,0:T(8,128)(2,1)} %slice.322), channel_id=1, source_target_pairs={{0,4},{4,0},{1,5},{5,1},{2,6},{6,2},{3,7},{7,3},{8,12},{12,8},{9,1... | collective-permute-start | bytes 4718600 | tf_op jit(solution)/shard_map/ppermute | solution.py:68
  150.1 10.6 %shard_map.229 = (bf16[3,64,512]{2,1,0:T(8,128)(2,1)S(1)}, f32[3,1,512]{2,1,0:T(1,128)S(1)}) custom-call(bf16[3,192,2048]{2,1,0:T(8,128)(2,1)S(1)} %bitcast.129, bf16[3,192,2048]{2,1,0:T(8,128)(2,1)S(1)} %bitcast.130, bf16[3,192,2048]{2,1,0:T(8,128)(2,1)S(1)} %bitcast.131, bf16[3,128,2048]{2,1,0:T(8,128)(2,1)} %collective-permute-done.12.refs_3_.refs_4_.refs_1_.refs_2_, ...), custom_call_target="tpu_custom_call" | custom-call | flops 6442450944 | bytes 3538944 | tf_op jit(solution)/shard_map/pallas_call | solution.py:122
  160.7 10.7 %shard_map.230 = (bf16[3,64,512]{2,1,0:T(8,128)(2,1)S(1)}, f32[3,1,512]{2,1,0:T(1,128)S(1)}) custom-call(bf16[3,192,2048]{2,1,0:T(8,128)(2,1)S(1)} %bitcast.132, bf16[3,192,2048]{2,1,0:T(8,128)(2,1)S(1)} %bitcast.133, bf16[3,192,2048]{2,1,0:T(8,128)(2,1)S(1)} %bitcast.134, bf16[3,128,2048]{2,1,0:T(8,128)(2,1)} %collective-permute-done.12.refs_3_.refs_4_.refs_1_.refs_2_, ...), custom_call_target="tpu_custom_call" | custom-call | flops 6442450944 | bytes 3538944 | tf_op jit(solution)/shard_map/pallas_call | solution.py:122
  173.4 4.0 collective-permute-start.14
  177.4 10.6 %shard_map.231 = (bf16[3,64,512]{2,1,0:T(8,128)(2,1)S(1)}, f32[3,1,512]{2,1,0:T(1,128)S(1)}) custom-call(bf16[3,192,2048]{2,1,0:T(8,128)(2,1)S(1)} %bitcast.135, bf16[3,192,2048]{2,1,0:T(8,128)(2,1)S(1)} %bitcast.136, bf16[3,192,2048]{2,1,0:T(8,128)(2,1)S(1)} %bitcast.137, bf16[3,128,2048]{2,1,0:T(8,128)(2,1)} %collective-permute-done.12.refs_3_.refs_4_.refs_1_.refs_2_, ...), custom_call_target="tpu_custom_call" | custom-call | flops 6442450944 | bytes 3538944 | tf_op jit(solution)/shard_map/pallas_call | solution.py:122
  188.5 10.6 %shard_map.232 = (bf16[3,64,512]{2,1,0:T(8,128)(2,1)S(1)}, f32[3,1,512]{2,1,0:T(1,128)S(1)}) custom-call(bf16[3,192,2048]{2,1,0:T(8,128)(2,1)S(1)} %bitcast.139, bf16[3,192,2048]{2,1,0:T(8,128)(2,1)S(1)} %bitcast.138, bf16[3,192,2048]{2,1,0:T(8,128)(2,1)S(1)} %bitcast.140, bf16[3,128,2048]{2,1,0:T(8,128)(2,1)} %collective-permute-done.12.refs_3_.refs_4_.refs_1_.refs_2_, ...), custom_call_target="tpu_custom_call" | custom-call | flops 6442450944 | bytes 3538944 | tf_op jit(solution)/shard_map/pallas_call | solution.py:122
  201.4 6.8 %all-gather.5.cloned.1.call-done.refs_0_ = bf16[768,1536]{1,0:T(8,128)(2,1)} async-done(((bf16[192,1536]{1,0:T(8,128)(2,1)}), bf16[768,1536]{1,0:T(8,128)(2,1)}) %all-gather.5.cloned.1.call-update) | async-done | bytes 2359312 | tf_op jit(solution)/shard_map/all_gather | solution.py:474
  208.9 3.9 fusion.102
  216.7 5.3 convert_reduce_fusion.2
  223.4 7.1 %convert_reduce_fusion.1 = (f32[1536]{0:T(1024)}, bf16[512,1536]{1,0:T(8,128)(2,1)S(1)}, bf16[512,1536]{1,0:T(8,128)(2,1)}) fusion(f32[512,1536]{1,0:T(8,128)S(1)} %convolution_add_fusion, bf16[512,768]{1,0:T(8,128)(2,1)S(1)} %get-tuple-element.168.feed_ref, bf16[768,1536]{1,0:T(8,128)(2,1)} %collective-permute-done.23), kind=kOutput, calls=%fused_computation.26 | convolution fusion | flops 1229978112 | bytes 9443328 | tf_op jit(solution)/shard_map/dot_general | solution.py:41
  236.3 12.0 %shard_map.237 = (bf16[768,4096]{1,0:T(8,128)(2,1)}, bf16[768,4096]{1,0:T(8,128)(2,1)}) custom-call(bf16[512,768]{1,0:T(8,128)(2,1)S(1)} %add_convert_fusion.3.normed_ref, bf16[512,1536]{1,0:T(8,128)(2,1)S(1)} %get-tuple-element.162.hidden_ref, bf16[512,1536]{1,0:T(8,128)(2,1)} %copy-done.124, bf16[512,768]{1,0:T(8,128)(2,1)S(1)} %get-tuple-element.168.feed_ref, ...), custom_call_target="tpu_custom_call" | custom-call | flops 5435817984 | bytes 33554432 | tf_op jit(solution)/shard_map/pallas_call | solution.py:358
  257.8 21.9 %collective-permute-done.25 = bf16[192,512]{1,0:T(8,128)(2,1)S(1)} collective-permute-done((bf16[192,512]{1,0:T(8,128)(2,1)S(1)}, bf16[192,512]{1,0:T(8,128)(2,1)S(1)}, u32[]{:S(2)}, u32[]{:S(2)}) %collective-permute-start.25) | collective-permute-done | bytes 196640 | tf_op jit(solution)/shard_map/ppermute | solution.py:57
  279.6 10.4 %collective-permute-done.24 = bf16[192,512]{1,0:T(8,128)(2,1)S(1)} collective-permute-done((bf16[192,512]{1,0:T(8,128)(2,1)S(1)}, bf16[192,512]{1,0:T(8,128)(2,1)S(1)}, u32[]{:S(2)}, u32[]{:S(2)}) %collective-permute-start.24) | collective-permute-done | bytes 196640 | tf_op jit(solution)/shard_map/ppermute | solution.py:57
  290.2 12.3 %shard_map.236 = (f32[1,64,2048]{2,1,0:T(8,128)S(1)}, bf16[1,128,2048]{2,1,0:T(8,128)(2,1)S(1)}) custom-call(bf16[3,192,2048]{2,1,0:T(8,128)(2,1)} %bitcast.123, bf16[3,128,2048]{2,1,0:T(8,128)(2,1)} %collective-permute-done.12.refs_3_.refs_4_.refs_1_.refs_2_, bf16[3,128,2048]{2,1,0:T(8,128)(2,1)} %collective-permute-done.12.refs_3_.refs_4_.refs_1_.refs_2_, ...), custom_call_target="tpu_custom_call" | custom-call | flops 10737418240 | bytes 2359296 | tf_op jit(solution)/shard_map/pallas_call | solution.py:122
  304.0 10.3 %add_convert_fusion.refs_7_ = bf16[768,4096]{1,0:T(8,128)(2,1)} fusion(bf16[768,4096]{1,0:T(8,128)(2,1)} %shard_map.238, bf16[768,4096]{1,0:T(8,128)(2,1)} %get-tuple-element.88), kind=kLoop, calls=%fused_computation | loop fusion | flops 12582912 | bytes 18874368 | tf_op jit(solution)/shard_map/convert_element_type | solution.py:389
  316.3 4.8 fusion.111
  326.7 11.4 %shard_map.239 = (bf16[1,64,2048]{2,1,0:T(8,128)(2,1)S(1)}, bf16[1,128,2048]{2,1,0:T(8,128)(2,1)S(1)}) custom-call(bf16[3,192,2048]{2,1,0:T(8,128)(2,1)S(1)} %bitcast.141, bf16[3,192,2048]{2,1,0:T(8,128)(2,1)S(1)} %bitcast.142, bf16[3,192,2048]{2,1,0:T(8,128)(2,1)S(1)} %bitcast.143, bf16[3,64,2048]{2,1,0:T(8,128)(2,1)S(1)} %bitcast.158, ...), custom_call_target="tpu_custom_call" | custom-call | flops 10737418240 | bytes 2359296 | tf_op jit(solution)/shard_map/pallas_call | solution.py:122
  339.8 12.9 %shard_map.240 = (f32[1,64,2048]{2,1,0:T(8,128)S(1)}, bf16[1,128,2048]{2,1,0:T(8,128)(2,1)}) custom-call(bf16[3,192,2048]{2,1,0:T(8,128)(2,1)} %bitcast.124, bf16[3,128,2048]{2,1,0:T(8,128)(2,1)} %collective-permute-done.12.refs_3_.refs_4_.refs_1_.refs_2_, bf16[3,128,2048]{2,1,0:T(8,128)(2,1)} %collective-permute-done.12.refs_3_.refs_4_.refs_1_.refs_2_, ...), custom_call_target="tpu_custom_call" | custom-call | flops 10737418240 | bytes 2359296 | tf_op jit(solution)/shard_map/pallas_call | solution.py:122
  361.5 11.1 %shard_map.241 = (bf16[1,64,2048]{2,1,0:T(8,128)(2,1)S(1)}, bf16[1,128,2048]{2,1,0:T(8,128)(2,1)S(1)}) custom-call(bf16[3,192,2048]{2,1,0:T(8,128)(2,1)S(1)} %bitcast.144, bf16[3,192,2048]{2,1,0:T(8,128)(2,1)S(1)} %bitcast.145, bf16[3,192,2048]{2,1,0:T(8,128)(2,1)S(1)} %bitcast.146, bf16[3,64,2048]{2,1,0:T(8,128)(2,1)S(1)} %bitcast.160, ...), custom_call_target="tpu_custom_call" | custom-call | flops 10737418240 | bytes 2359296 | tf_op jit(solution)/shard_map/pallas_call | solution.py:122
  390.1 12.9 %shard_map.242 = (f32[1,64,2048]{2,1,0:T(8,128)S(1)}, bf16[1,128,2048]{2,1,0:T(8,128)(2,1)}) custom-call(bf16[3,192,2048]{2,1,0:T(8,128)(2,1)} %bitcast.125, bf16[3,128,2048]{2,1,0:T(8,128)(2,1)} %collective-permute-done.12.refs_3_.refs_4_.refs_1_.refs_2_, bf16[3,128,2048]{2,1,0:T(8,128)(2,1)} %collective-permute-done.12.refs_3_.refs_4_.refs_1_.refs_2_, ...), custom_call_target="tpu_custom_call" | custom-call | flops 10737418240 | bytes 2359296 | tf_op jit(solution)/shard_map/pallas_call | solution.py:122
  411.7 12.2 %shard_map.245 = (bf16[1,64,2048]{2,1,0:T(8,128)(2,1)S(1)}, bf16[1,128,2048]{2,1,0:T(8,128)(2,1)S(1)}) custom-call(bf16[3,192,2048]{2,1,0:T(8,128)(2,1)} %bitcast.126, bf16[3,192,2048]{2,1,0:T(8,128)(2,1)} %bitcast.127, bf16[3,192,2048]{2,1,0:T(8,128)(2,1)} %bitcast.128, bf16[3,64,2048]{2,1,0:T(8,128)(2,1)S(1)} %bitcast.162, ...), custom_call_target="tpu_custom_call" | custom-call | flops 10737418240 | bytes 2359296 | tf_op jit(solution)/shard_map/pallas_call | solution.py:122
  447.5 3.1 fusion.113
  450.6 3.7 fusion.114
  457.5 5.0 fusion.42
  464.9 3.4 collective-permute-start.43
  470.3 3.4 collective-permute-done.44
  490.2 3.5 collective-permute-start.53
  494.4 8.7 %reduce-scatter.6.cloned.1.call-done.refs_1_ = bf16[96,192]{1,0:T(8,128)(2,1)} async-done(((bf16[384,192]{1,0:T(8,128)(2,1)}), bf16[96,192]{1,0:T(8,128)(2,1)}) %reduce-scatter.6.cloned.1.call-update) | async-done | bytes 36880 | tf_op jit(solution)/shard_map/reduce_scatter | solution.py:637
  503.1 16.0 %collective-permute-done.53 = bf16[192,1024]{1,0:T(8,128)(2,1)S(1)} collective-permute-done((bf16[192,1024]{1,0:T(8,128)(2,1)S(1)}, bf16[192,1024]{1,0:T(8,128)(2,1)S(1)}, u32[]{:S(2)}, u32[]{:S(2)}) %collective-permute-start.53) | collective-permute-done | bytes 393248 | tf_op jit(solution)/shard_map/ppermute | solution.py:57
  519.1 7.5 %collective-permute-done.52 = bf16[192,1024]{1,0:T(8,128)(2,1)} collective-permute-done((bf16[192,1024]{1,0:T(8,128)(2,1)S(1)}, bf16[192,1024]{1,0:T(8,128)(2,1)}, u32[]{:S(2)}, u32[]{:S(2)}) %collective-permute-start.52) | collective-permute-done | bytes 393248 | tf_op jit(solution)/shard_map/ppermute | solution.py:57
  (562 shorter events, 195.9 us)
Async XLA Ops:
  8.1 192.7 %all-gather.9.cloned.1.call-start = ((), (), s32[]{:S(2)}) async-start(), calls=%async_computation.5 | async-start | bytes 2949120 | tf_op jit(solution)/shard_map/all_gather | solution.py:425
  25.3 81.6 %collective-permute-start.9 = (bf16[512,768]{1,0:T(8,128)(2,1)S(1)}, bf16[512,768]{1,0:T(8,128)(2,1)S(1)}, u32[]{:S(2)}, u32[]{:S(2)}) collective-permute-start(bf16[512,768]{1,0:T(8,128)(2,1)S(1)} %bitcast.167), channel_id=1, source_target_pairs={{0,3},{1,0},{2,1},{3,2},{4,7},{5,4},{6,5},{7,6},{8,11},{9,8},{10,9... | collective-permute-start | bytes 2359304 | tf_op jit(solution)/shard_map/ppermute | solution.py:49
  26.7 80.2 %collective-permute-start.10 = (bf16[512,768]{1,0:T(8,128)(2,1)S(1)}, bf16[512,768]{1,0:T(8,128)(2,1)}, u32[]{:S(2)}, u32[]{:S(2)}) collective-permute-start(bf16[512,768]{1,0:T(8,128)(2,1)S(1)} %bitcast.168), channel_id=1, source_target_pairs={{0,2},{1,3},{2,0},{3,1},{4,6},{5,7},{6,4},{7,5},{8,10},{9,11},{10,... | collective-permute-start | bytes 2359304 | tf_op jit(solution)/shard_map/ppermute | solution.py:49
  26.8 80.2 %collective-permute-start.11 = (bf16[512,768]{1,0:T(8,128)(2,1)S(1)}, bf16[512,768]{1,0:T(8,128)(2,1)}, u32[]{:S(2)}, u32[]{:S(2)}) collective-permute-start(bf16[512,768]{1,0:T(8,128)(2,1)S(1)} %bitcast.169), channel_id=1, source_target_pairs={{0,1},{1,2},{2,3},{3,0},{4,5},{5,6},{6,7},{7,4},{8,9},{9,10},{10,1... | collective-permute-start | bytes 2359304 | tf_op jit(solution)/shard_map/ppermute | solution.py:49
  29.0 66.2 %collective-permute-start.19 = (bf16[192,384]{1,0:T(8,128)(2,1)S(1)}, bf16[192,384]{1,0:T(8,128)(2,1)S(1)}, u32[]{:S(2)}, u32[]{:S(2)}) collective-permute-start(bf16[192,384]{1,0:T(8,128)(2,1)S(1)} %dynamic-slice_bitcast_fusion.1), channel_id=1, source_target_pairs={{0,3},{1,0},{2,1},{3,2},{4,7},{5,4},{6,5},{7,6},{8,11},{9,8},{10,9... | collective-permute-start | bytes 442376 | tf_op jit(solution)/shard_map/ppermute | solution.py:49
  29.0 67.3 %collective-permute-start.6 = (bf16[192,576]{0,1:T(8,128)(2,1)}, bf16[192,576]{0,1:T(8,128)(2,1)}, u32[]{:S(2)}, u32[]{:S(2)}) collective-permute-start(bf16[192,576]{0,1:T(8,128)(2,1)} %bitcast.173), channel_id=1, source_target_pairs={{0,24},{8,16},{16,8},{24,0},{1,25},{9,17},{17,9},{25,1},{2,26},{10... | collective-permute-start | bytes 663560 | tf_op jit(solution)/shard_map/ppermute | solution.py:87
  99.3 102.1 %all-gather.7.cloned.1.call-start = ((), (), s32[]{:S(2)}) async-start(), calls=%async_computation.4 | async-start | bytes 1474560 | tf_op jit(solution)/shard_map/all_gather | solution.py:480
  128.5 79.7 %all-gather.5.cloned.1.call-start = ((), (), s32[]{:S(2)}) async-start(), calls=%async_computation.3 | async-start | bytes 2949120 | tf_op jit(solution)/shard_map/all_gather | solution.py:474
  142.2 214.5 %all-gather.11.cloned.1.call-start = ((), (), s32[]{:S(2)}) async-start(), calls=%async_computation.6 | async-start | bytes 2211840 | tf_op jit(solution)/shard_map/all_gather | solution.py:507
  171.4 28.4 %collective-permute-start.15 = (bf16[192,512]{1,0:T(8,128)(2,1)S(1)}, bf16[192,512]{1,0:T(8,128)(2,1)S(1)}, u32[]{:S(2)}, u32[]{:S(2)}) collective-permute-start(bf16[192,512]{1,0:T(8,128)(2,1)S(1)} %bitcast.164), channel_id=1, source_target_pairs={{0,1},{1,2},{2,3},{3,0},{4,5},{5,6},{6,7},{7,4},{8,9},{9,10},{10,1... | collective-permute-start | bytes 589832 | tf_op jit(solution)/shard_map/ppermute | solution.py:57
  173.4 26.3 %collective-permute-start.14 = (bf16[192,512]{1,0:T(8,128)(2,1)S(1)}, bf16[192,512]{1,0:T(8,128)(2,1)S(1)}, u32[]{:S(2)}, u32[]{:S(2)}) collective-permute-start(bf16[192,512]{1,0:T(8,128)(2,1)S(1)} %bitcast.163), channel_id=1, source_target_pairs={{0,2},{1,3},{2,0},{3,1},{4,6},{5,7},{6,4},{7,5},{8,10},{9,11},{10,... | collective-permute-start | bytes 589832 | tf_op jit(solution)/shard_map/ppermute | solution.py:57
  200.7 22.7 %collective-permute-start.23 = (bf16[768,1536]{1,0:T(8,128)(2,1)}, bf16[768,1536]{1,0:T(8,128)(2,1)}, u32[]{:S(2)}, u32[]{:S(2)}) collective-permute-start(bf16[768,1536]{1,0:T(8,128)(2,1)} %all-gather.9.cloned.1.call-done), channel_id=1, source_target_pairs={{0,4},{4,0},{1,5},{5,1},{2,6},{6,2},{3,7},{7,3},{8,12},{12,8},{9,1... | collective-permute-start | bytes 7077896 | tf_op jit(solution)/shard_map/ppermute | solution.py:68
  248.3 54.9 %collective-permute-start.27 = (bf16[768,4096]{1,0:T(8,128)(2,1)}, bf16[768,4096]{1,0:T(8,128)(2,1)}, u32[]{:S(2)}, u32[]{:S(2)}) collective-permute-start(bf16[768,4096]{1,0:T(8,128)(2,1)} %get-tuple-element.89), channel_id=1, source_target_pairs={{0,4},{4,0},{1,5},{5,1},{2,6},{6,2},{3,7},{7,3},{8,12},{12,8},{9,1... | collective-permute-start | bytes 18874376 | tf_op jit(solution)/shard_map/ppermute | solution.py:68
  249.2 238.5 %reduce-scatter.8.cloned.1.call-start = ((), (), s32[]{:S(2)}) async-start(), calls=%async_computation.9 | async-start | bytes 7864320 | tf_op jit(solution)/shard_map/reduce_scatter | solution.py:582
  253.0 26.6 %collective-permute-start.25 = (bf16[192,512]{1,0:T(8,128)(2,1)S(1)}, bf16[192,512]{1,0:T(8,128)(2,1)S(1)}, u32[]{:S(2)}, u32[]{:S(2)}) collective-permute-start(bf16[192,512]{1,0:T(8,128)(2,1)S(1)} %get-tuple-element.206), channel_id=1, source_target_pairs={{0,2},{1,3},{2,0},{3,1},{4,6},{5,7},{6,4},{7,5},{8,10},{9,11},{10,... | collective-permute-start | bytes 589832 | tf_op jit(solution)/shard_map/ppermute | solution.py:57
  254.2 35.9 %collective-permute-start.24 = (bf16[192,512]{1,0:T(8,128)(2,1)S(1)}, bf16[192,512]{1,0:T(8,128)(2,1)S(1)}, u32[]{:S(2)}, u32[]{:S(2)}) collective-permute-start(bf16[192,512]{1,0:T(8,128)(2,1)S(1)} %get-tuple-element.207), channel_id=1, source_target_pairs={{0,3},{1,0},{2,1},{3,2},{4,7},{5,4},{6,5},{7,6},{8,11},{9,8},{10,9... | collective-permute-start | bytes 589832 | tf_op jit(solution)/shard_map/ppermute | solution.py:57
  314.4 180.0 %reduce-scatter.4.cloned.1.call-start = ((), (), s32[]{:S(2)}) async-start(), calls=%async_computation.7 | async-start | bytes 368640 | tf_op jit(solution)/shard_map/reduce_scatter | solution.py:637
  352.7 24.6 %collective-permute-start.32 = (bf16[128,2048]{1,0:T(8,128)(2,1)}, bf16[128,2048]{1,0:T(8,128)(2,1)}, u32[]{:S(2)}, u32[]{:S(2)}) collective-permute-start(bf16[128,2048]{1,0:T(8,128)(2,1)} %bitcast.21), channel_id=1, source_target_pairs={{0,4},{4,0},{1,5},{5,1},{2,6},{6,2},{3,7},{7,3},{8,12},{12,8},{9,1... | collective-permute-start | bytes 1572872 | tf_op jit(solution)/shard_map/ppermute | solution.py:68
  355.2 18.1 %collective-permute-start.29 = (bf16[192,512]{1,0:T(8,128)(2,1)}, bf16[192,512]{1,0:T(8,128)(2,1)S(1)}, u32[]{:S(2)}, u32[]{:S(2)}) collective-permute-start(bf16[192,512]{1,0:T(8,128)(2,1)} %get-tuple-element.200), channel_id=1, source_target_pairs={{0,3},{1,0},{2,1},{3,2},{4,7},{5,4},{6,5},{7,6},{8,11},{9,8},{10,9... | collective-permute-start | bytes 589832 | tf_op jit(solution)/shard_map/ppermute | solution.py:57
  355.2 18.8 %collective-permute-start.30 = (bf16[192,512]{1,0:T(8,128)(2,1)}, bf16[192,512]{1,0:T(8,128)(2,1)}, u32[]{:S(2)}, u32[]{:S(2)}) collective-permute-start(bf16[192,512]{1,0:T(8,128)(2,1)} %get-tuple-element.201), channel_id=1, source_target_pairs={{0,2},{1,3},{2,0},{3,1},{4,6},{5,7},{6,4},{7,5},{8,10},{9,11},{10,... | collective-permute-start | bytes 589832 | tf_op jit(solution)/shard_map/ppermute | solution.py:57
  355.3 20.4 %collective-permute-start.31 = (bf16[192,512]{1,0:T(8,128)(2,1)}, bf16[192,512]{1,0:T(8,128)(2,1)}, u32[]{:S(2)}, u32[]{:S(2)}) collective-permute-start(bf16[192,512]{1,0:T(8,128)(2,1)} %get-tuple-element.199), channel_id=1, source_target_pairs={{0,1},{1,2},{2,3},{3,0},{4,5},{5,6},{6,7},{7,4},{8,9},{9,10},{10,1... | collective-permute-start | bytes 589832 | tf_op jit(solution)/shard_map/ppermute | solution.py:57
  356.7 50.9 %collective-permute-start.36 = (bf16[2304,384]{1,0:T(8,128)(2,1)}, bf16[2304,384]{1,0:T(8,128)(2,1)}, u32[]{:S(2)}, u32[]{:S(2)}) collective-permute-start(bf16[2304,384]{1,0:T(8,128)(2,1)} %shard_map.244), channel_id=1, source_target_pairs={{0,4},{4,0},{1,5},{5,1},{2,6},{6,2},{3,7},{7,3},{8,12},{12,8},{9,1... | collective-permute-start | bytes 5308424 | tf_op jit(solution)/shard_map/ppermute | solution.py:68
  380.4 22.6 %collective-permute-start.33 = (bf16[192,512]{1,0:T(8,128)(2,1)S(1)}, bf16[192,512]{1,0:T(8,128)(2,1)S(1)}, u32[]{:S(2)}, u32[]{:S(2)}) collective-permute-start(bf16[192,512]{1,0:T(8,128)(2,1)S(1)} %get-tuple-element.195), channel_id=1, source_target_pairs={{0,3},{1,0},{2,1},{3,2},{4,7},{5,4},{6,5},{7,6},{8,11},{9,8},{10,9... | collective-permute-start | bytes 589832 | tf_op jit(solution)/shard_map/ppermute | solution.py:57
  381.6 22.8 %collective-permute-start.34 = (bf16[192,512]{1,0:T(8,128)(2,1)S(1)}, bf16[192,512]{1,0:T(8,128)(2,1)S(1)}, u32[]{:S(2)}, u32[]{:S(2)}) collective-permute-start(bf16[192,512]{1,0:T(8,128)(2,1)S(1)} %get-tuple-element.196), channel_id=1, source_target_pairs={{0,2},{1,3},{2,0},{3,1},{4,6},{5,7},{6,4},{7,5},{8,10},{9,11},{10,... | collective-permute-start | bytes 589832 | tf_op jit(solution)/shard_map/ppermute | solution.py:57
  383.7 21.4 %collective-permute-start.35 = (bf16[192,512]{1,0:T(8,128)(2,1)S(1)}, bf16[192,512]{1,0:T(8,128)(2,1)S(1)}, u32[]{:S(2)}, u32[]{:S(2)}) collective-permute-start(bf16[192,512]{1,0:T(8,128)(2,1)S(1)} %get-tuple-element.194), channel_id=1, source_target_pairs={{0,1},{1,2},{2,3},{3,0},{4,5},{5,6},{6,7},{7,4},{8,9},{9,10},{10,1... | collective-permute-start | bytes 589832 | tf_op jit(solution)/shard_map/ppermute | solution.py:57
  388.1 18.4 %collective-permute-start.37 = (bf16[384,384]{1,0:T(8,128)(2,1)S(1)}, bf16[384,384]{1,0:T(8,128)(2,1)S(1)}, u32[]{:S(2)}, u32[]{:S(2)}) collective-permute-start(bf16[384,384]{1,0:T(8,128)(2,1)S(1)} %bitcast.178), channel_id=1, source_target_pairs={{0,4},{4,0},{1,5},{5,1},{2,6},{6,2},{3,7},{7,3},{8,12},{12,8},{9,1... | collective-permute-start | bytes 884744 | tf_op jit(solution)/shard_map/ppermute | solution.py:68
  403.0 21.0 %collective-permute-start.38 = (bf16[128,2048]{1,0:T(8,128)(2,1)}, bf16[128,2048]{1,0:T(8,128)(2,1)}, u32[]{:S(2)}, u32[]{:S(2)}) collective-permute-start(bf16[128,2048]{1,0:T(8,128)(2,1)} %bitcast.28), channel_id=1, source_target_pairs={{0,4},{4,0},{1,5},{5,1},{2,6},{6,2},{3,7},{7,3},{8,12},{12,8},{9,1... | collective-permute-start | bytes 1572872 | tf_op jit(solution)/shard_map/ppermute | solution.py:68
  407.3 95.8 %reduce-scatter.6.cloned.1.call-start = ((), (), s32[]{:S(2)}) async-start(), calls=%async_computation.8 | async-start | bytes 245760 | tf_op jit(solution)/shard_map/reduce_scatter | solution.py:637
  428.3 17.6 %collective-permute-start.41 = (bf16[192,512]{1,0:T(8,128)(2,1)}, bf16[192,512]{1,0:T(8,128)(2,1)}, u32[]{:S(2)}, u32[]{:S(2)}) collective-permute-start(bf16[192,512]{1,0:T(8,128)(2,1)} %get-tuple-element.190), channel_id=1, source_target_pairs={{0,1},{1,2},{2,3},{3,0},{4,5},{5,6},{6,7},{7,4},{8,9},{9,10},{10,1... | collective-permute-start | bytes 589832 | tf_op jit(solution)/shard_map/ppermute | solution.py:57
  438.1 38.3 %collective-permute-start.51 = (bf16[384,192]{1,0:T(8,128)(2,1)}, bf16[384,192]{1,0:T(8,128)(2,1)}, u32[]{:S(2)}, u32[]{:S(2)}) collective-permute-start(bf16[384,192]{1,0:T(8,128)(2,1)} %bitcast.179), channel_id=1, source_target_pairs={{0,4},{4,0},{1,5},{5,1},{2,6},{6,2},{3,7},{7,3},{8,12},{12,8},{9,1... | collective-permute-start | bytes 442376 | tf_op jit(solution)/shard_map/ppermute | solution.py:68
  490.2 28.9 %collective-permute-start.53 = (bf16[192,1024]{1,0:T(8,128)(2,1)S(1)}, bf16[192,1024]{1,0:T(8,128)(2,1)S(1)}, u32[]{:S(2)}, u32[]{:S(2)}) collective-permute-start(bf16[192,1024]{1,0:T(8,128)(2,1)S(1)} %get-tuple-element.185), channel_id=1, source_target_pairs={{0,2},{1,3},{2,0},{3,1},{4,6},{5,7},{6,4},{7,5},{8,10},{9,11},{10,... | collective-permute-start | bytes 1179656 | tf_op jit(solution)/shard_map/ppermute | solution.py:57
  493.7 33.0 %collective-permute-start.52 = (bf16[192,1024]{1,0:T(8,128)(2,1)S(1)}, bf16[192,1024]{1,0:T(8,128)(2,1)}, u32[]{:S(2)}, u32[]{:S(2)}) collective-permute-start(bf16[192,1024]{1,0:T(8,128)(2,1)S(1)} %get-tuple-element.183), channel_id=1, source_target_pairs={{0,3},{1,0},{2,1},{3,2},{4,7},{5,4},{6,5},{7,6},{8,11},{9,8},{10,9... | collective-permute-start | bytes 1179656 | tf_op jit(solution)/shard_map/ppermute | solution.py:57
  (156 other events, 1501.0 us)
Sparse Core Ops, SparseCore 0:
  99.4 38.6 all-gather.8
  140.5 27.7 all-gather.6
  170.7 37.4 all-gather.4
  314.5 68.5 reduce-scatter.7
  407.4 21.6 reduce-scatter.3
  478.2 24.8 reduce-scatter.5
Sparse Core Ops, SparseCore 1:
  249.3 49.5 all-gather.10
